TPU v7x, 512 devices: a whole 4x8x8 slice. The times are simulated.
512 devices in a mesh: fsdp: 64 (over x, z, core), tensor: 8 (over y).
Axes of the slice: x: 4, y: 8, z: 8, core: 2. Of those that a mesh axis runs over, the one named last changes fastest.
Arguments:
- momentum: float32 [8192, 28672], P('fsdp', 'tensor')
- gradient: bfloat16 [8192, 28672], P('fsdp', 'tensor'), may hold values from -6 to 6
- right_factor: float32 [28672, 256], P(('tensor', 'fsdp')), may hold values from -6 to 6
Outputs:
- new_momentum: float32 [8192, 28672], P('fsdp', 'tensor')
- new_right: float32 [28672, 256], P(('tensor', 'fsdp'))
- row_factor: float32 [8192, 256], P('fsdp')
All inputs are finite; a program needn't handle non-finite values.
Results may differ from a plain program's by a relative error of at most 0.0003.
Values sent between devices are 32-bit elements; how exact they have to be, the bound alone decides.
No kernel may reach another device: no remote copies, remote signals or barrier semaphores. Data moves between devices by JAX's collectives and lax.ppermute only.
A program may use at most 64 MiB of HBM per device.

v0:
```python
import math

import jax
import jax.numpy as jnp
from jax import lax
from jax.sharding import PartitionSpec as P

ROWS = 8192
COLS = 28672


highest = lax.Precision.HIGHEST


def orthonormalize(power_rows, gram_matrix):
    lower_factor = jnp.linalg.cholesky(gram_matrix)
    return jax.scipy.linalg.solve_triangular(lower_factor, power_rows.T, lower=True).T


def gram_of(power_rows):
    return lax.dot_general(
        power_rows,
        power_rows,
        (((0,), (0,)), ((), ())),
        precision=highest,
        preferred_element_type=jnp.float32,
    )


def shards(momentum, gradient, right_factor):
    buffer = momentum + gradient.astype(jnp.float32)
    columns = buffer
    partial_value = jnp.dot(
        columns,
        lax.all_gather(right_factor, "fsdp", axis=0, tiled=True),
        precision=highest,
        preferred_element_type=jnp.float32,
    )
    power_rows = lax.psum(partial_value, "tensor")
    gram_matrix = lax.psum(gram_of(power_rows), "fsdp")
    orthonormal = orthonormalize(power_rows, gram_matrix)
    columns = buffer
    column_mine = lax.psum_scatter(
        lax.dot_general(
            columns,
            orthonormal,
            (((0,), (0,)), ((), ())),
            precision=highest,
            preferred_element_type=jnp.float32,
        ),
        "fsdp",
        scatter_dimension=0,
        tiled=True,
    )
    correction = lax.dot_general(
        orthonormal,
        lax.all_gather(column_mine, "fsdp", axis=0, tiled=True),
        (((1,), (1,)), ((), ())),
        precision=highest,
        preferred_element_type=jnp.float32,
    )
    new_momentum = buffer - 0.05 * correction
    squares = lax.psum(jnp.sum(column_mine * column_mine, axis=0), ("fsdp", "tensor"))
    col_scale = jnp.sqrt(squares / COLS + 1e-06)
    new_right = column_mine / col_scale
    row_factor = orthonormal * math.sqrt(ROWS)
    return (new_momentum, new_right, row_factor)


def solution(mesh):
    return jax.shard_map(
        shards,
        mesh=mesh,
        in_specs=(P("fsdp", "tensor"), P("fsdp", "tensor"), P(("tensor", "fsdp"), None)),
        out_specs=(P("fsdp", "tensor"), P(("tensor", "fsdp"), None), P("fsdp", None)),
        check_vma=False,
    )
```

profile of v0, /device:TPU:1, one launch (start us, length us, event | category | flops | bytes accessed | tf_op | source)
XLA Modules:
  0.0 703.3 jit_solution(10338337822264493617)
XLA Ops:
  7.2 0.7 all-gather.3.cloned.1.call-update
  7.9 93.9 %all-gather.3.cloned.1.call-done = f32[3584,256]{1,0:T(8,128)} async-done(((f32[56,256]{1,0:T(8,128)}), f32[3584,256]{1,0:T(8,128)}) %all-gather.3.cloned.1.call-update) | async-done | bytes 3670032 | tf_op jit(solution)/shard_map/all_gather | solution.py:35
  101.8 5.5 fusion.2
  107.4 68.8 %all-reduce.4.cloned.1.call-done = f32[128,256]{1,0:T(8,128)} async-done(((f32[128,256]{1,0:T(8,128)}), f32[128,256]{1,0:T(8,128)}) %all-reduce.4.cloned.1.call-update) | async-done | bytes 131088 | tf_op jit(solution)/shard_map/psum | solution.py:39
  176.2 2.1 fusion.14
  178.6 192.7 %all-reduce.6.cloned.1.call-done = f32[256,256]{0,1:T(8,128)} async-done(((f32[256,256]{0,1:T(8,128)}), f32[256,256]{0,1:T(8,128)}) %all-reduce.6.cloned.1.call-update) | async-done | bytes 262160 | tf_op jit(solution)/shard_map/psum | solution.py:40
  371.4 1.1 copy.7
  372.5 1.1 fusion.3
  373.6 11.7 %cholesky.50 = f32[128,128]{1,0:T(8,128)S(1)} custom-call(f32[128,128]{1,0:T(8,128)S(1)} %cholesky.118), custom_call_target="Cholesky" | custom-call | tf_op jit(solution)/shard_map/jit(cholesky)/cholesky | solution.py:16
  385.3 9.8 %custom-call.15 = f32[1,128,128]{1,2,0:T(8,128)S(1)} custom-call(f32[1,128,128]{2,1,0:T(8,128)S(1)} %get-tuple-element.27), custom_call_target="InvertDiagBlocksLowerTriangular" | custom-call | tf_op jit(solution)/shard_map/jit(cholesky)/cholesky | solution.py:16
  395.6 11.7 %cholesky.105 = f32[128,128]{1,0:T(8,128)S(1)} custom-call(f32[128,128]{1,0:T(8,128)S(1)} %convolution_subtract_fusion.1), custom_call_target="Cholesky" | custom-call | tf_op jit(solution)/shard_map/jit(cholesky)/cholesky | solution.py:16
  407.4 0.7 compare_reduce_fusion
  409.6 5.5 while.1
  410.3 2.1 bitcast_dynamic-update-slice_fusion.2
  412.4 0.6 fusion.24
  413.0 2.1 bitcast_dynamic-update-slice_fusion.2
  415.1 20.5 %custom-call.16 = f32[2,128,128]{1,2,0:T(8,128)S(1)} custom-call(f32[2,128,128]{2,1,0:T(8,128)} %get-tuple-element.10), custom_call_target="InvertDiagBlocksLowerTriangular" | custom-call | tf_op jit(solution)/shard_map/jit(_solve_triangular)/triangular_solve | solution.py:17
  436.5 4.9 fusion.1
  441.4 143.7 %reduce-scatter.2.cloned.1.call-done = f32[56,256]{1,0:T(8,128)} async-done(((f32[3584,256]{1,0:T(8,128)}), f32[56,256]{1,0:T(8,128)}) %reduce-scatter.2.cloned.1.call-update) | async-done | bytes 57360 | tf_op jit(solution)/shard_map/reduce_scatter | solution.py:43
  585.2 0.8 copy.8
  585.9 0.8 multiply_reduce_fusion
  586.8 101.3 %psum.23 = f32[256]{0:T(256)S(1)} all-reduce(f32[256]{0:T(256)S(1)} %multiply_reduce_fusion), channel_id=1, replica_groups=mesh['fsdp'=64,'tensor'=8] {'fsdp','tensor'}, use_global_device_ids=true, to_apply=%region_8.9 | all-reduce | flops 256 | bytes 2048 | tf_op jit(solution)/shard_map/psum | solution.py:63
  688.1 1.5 broadcast_divide_fusion
  689.6 7.2 %fusion = f32[128,3584]{1,0:T(8,128)} fusion(f32[3584,256]{1,0:T(8,128)} %all-gather.5.cloned.1.call-done, f32[128,3584]{1,0:T(8,128)S(1)} %copy-done, bf16[128,3584]{1,0:T(8,128)(2,1)S(1)} %copy-done.1, f32[128,128]{1,0:T(8,128)S(1)} %fusion.5, f32[128,128]{1,0:T(8,128)S(1)} %fusion.6), kind=kOutput, calls=%fused_computation.3 | convolution fusion | flops 1411153920 | bytes 8388608 | tf_op jit(solution)/shard_map/dot_general | solution.py:55
  (34 shorter events, 2.6 us)
Async XLA Ops:
  7.2 94.7 %all-gather.3.cloned.1.call-start = ((), (), s32[]{:S(2)}) async-start(), calls=%async_computation.1 | async-start | bytes 3727360 | tf_op jit(solution)/shard_map/all_gather | solution.py:35
  7.9 168.3 %all-reduce.4.cloned.1.call-start = ((), (), s32[]{:S(2)}) async-start(), calls=%async_computation.2 | async-start | bytes 262144 | tf_op jit(solution)/shard_map/psum | solution.py:39
  107.3 264.0 %all-reduce.6.cloned.1.call-start = ((), (), s32[]{:S(2)}) async-start(), calls=%async_computation.3 | async-start | bytes 524288 | tf_op jit(solution)/shard_map/psum | solution.py:40
  178.4 406.8 %reduce-scatter.2.cloned.1.call-start = ((), (), s32[]{:S(2)}) async-start(), calls=%async_computation.4 | async-start | bytes 3727360 | tf_op jit(solution)/shard_map/reduce_scatter | solution.py:43
  372.4 63.1 %copy-start.2 = (f32[128,256]{1,0:T(8,128)S(1)}, f32[128,256]{1,0:T(8,128)}, u32[]{:S(2)}) copy-start(f32[128,256]{1,0:T(8,128)} %all-reduce.4.cloned.1.call-done) | copy-start | bytes 393220
  372.4 64.0 %copy-start.1 = (bf16[128,3584]{1,0:T(8,128)(2,1)S(1)}, bf16[128,3584]{1,0:T(8,128)(2,1)}, u32[]{:S(2)}) copy-start(bf16[128,3584]{1,0:T(8,128)(2,1)} %param.4) | copy-start | bytes 2752516
  373.5 62.9 %copy-start = (f32[128,3584]{1,0:T(8,128)S(1)}, f32[128,3584]{1,0:T(8,128)}, u32[]{:S(2)}) copy-start(f32[128,3584]{1,0:T(8,128)} %param.3) | copy-start | bytes 5505028
  441.4 248.2 %all-gather.5.cloned.1.call-start = ((), (), s32[]{:S(2)}) async-start(), calls=%async_computation.5 | async-start | bytes 3727360 | tf_op jit(solution)/shard_map/all_gather | solution.py:57
Sparse Core Ops, SparseCore 0:
  11.3 90.4 all-gather.2
  107.5 68.7 all-reduce.3
  180.7 190.6 all-reduce.5
  441.5 143.5 reduce-scatter.1
  588.8 87.9 all-gather.4
where the time goes:
time: 704 us; the launch traced here: 703 us
  waiting for transfers between devices  500 us (71%)
  blocking collectives  101 us (14%)
  other arithmetic  57.9 us (8%)
  matrix products  21 us (3%)
  between operations  15.3 us (2%)
  local copies, waits for them, and re-layouts  7.27 us (1%)
    psum x1, waiting for transfers between devices, shards(): gram_matrix = lax.psum(gram_of(power_rows), 'fsdp')  193 us
    reduce_scatter x1, waiting for transfers between devices, shards(): lax.psum_scatter(lax.dot_general(columns, orthonormal, (((0,), (0,)), (()...  144 us
    psum x1, blocking collectives, shards(): lax.psum(jnp.sum(column_mine * column_mine, axis=0), ('fsdp', 'tensor'))  101 us
    all_gather x1, waiting for transfers between devices, shards(): lax.all_gather(right_factor, 'fsdp', axis=0, tiled=True)  93.9 us
    psum x1, waiting for transfers between devices, shards(): power_rows = lax.psum(partial_value, 'tensor')  68.8 us
    another operation x6, other arithmetic, orthonormalize(): lower_factor = jnp.linalg.cholesky(gram_matrix)  34 us
    another operation x3, other arithmetic, orthonormalize(): jax.scipy.linalg.solve_triangular(lower_factor, power_rows.T, lower=True)  20.5 us
  transfers between devices with their start and end apart: 5, of which 4 were waited for; matrix products, arithmetic and copies ran while one was open for 0% of the time, Pallas kernels for 0%

commit v1 on v0

v1 whole, which is shorter than its diff:
```python
import math

import jax
import jax.numpy as jnp
import numpy as np
from jax import lax
from jax.experimental import pallas as pl
from jax.experimental.pallas import tpu as pltpu
from jax.sharding import Mesh, PartitionSpec as P

ROWS = 8192
COLS = 28672
RANK = 256
NX, NZ, NC, NY = 4, 8, 2, 8
CHIPS = NX * NZ
MY_ROWS = 128
MY_COLS = 3584
SHARD = 56
STEPS = 4
SOME = CHIPS // STEPS
CHUNK = SOME * NC * SHARD
BLOCK = 32
MACS = MY_ROWS * MY_COLS * RANK

highest = lax.Precision.HIGHEST
f32 = jnp.float32
bf16 = jnp.bfloat16
VMEM = pl.BlockSpec(memory_space=pltpu.VMEM)
SMEM = pl.BlockSpec(memory_space=pltpu.SMEM)
ANY = pl.BlockSpec(memory_space=pl.ANY)
HBM = pl.BlockSpec(memory_space=pltpu.HBM)


def dot(a, b, ca, cb, precision=highest):
    return lax.dot_general(
        a, b, (((ca,), (cb,)), ((), ())), precision=precision, preferred_element_type=f32
    )


def shape(*dims):
    return jax.ShapeDtypeStruct(dims, f32)


def in_hbm(*dims):
    return pltpu.HBM(dims, f32)


TOKEN = shape(8, 128)


def call(kernel, out_shape, in_specs, scratch=(), out_specs=None, flops=1_000_000, nbytes=100_000, limit=12):
    return pl.pallas_call(
        kernel,
        out_shape=out_shape,
        in_specs=in_specs,
        out_specs=out_specs or jax.tree.map(lambda _: VMEM, out_shape),
        scratch_shapes=scratch,
        compiler_params=pltpu.CompilerParams(vmem_limit_bytes=limit * 2**20),
        cost_estimate=pl.CostEstimate(
            flops=flops, bytes_accessed=nbytes, transcendentals=0
        ),
    )


def buffer_copies(mom, grad, mom_here, grad_here, sems, j):
    cols = pl.ds(j * CHUNK, CHUNK)
    return [
        pltpu.make_async_copy(mom.at[:, cols], mom_here.at[:, cols], sems.at[j, 0]),
        pltpu.make_async_copy(grad.at[:, cols], grad_here.at[:, cols], sems.at[j, 1]),
    ]


def factor_copies(core, own, other, full, sems, j):
    chips = pl.ds(j * SOME, SOME)
    return [
        pltpu.make_async_copy(own.at[chips], full.at[chips, core], sems.at[j, 2]),
        pltpu.make_async_copy(other.at[chips], full.at[chips, 1 - core], sems.at[j, 3]),
    ]


def buffer_chunk(mom, grad, j):
    cols = pl.ds(j * CHUNK, CHUNK)
    return mom[:, cols] + grad[:, cols].astype(f32)


BUFFER_SCRATCH = [pltpu.VMEM((MY_ROWS, MY_COLS), f32), pltpu.VMEM((MY_ROWS, MY_COLS), bf16)]
SEMS = [pltpu.SemaphoreType.DMA((STEPS, 4))]
FULL = [pltpu.VMEM((CHIPS, NC, SHARD, RANK), f32)]


def power_kernel(where, own, other, mom, grad, out, mom_here, grad_here, full, sems):
    copies = []
    for j in range(STEPS):
        copies.append(
            factor_copies(where[0], own, other, full, sems, j)
            + buffer_copies(mom, grad, mom_here, grad_here, sems, j)
        )
        for copy in copies[j]:
            copy.start()
    total = None
    for j in range(STEPS):
        for copy in copies[j]:
            copy.wait()
        part = full[pl.ds(j * SOME, SOME)].reshape(CHUNK, RANK)
        part = dot(buffer_chunk(mom_here, grad_here, j), part, 1, 0)
        total = part if total is None else total + part
    out[...] = total


def sum_spread_kernel(pieces, out):
    total = jnp.sum(pieces[...], axis=0)
    for i in range(out.shape[0]):
        out[i] = total


def gram_kernel(power, out, token):
    token[...] = jnp.zeros_like(token)
    gram = dot(power[...], power[...], 0, 0)
    for i in range(RANK // 8):
        for h in range(RANK // 128):
            out[i * 2 + h] = gram[i * 8 : i * 8 + 8, h * 128 : h * 128 + 128]


def column_kernel(where, power, mom, grad, after, keep, send, mom_here, grad_here, sems, kept, sent):
    copies = []
    for j in range(STEPS):
        copies.append(buffer_copies(mom, grad, mom_here, grad_here, sems, j))
        for copy in copies[j]:
            copy.start()
    for j in range(STEPS):
        for copy in copies[j]:
            copy.wait()
        part = dot(buffer_chunk(mom_here, grad_here, j), power[...], 0, 0)
        part = part.reshape(SOME, NC, SHARD, RANK)
        first = where[0] == 0
        chips = pl.ds(j * SOME, SOME)
        kept[chips] = jnp.where(first, part[:, 0], part[:, 1])
        sent[chips] = jnp.where(first, part[:, 1], part[:, 0])
        copies[j] = [
            pltpu.make_async_copy(sent.at[chips], send.at[chips], sems.at[j, 2]),
            pltpu.make_async_copy(kept.at[chips], keep.at[chips], sems.at[j, 3]),
        ]
        for copy in copies[j]:
            copy.start()
    for j in range(STEPS):
        for copy in copies[j]:
            copy.wait()


def add_kernel(mine, arrived, after, out, token):
    token[...] = jnp.zeros_like(token)
    out[...] = mine[...] + arrived[...]


def sum_kernel(pieces, after, out, token):
    token[...] = jnp.zeros_like(token)
    out[...] = jnp.sum(pieces[...], axis=0)


def copies_kernel(value, after, out):
    for i in range(out.shape[0]):
        out[i] = value[...]


def column_mine_kernel(pieces, after, mine, copies):
    total = jnp.sum(pieces[...], axis=0)
    mine[...] = total
    for i in range(NZ):
        copies[i] = total


def eliminate(a, blocks):
    row = lax.broadcasted_iota(jnp.int32, (BLOCK, BLOCK), 0)
    col = lax.broadcasted_iota(jnp.int32, (BLOCK, BLOCK), 1)
    eye = (row == col).astype(f32)
    wide = lax.broadcasted_iota(jnp.int32, (BLOCK, RANK), 1)
    for k in blocks:
        lo, hi = k * BLOCK, (k + 1) * BLOCK
        d = a[lo:hi, lo:hi]
        for j in range(BLOCK - 1):
            column = jnp.broadcast_to(d[:, j : j + 1], (BLOCK, BLOCK))
            pivot = jnp.broadcast_to(1.0 / column[j : j + 1, :], (BLOCK, BLOCK))
            line = jnp.broadcast_to(d[j : j + 1, :], (BLOCK, BLOCK))
            line = jnp.where(col == j, 1.0, line)
            rest = jnp.where(col == j, 0.0, d)
            d = jnp.where(row > j, rest - column * (line * pivot), d)
        diagonal = jnp.sum(d * eye, axis=1, keepdims=True)
        inner = (jnp.where(row > col, d, 0.0) + eye) * lax.rsqrt(diagonal)
        panel = a[lo:hi, :]
        panel = jnp.where((wide >= lo) & (wide < hi), 0.0, panel)
        panel = dot(inner, panel, 1, 0)
        a[lo:hi, :] = panel
        a[lo:hi, lo:hi] = inner
        panel = a[lo:hi, :]
        if hi < RANK:
            change = dot(panel, panel, 0, 0)
            a[hi:, lo:hi] = jnp.zeros((RANK - hi, BLOCK), f32)
            a[hi:, :] = a[hi:, :] - change[hi:, :]


def first_half_kernel(gram, after, a):
    for i in range(RANK // 8):
        for h in range(RANK // 128):
            a[i * 8 : i * 8 + 8, h * 128 : h * 128 + 128] = gram[i * 2 + h]
    eliminate(a, range(0, RANK // BLOCK // 2))


def second_half_kernel(half, after, a):
    a[...] = half[...]
    eliminate(a, range(RANK // BLOCK // 2, RANK // BLOCK))
    row = lax.broadcasted_iota(jnp.int32, (RANK, RANK), 0)
    col = lax.broadcasted_iota(jnp.int32, (RANK, RANK), 1)
    a[...] = jnp.where(col <= row, a[...], 0.0)


def squares_kernel(column_mine, inverse, after, factor_mine, squares):
    c = dot(column_mine[...], inverse[...], 1, 1)
    factor_mine[...] = c
    squares[...] = jnp.sum(c * c, axis=0, keepdims=True)


def ortho_kernel(power, inverse, row_factor, weights):
    o = dot(power[...], inverse[...], 1, 1)
    row_factor[...] = o * math.sqrt(ROWS)
    weights[...] = 0.05 * dot(o, inverse[...], 1, 0)


def new_right_kernel(pieces, factor_mine, after, out):
    squares = jnp.sum(pieces[...], axis=0)
    out[...] = factor_mine[...] / jnp.sqrt(squares / COLS + 1e-06)


def split(value):
    high = value.astype(bf16)
    return high, (value - high.astype(f32)).astype(bf16)


def momentum_kernel(where, own, other, weights, mom, grad, out, token, mom_here, grad_here, full, sems, done):
    copies = []
    for j in range(STEPS):
        copies.append(
            factor_copies(where[0], own, other, full, sems, j)
            + buffer_copies(mom, grad, mom_here, grad_here, sems, j)
        )
        for copy in copies[j]:
            copy.start()
    high, low = split(weights[...])
    token[...] = jnp.zeros_like(token)
    for j in range(STEPS):
        for copy in copies[j]:
            copy.wait()
        fh, fl = split(full[pl.ds(j * SOME, SOME)].reshape(CHUNK, RANK))
        change = dot(high, fh, 1, 1, None) + (dot(high, fl, 1, 1, None) + dot(low, fh, 1, 1, None))
        cols = pl.ds(j * CHUNK, CHUNK)
        mom_here[:, cols] = buffer_chunk(mom_here, grad_here, j) - change
        copies[j] = pltpu.make_async_copy(mom_here.at[:, cols], out.at[:, cols], done.at[j])
        copies[j].start()
    for j in range(STEPS):
        copies[j].wait()


def spread(value, axis, size):
    copies = jnp.broadcast_to(value[None], (size,) + value.shape)
    return swap(copies, axis)


def swap(pieces, axis):
    return lax.all_to_all(pieces, axis, 0, 0)


def other_core(value):
    return lax.ppermute(value, "c", [(0, 1), (1, 0)])


def shards(momentum, gradient, right_factor):
    where = lax.axis_index("c").astype(jnp.int32).reshape(1)
    momentum = pltpu.with_memory_space_constraint(momentum, pltpu.HBM)
    gradient = pltpu.with_memory_space_constraint(gradient, pltpu.HBM)
    fsdp = ("x", "z", "c")

    own = spread(spread(right_factor, "z", NZ), "x", NX).reshape(CHIPS, SHARD, RANK)
    partial_power = call(
        power_kernel, shape(MY_ROWS, RANK), [SMEM] + [HBM] * 4,
        BUFFER_SCRATCH + FULL + SEMS, None, 12 * MACS, 7_000_000,
    )(where, own, other_core(own), momentum, gradient)

    pieces = swap(partial_power.reshape(NY, MY_ROWS // NY, RANK), "y")
    copies = call(sum_spread_kernel, shape(NY, MY_ROWS // NY, RANK), [VMEM])(pieces)
    power = swap(copies, "y").reshape(MY_ROWS, RANK)

    gram, token = call(gram_kernel, [shape(64, 8, 128), TOKEN], [VMEM])(power)
    gram_pieces = swap(gram, fsdp)
    keep, send = call(
        column_kernel, [in_hbm(CHIPS, SHARD, RANK)] * 2, [SMEM, VMEM, HBM, HBM, ANY],
        BUFFER_SCRATCH + SEMS + [pltpu.VMEM((CHIPS, SHARD, RANK), f32)] * 2,
        [HBM, HBM], 12 * MACS, 7_000_000,
    )(where, power, momentum, gradient, token)
    gram = call(sum_spread_kernel, shape(64, 8, 128), [VMEM])(gram_pieces)
    send, gram = lax.optimization_barrier((send, gram))
    arrived = other_core(send)
    block = pl.BlockSpec((SOME, SHARD, RANK), lambda i: (i, 0, 0))
    sums, token = pl.pallas_call(
        add_kernel,
        out_shape=[in_hbm(CHIPS, SHARD, RANK), TOKEN],
        grid=(STEPS,),
        in_specs=[block, block, ANY],
        out_specs=[block, pl.BlockSpec((8, 128), lambda i: (0, 0))],
        compiler_params=pltpu.CompilerParams(vmem_limit_bytes=8 * 2**20),
        cost_estimate=pl.CostEstimate(
            flops=1_000_000, bytes_accessed=6_000_000, transcendentals=0
        ),
    )(pltpu.with_memory_space_constraint(keep, pltpu.HBM), arrived, gram)
    gram = swap(gram, fsdp)

    by_x = swap(sums.reshape(NX, NZ, SHARD, RANK), "x")
    half = call(
        first_half_kernel, shape(RANK, RANK), [VMEM, ANY], flops=15_000_000_000
    )(gram, token)
    by_z, token = call(
        sum_kernel, [shape(NZ, SHARD, RANK), TOKEN], [VMEM, ANY], nbytes=3_000_000
    )(by_x, half)
    swapped = swap(by_z, "z")
    inverse = call(
        second_half_kernel, shape(RANK, RANK), [VMEM, ANY], flops=15_000_000_000
    )(half, token)
    column_mine, copies = call(
        column_mine_kernel, [shape(SHARD, RANK), shape(NZ, SHARD, RANK)], [VMEM, ANY]
    )(swapped, inverse)

    gathered = swap(copies, "z")
    factor_mine, squares = call(
        squares_kernel, [shape(SHARD, RANK), shape(1, RANK)], [VMEM, VMEM, ANY]
    )(column_mine, inverse, copies)
    for bit in (1, 2, 4):
        squares = squares + lax.ppermute(squares, "y", [(i, i ^ bit) for i in range(NY)])
    squares = jnp.broadcast_to(squares[None], (64, 1, RANK))
    copies = call(
        copies_kernel, shape(NX, NZ, SHARD, RANK), [VMEM, ANY], nbytes=3_000_000
    )(gathered, squares)
    own = swap(copies, "x").reshape(CHIPS, SHARD, RANK)
    row_factor, weights = call(
        ortho_kernel, [shape(MY_ROWS, RANK)] * 2, [VMEM, VMEM]
    )(power, inverse)
    squares = swap(squares, fsdp)
    new_momentum, token = call(
        momentum_kernel, [in_hbm(MY_ROWS, MY_COLS), TOKEN], [SMEM, HBM, HBM, VMEM, HBM, HBM],
        BUFFER_SCRATCH + FULL + SEMS + [pltpu.SemaphoreType.DMA((STEPS,))],
        [HBM, VMEM], 6 * MACS, 9_000_000,
    )(where, own, other_core(own), weights, momentum, gradient)
    new_right = call(
        new_right_kernel, shape(SHARD, RANK), [VMEM, VMEM, ANY]
    )(squares, factor_mine, token)
    return (new_momentum, new_right, row_factor)


def solution(mesh):
    devices = np.asarray(mesh.devices).reshape(NX, NZ, NC, NY)
    grid = Mesh(devices, ("x", "z", "c", "y"))
    fsdp = ("x", "z", "c")
    return jax.shard_map(
        shards,
        mesh=grid,
        in_specs=(P(fsdp, "y"), P(fsdp, "y"), P(("y",) + fsdp, None)),
        out_specs=(P(fsdp, "y"), P(("y",) + fsdp, None), P(fsdp, None)),
        check_vma=False,
    )
```

time: 704 us -> 253 us (0.36)
  waiting for transfers between devices: 500 us -> 41.7 us
  other arithmetic: 57.9 us -> 0.01 us
  starting transfers between devices: 0.38 us -> 57.7 us
  Pallas kernels: 0 us -> 55 us
  matrix products: 21 us -> 0 us
  between operations: 15.3 us -> 0.79 us
    psum x2 -> x0, waiting for transfers between devices: 262 us -> none  [the longest x1 193 us: shards(): gram_matrix = lax.psum(gram_of(power_rows), 'fsdp')]
    reduce_scatter x1 -> x0, waiting for transfers between devices: 144 us -> none  [shards(): lax.psum_scatter(lax.dot_general(columns, orthonormal, (((0,), (0,)), (()...]
    psum x1 -> x0, blocking collectives: 101 us -> none  [shards(): lax.psum(jnp.sum(column_mine * column_mine, axis=0), ('fsdp', 'tensor'))]
    all_to_all x0 -> x5, blocking collectives: none -> 95.1 us  [swap(): return lax.all_to_all(pieces, axis, 0, 0)]
    all_gather x2 -> x0, waiting for transfers between devices: 93.9 us -> none  [the longest x1 93.9 us: shards(): lax.all_gather(right_factor, 'fsdp', axis=0, tiled=True)]
    pallas_call x0 -> x15, Pallas kernels: none -> 55 us  [the longest x1 13.3 us: shards(): call(first_half_kernel, shape(RANK, RANK), [VMEM, ANY], flops=15000000000)]
    another operation x9 -> x0, other arithmetic: 54.5 us -> none  [the longest x6 34 us: orthonormalize(): lower_factor = jnp.linalg.cholesky(gram_matrix)]
    all_to_all x0 -> x6, starting transfers between devices: none -> 35.1 us  [swap(): return lax.all_to_all(pieces, axis, 0, 0)]
  transfers between devices with their start and end apart: 5 -> 12, of which waited for: 4 -> 9; matrix products, arithmetic and copies ran while one was open for 0% -> 0% of each run, Pallas kernels for 0% -> 18%
where the time goes in v1:
time: 253 us; the launch traced here: 252 us
  blocking collectives  95.1 us (38%)
  starting transfers between devices  57.7 us (23%)
  Pallas kernels  55 us (22%)
  waiting for transfers between devices  41.7 us (16%)
    all_to_all x5, blocking collectives, swap(): return lax.all_to_all(pieces, axis, 0, 0)  95.1 us
    all_to_all x6, starting transfers between devices, swap(): return lax.all_to_all(pieces, axis, 0, 0)  35.1 us
    all_to_all x6, waiting for transfers between devices, swap(): return lax.all_to_all(pieces, axis, 0, 0)  26.5 us
    ppermute x3, starting transfers between devices, other_core(): return lax.ppermute(value, 'c', [(0, 1), (1, 0)])  16.3 us
    pallas_call x1, Pallas kernels, shards(): call(first_half_kernel, shape(RANK, RANK), [VMEM, ANY], flops=15000000000)  13.3 us
    pallas_call x1, Pallas kernels, shards(): call(second_half_kernel, shape(RANK, RANK), [VMEM, ANY], flops=15000000000)  12.7 us
    ppermute x3, waiting for transfers between devices, shards(): lax.ppermute(squares, 'y', [(i, i ^ bit) for i in range(NY)])  11.7 us
    pallas_call x1, Pallas kernels, shards(): call(column_kernel, [in_hbm(CHIPS, SHARD, RANK)] * 2, [SMEM, VMEM, HBM, H...  8.58 us
  transfers between devices with their start and end apart: 12, of which 9 were waited for; matrix products, arithmetic and copies ran while one was open for 0% of the time, Pallas kernels for 18%

profile of v1, /device:TPU:1, one launch (start us, length us, event | category | flops | bytes accessed | tf_op | source)
XLA Modules:
  0.0 252.0 jit_solution(18123328328939983571)
XLA Ops:
  1.5 25.2 %all_to_all.55 = f32[8,56,256]{2,1,0:T(8,128)S(1)} all-to-all(f32[8,56,256]{2,1,0:T(8,128)S(1)} %broadcast_in_dim.8), channel_id=1, replica_groups=mesh['x'=4,'z'=8,'c'=2,'y'=8] {'z'}, dimensions={0} | all-to-all | bytes 917504 | tf_op jit(solution)/shard_map/all_to_all | solution.py:268
  26.8 24.3 %all_to_all.56 = f32[4,8,56,256]{3,2,1,0:T(8,128)S(1)} all-to-all(f32[4,8,56,256]{3,2,1,0:T(8,128)S(1)} %broadcast_in_dim.9), channel_id=1, replica_groups=mesh['x'=4,'z'=8,'c'=2,'y'=8] {'x'}, dimensions={0} | all-to-all | bytes 3670016 | tf_op jit(solution)/shard_map/all_to_all | solution.py:268
  51.1 5.9 %collective-permute-start = (f32[32,56,256]{2,1,0:T(8,128)S(1)}, f32[32,56,256]{2,1,0:T(8,128)}, u32[]{:S(2)}, u32[]{:S(2)}) collective-permute-start(f32[32,56,256]{2,1,0:T(8,128)S(1)} %bitcast.9), channel_id=1, source_target_pairs={{0,8},{8,0},{1,9},{9,1},{2,10},{10,2},{3,11},{11,3},{4,12},{12,4},... | collective-permute-start | bytes 5505032 | tf_op jit(solution)/shard_map/ppermute | solution.py:272
  57.0 3.5 %collective-permute-done.other = f32[32,56,256]{2,1,0:T(8,128)} collective-permute-done((f32[32,56,256]{2,1,0:T(8,128)S(1)}, f32[32,56,256]{2,1,0:T(8,128)}, u32[]{:S(2)}, u32[]{:S(2)}) %collective-permute-start) | collective-permute-done | bytes 1835040 | tf_op jit(solution)/shard_map/ppermute | solution.py:272
  60.5 5.4 %shard_map.58 = f32[128,256]{1,0:T(8,128)S(1)} custom-call(s32[1]{0:T(128)} %bitcast.where, f32[32,56,256]{2,1,0:T(8,128)S(1)} %bitcast.10, f32[32,56,256]{2,1,0:T(8,128)} %collective-permute-done.other, f32[128,3584]{1,0:T(8,128)} %mom.5, bf16[128,3584]{1,0:T(8,128)(2,1)} %grad.5), custom_call_target="tpu_custom_call" | custom-call | flops 1409286144 | bytes 7000000 | tf_op jit(solution)/shard_map/pallas_call | solution.py:282
  65.9 14.5 %all_to_all.57.pieces = f32[8,16,256]{2,1,0:T(8,128)S(1)} all-to-all(f32[8,16,256]{2,1,0:T(8,128)S(1)} %bitcast.14), channel_id=1, replica_groups=mesh['x'=4,'z'=8,'c'=2,'y'=8] {'y'}, dimensions={0} | all-to-all | bytes 262144 | tf_op jit(solution)/shard_map/all_to_all | solution.py:268
  80.4 10.4 %all_to_all.58 = f32[8,16,256]{2,1,0:T(8,128)S(1)} all-to-all(f32[8,16,256]{2,1,0:T(8,128)S(1)} %shard_map.59), channel_id=1, replica_groups=mesh['x'=4,'z'=8,'c'=2,'y'=8] {'y'}, dimensions={0} | all-to-all | bytes 262144 | tf_op jit(solution)/shard_map/all_to_all | solution.py:268
  92.0 7.5 %all-to-all-start.4 = ((f32[64,8,128]{2,1,0:T(8,128)}), f32[64,8,128]{2,1,0:T(8,128)S(1)}, u32[]{:S(2)}, u32[]{:S(2)}) async-start(f32[64,8,128]{2,1,0:T(8,128)} %get-tuple-element.24), calls=%async_computation.4 | async-start | bytes 524288 | tf_op jit(solution)/shard_map/all_to_all | solution.py:268
  99.5 8.6 %shard_map.61 = (f32[32,56,256]{2,1,0:T(8,128)}, f32[32,56,256]{2,1,0:T(8,128)}) custom-call(s32[1]{0:T(128)} %bitcast.where, f32[128,256]{1,0:T(8,128)S(1)} %bitcast.12, f32[128,3584]{1,0:T(8,128)} %mom.5, bf16[128,3584]{1,0:T(8,128)(2,1)} %grad.5, f32[8,128]{1,0:T(8,128)S(1)} %get-tuple-element.21.after), custom_call_target="tpu_custom_call" | custom-call | flops 1409286144 | bytes 7000000 | tf_op jit(solution)/shard_map/pallas_call | solution.py:293
  114.6 6.6 %all-to-all-start.6 = ((f32[64,8,128]{2,1,0:T(8,128)}), f32[64,8,128]{2,1,0:T(8,128)S(1)}, u32[]{:S(2)}, u32[]{:S(2)}) async-start(f32[64,8,128]{2,1,0:T(8,128)} %shard_map.62.after), calls=%async_computation.6 | async-start | bytes 524288 | tf_op jit(solution)/shard_map/all_to_all | solution.py:268
  121.3 3.8 %shard_map.63 = (f32[32,56,256]{2,1,0:T(8,128)}, f32[8,128]{1,0:T(8,128)S(1)}) custom-call(f32[32,56,256]{2,1,0:T(8,128)} %get-tuple-element.22.mine, f32[32,56,256]{2,1,0:T(8,128)S(1)} %collective-permute-done.1.arrived, f32[64,8,128]{2,1,0:T(8,128)} %shard_map.62.after), custom_call_target="tpu_custom_call" | custom-call | flops 1000000 | bytes 6000000 | tf_op jit(solution)/shard_map/pallas_call | solution.py:302
  125.0 8.2 %all-to-all-done.6.gram = f32[64,8,128]{2,1,0:T(8,128)S(1)} async-done(((f32[64,8,128]{2,1,0:T(8,128)}), f32[64,8,128]{2,1,0:T(8,128)S(1)}, u32[]{:S(2)}, u32[]{:S(2)}) %all-to-all-start.6) | async-done | bytes 262176 | tf_op jit(solution)/shard_map/all_to_all | solution.py:268
  133.3 3.8 %all-to-all-start.5 = ((f32[4,8,56,256]{3,2,1,0:T(8,128)}), f32[4,8,56,256]{3,2,1,0:T(8,128)S(1)}, u32[]{:S(2)}, u32[]{:S(2)}) async-start(f32[4,8,56,256]{3,2,1,0:T(8,128)} %bitcast.15), calls=%async_computation.5 | async-start | bytes 3670016 | tf_op jit(solution)/shard_map/all_to_all | solution.py:268
  137.1 13.3 %shard_map.64.after.half = f32[256,256]{1,0:T(8,128)S(1)} custom-call(f32[64,8,128]{2,1,0:T(8,128)S(1)} %all-to-all-done.6.gram, f32[8,128]{1,0:T(8,128)S(1)} %get-tuple-element.28.after), custom_call_target="tpu_custom_call" | custom-call | flops 15000000512 | bytes 100000 | tf_op jit(solution)/shard_map/pallas_call | solution.py:316
  150.4 9.6 %all-to-all-done.5.pieces = f32[4,8,56,256]{3,2,1,0:T(8,128)S(1)} async-done(((f32[4,8,56,256]{3,2,1,0:T(8,128)}), f32[4,8,56,256]{3,2,1,0:T(8,128)S(1)}, u32[]{:S(2)}, u32[]{:S(2)}) %all-to-all-start.5) | async-done | bytes 1835040 | tf_op jit(solution)/shard_map/all_to_all | solution.py:268
  160.9 3.9 %all-to-all-start.7 = ((f32[8,56,256]{2,1,0:T(8,128)}), f32[8,56,256]{2,1,0:T(8,128)S(1)}, u32[]{:S(2)}, u32[]{:S(2)}) async-start(f32[8,56,256]{2,1,0:T(8,128)} %get-tuple-element.29), calls=%async_computation.7 | async-start | bytes 917504 | tf_op jit(solution)/shard_map/all_to_all | solution.py:268
  164.8 12.7 %shard_map.66.after.inverse = f32[256,256]{1,0:T(8,128)S(1)} custom-call(f32[256,256]{1,0:T(8,128)S(1)} %shard_map.64.after.half, f32[8,128]{1,0:T(8,128)S(1)} %get-tuple-element.30.after), custom_call_target="tpu_custom_call" | custom-call | flops 15000000512 | bytes 100000 | tf_op jit(solution)/shard_map/pallas_call | solution.py:323
  180.2 4.7 %all-to-all-start.8 = ((f32[8,56,256]{2,1,0:T(8,128)}), f32[8,56,256]{2,1,0:T(8,128)S(1)}, u32[]{:S(2)}, u32[]{:S(2)}) async-start(f32[8,56,256]{2,1,0:T(8,128)} %get-tuple-element.31.after), calls=%async_computation.8 | async-start | bytes 917504 | tf_op jit(solution)/shard_map/all_to_all | solution.py:268
  191.6 3.6 %collective-permute-done.3 = f32[1,256]{1,0:T(1,128)S(1)} collective-permute-done((f32[1,256]{1,0:T(1,128)S(1)}, f32[1,256]{1,0:T(1,128)S(1)}, u32[]{:S(2)}, u32[]{:S(2)}) %collective-permute-start.3) | collective-permute-done | bytes 1056 | tf_op jit(solution)/shard_map/ppermute | solution.py:335
  197.3 6.0 %collective-permute-done.4 = f32[1,256]{1,0:T(1,128)S(1)} collective-permute-done((f32[1,256]{1,0:T(1,128)S(1)}, f32[1,256]{1,0:T(1,128)S(1)}, u32[]{:S(2)}, u32[]{:S(2)}) %collective-permute-start.4) | collective-permute-done | bytes 1056 | tf_op jit(solution)/shard_map/ppermute | solution.py:335
  204.1 20.8 %all_to_all.59 = f32[4,8,56,256]{3,2,1,0:T(8,128)S(1)} all-to-all(f32[4,8,56,256]{3,2,1,0:T(8,128)S(1)} %shard_map.69), channel_id=1, replica_groups=mesh['x'=4,'z'=8,'c'=2,'y'=8] {'x'}, dimensions={0} | all-to-all | bytes 3670016 | tf_op jit(solution)/shard_map/all_to_all | solution.py:268
  224.9 8.1 %collective-permute-start.5 = (f32[32,56,256]{2,1,0:T(8,128)S(1)}, f32[32,56,256]{2,1,0:T(8,128)}, u32[]{:S(2)}, u32[]{:S(2)}) collective-permute-start(f32[32,56,256]{2,1,0:T(8,128)S(1)} %bitcast.7), channel_id=1, source_target_pairs={{0,8},{8,0},{1,9},{9,1},{2,10},{10,2},{3,11},{11,3},{4,12},{12,4},... | collective-permute-start | bytes 5505032 | tf_op jit(solution)/shard_map/ppermute | solution.py:272
  233.0 8.5 %all-to-all-start.10 = ((f32[64,1,256]{2,1,0:T(1,128)}), f32[64,1,256]{2,1,0:T(1,128)S(1)}, u32[]{:S(2)}, u32[]{:S(2)}) async-start(f32[64,1,256]{2,1,0:T(1,128)} %broadcast_in_dim.11.after), calls=%async_computation.10 | async-start | bytes 131072 | tf_op jit(solution)/shard_map/all_to_all | solution.py:268
  242.7 5.4 %shard_map.71 = (f32[128,3584]{1,0:T(8,128)}, f32[8,128]{1,0:T(8,128)S(1)}) custom-call(s32[1]{0:T(128)} %bitcast.where, f32[32,56,256]{2,1,0:T(8,128)S(1)} %bitcast.8, f32[32,56,256]{2,1,0:T(8,128)} %collective-permute-done.5.other, f32[128,256]{1,0:T(8,128)S(1)} %get-tuple-element.34.weights, f32[128,3584]{1,0:T(8,128)} %mom.5, bf16[128,3584]{1,0:T(8,128)(2,1)} %grad.5), custom_call_target="tpu_custom_call" | custom-call | flops 704643072 | bytes 9000000 | tf_op jit(solution)/shard_map/pallas_call | solution.py:345
  (26 shorter events, 26.9 us)
Async XLA Ops:
  51.1 9.5 %collective-permute-start = (f32[32,56,256]{2,1,0:T(8,128)S(1)}, f32[32,56,256]{2,1,0:T(8,128)}, u32[]{:S(2)}, u32[]{:S(2)}) collective-permute-start(f32[32,56,256]{2,1,0:T(8,128)S(1)} %bitcast.9), channel_id=1, source_target_pairs={{0,8},{8,0},{1,9},{9,1},{2,10},{10,2},{3,11},{11,3},{4,12},{12,4},... | collective-permute-start | bytes 5505032 | tf_op jit(solution)/shard_map/ppermute | solution.py:272
  92.0 19.5 %all-to-all-start.4 = ((f32[64,8,128]{2,1,0:T(8,128)}), f32[64,8,128]{2,1,0:T(8,128)S(1)}, u32[]{:S(2)}, u32[]{:S(2)}) async-start(f32[64,8,128]{2,1,0:T(8,128)} %get-tuple-element.24), calls=%async_computation.4 | async-start | bytes 524288 | tf_op jit(solution)/shard_map/all_to_all | solution.py:268
  112.3 9.0 %collective-permute-start.1 = (f32[32,56,256]{2,1,0:T(8,128)}, f32[32,56,256]{2,1,0:T(8,128)S(1)}, u32[]{:S(2)}, u32[]{:S(2)}) collective-permute-start(f32[32,56,256]{2,1,0:T(8,128)} %get-tuple-element.25), channel_id=1, source_target_pairs={{0,8},{8,0},{1,9},{9,1},{2,10},{10,2},{3,11},{11,3},{4,12},{12,4},... | collective-permute-start | bytes 5505032 | tf_op jit(solution)/shard_map/ppermute | solution.py:272
  114.6 18.6 %all-to-all-start.6 = ((f32[64,8,128]{2,1,0:T(8,128)}), f32[64,8,128]{2,1,0:T(8,128)S(1)}, u32[]{:S(2)}, u32[]{:S(2)}) async-start(f32[64,8,128]{2,1,0:T(8,128)} %shard_map.62.after), calls=%async_computation.6 | async-start | bytes 524288 | tf_op jit(solution)/shard_map/all_to_all | solution.py:268
  133.3 26.7 %all-to-all-start.5 = ((f32[4,8,56,256]{3,2,1,0:T(8,128)}), f32[4,8,56,256]{3,2,1,0:T(8,128)S(1)}, u32[]{:S(2)}, u32[]{:S(2)}) async-start(f32[4,8,56,256]{3,2,1,0:T(8,128)} %bitcast.15), calls=%async_computation.5 | async-start | bytes 3670016 | tf_op jit(solution)/shard_map/all_to_all | solution.py:268
  160.9 18.6 %all-to-all-start.7 = ((f32[8,56,256]{2,1,0:T(8,128)}), f32[8,56,256]{2,1,0:T(8,128)S(1)}, u32[]{:S(2)}, u32[]{:S(2)}) async-start(f32[8,56,256]{2,1,0:T(8,128)} %get-tuple-element.29), calls=%async_computation.7 | async-start | bytes 917504 | tf_op jit(solution)/shard_map/all_to_all | solution.py:268
  180.2 23.1 %all-to-all-start.8 = ((f32[8,56,256]{2,1,0:T(8,128)}), f32[8,56,256]{2,1,0:T(8,128)S(1)}, u32[]{:S(2)}, u32[]{:S(2)}) async-start(f32[8,56,256]{2,1,0:T(8,128)} %get-tuple-element.31.after), calls=%async_computation.8 | async-start | bytes 917504 | tf_op jit(solution)/shard_map/all_to_all | solution.py:268
  185.3 4.3 %collective-permute-start.2 = (f32[1,256]{1,0:T(1,128)S(1)}, f32[1,256]{1,0:T(1,128)S(1)}, u32[]{:S(2)}, u32[]{:S(2)}) collective-permute-start(f32[1,256]{1,0:T(1,128)S(1)} %get-tuple-element.33), channel_id=1, source_target_pairs={{0,1},{1,0},{2,3},{3,2},{4,5},{5,4},{6,7},{7,6},{8,9},{9,8},{10,11... | collective-permute-start | bytes 3080 | tf_op jit(solution)/shard_map/ppermute | solution.py:335
  189.6 5.5 %collective-permute-start.3 = (f32[1,256]{1,0:T(1,128)S(1)}, f32[1,256]{1,0:T(1,128)S(1)}, u32[]{:S(2)}, u32[]{:S(2)}) collective-permute-start(f32[1,256]{1,0:T(1,128)S(1)} %add.9), channel_id=1, source_target_pairs={{0,2},{1,3},{2,0},{3,1},{4,6},{5,7},{6,4},{7,5},{8,10},{9,11},{10,... | collective-permute-start | bytes 3080 | tf_op jit(solution)/shard_map/ppermute | solution.py:335
  195.1 8.2 %collective-permute-start.4 = (f32[1,256]{1,0:T(1,128)S(1)}, f32[1,256]{1,0:T(1,128)S(1)}, u32[]{:S(2)}, u32[]{:S(2)}) collective-permute-start(f32[1,256]{1,0:T(1,128)S(1)} %add.10), channel_id=1, source_target_pairs={{0,4},{1,5},{2,6},{3,7},{4,0},{5,1},{6,2},{7,3},{8,12},{9,13},{10,... | collective-permute-start | bytes 3080 | tf_op jit(solution)/shard_map/ppermute | solution.py:335
  224.9 17.7 %collective-permute-start.5 = (f32[32,56,256]{2,1,0:T(8,128)S(1)}, f32[32,56,256]{2,1,0:T(8,128)}, u32[]{:S(2)}, u32[]{:S(2)}) collective-permute-start(f32[32,56,256]{2,1,0:T(8,128)S(1)} %bitcast.7), channel_id=1, source_target_pairs={{0,8},{8,0},{1,9},{9,1},{2,10},{10,2},{3,11},{11,3},{4,12},{12,4},... | collective-permute-start | bytes 5505032 | tf_op jit(solution)/shard_map/ppermute | solution.py:272
  233.0 18.3 %all-to-all-start.10 = ((f32[64,1,256]{2,1,0:T(1,128)}), f32[64,1,256]{2,1,0:T(1,128)S(1)}, u32[]{:S(2)}, u32[]{:S(2)}) async-start(f32[64,1,256]{2,1,0:T(1,128)} %broadcast_in_dim.11.after), calls=%async_computation.10 | async-start | bytes 131072 | tf_op jit(solution)/shard_map/all_to_all | solution.py:268

commit v2 on v1

v2 whole, which is shorter than its diff:
```python
import math

import jax
import jax.numpy as jnp
import numpy as np
from jax import lax
from jax.experimental import pallas as pl
from jax.experimental.pallas import tpu as pltpu
from jax.sharding import Mesh, PartitionSpec as P

ROWS = 8192
COLS = 28672
RANK = 256
NX, NZ, NC, NY = 4, 8, 2, 8
MY_ROWS = 128
MY_COLS = 3584
SHARD = 56
CHUNK = NZ * NC * SHARD
BLOCK = 32
MACS = MY_ROWS * MY_COLS * RANK

highest = lax.Precision.HIGHEST
f32 = jnp.float32
bf16 = jnp.bfloat16
VMEM = pl.BlockSpec(memory_space=pltpu.VMEM)
SMEM = pl.BlockSpec(memory_space=pltpu.SMEM)
ANY = pl.BlockSpec(memory_space=pl.ANY)
HBM = pl.BlockSpec(memory_space=pltpu.HBM)


def dot(a, b, ca, cb, precision=highest):
    return lax.dot_general(
        a, b, (((ca,), (cb,)), ((), ())), precision=precision, preferred_element_type=f32
    )


def shape(*dims):
    return jax.ShapeDtypeStruct(dims, f32)


def in_hbm(*dims):
    return pltpu.HBM(dims, f32)


TOKEN = shape(8, 128)


def call(kernel, out_shape, in_specs, scratch=(), out_specs=None, flops=1_000_000, nbytes=100_000, limit=12):
    return pl.pallas_call(
        kernel,
        out_shape=out_shape,
        in_specs=in_specs,
        out_specs=out_specs or jax.tree.map(lambda _: VMEM, out_shape),
        scratch_shapes=scratch,
        compiler_params=pltpu.CompilerParams(vmem_limit_bytes=limit * 2**20),
        cost_estimate=pl.CostEstimate(
            flops=flops, bytes_accessed=nbytes, transcendentals=0
        ),
    )


def columns(x, dx):
    return pl.ds(pl.multiple_of(lax.rem(x - dx + NX, NX) * CHUNK, 128), CHUNK)


def buffer_copies(cols, mom, grad, mom_here, grad_here, sems, j):
    return [
        pltpu.make_async_copy(mom.at[:, cols], mom_here.at[:, cols], sems.at[j, 0]),
        pltpu.make_async_copy(grad.at[:, cols], grad_here.at[:, cols], sems.at[j, 1]),
    ]


def factor_copies(core, own, other, full, sems, j):
    return [
        pltpu.make_async_copy(own, full.at[j, :, core], sems.at[j, 2]),
        pltpu.make_async_copy(other, full.at[j, :, 1 - core], sems.at[j, 3]),
    ]


def gathered_copies(where, pieces, mom, grad, mom_here, grad_here, full, sems):
    copies = []
    for j in range(NX):
        copies.append(
            factor_copies(where[1], pieces[j], pieces[NX + j], full, sems, j)
            + buffer_copies(columns(where[0], j), mom, grad, mom_here, grad_here, sems, j)
        )
        for copy in copies[j]:
            copy.start()
    return copies


def buffer_chunk(mom, grad, cols):
    return mom[:, cols] + grad[:, cols].astype(f32)


BUFFER_SCRATCH = [pltpu.VMEM((MY_ROWS, MY_COLS), f32), pltpu.VMEM((MY_ROWS, MY_COLS), bf16)]
SEMS = [pltpu.SemaphoreType.DMA((NX, 4))]
FULL = [pltpu.VMEM((NX, NZ, NC, SHARD, RANK), f32)]


def power_kernel(where, *refs):
    pieces, (mom, grad, out, mom_here, grad_here, full, sems) = refs[:8], refs[8:]
    copies = gathered_copies(where, pieces, mom, grad, mom_here, grad_here, full, sems)
    total = None
    for j in range(NX):
        for copy in copies[j]:
            copy.wait()
        part = full[j].reshape(CHUNK, RANK)
        part = dot(buffer_chunk(mom_here, grad_here, columns(where[0], j)), part, 1, 0)
        total = part if total is None else total + part
    out[...] = total


def sum_spread_kernel(pieces, out):
    total = jnp.sum(pieces[...], axis=0)
    for i in range(out.shape[0]):
        out[i] = total


def gram_kernel(power, out, token):
    token[...] = jnp.zeros_like(token)
    gram = dot(power[...], power[...], 0, 0)
    for i in range(RANK // 8):
        for h in range(RANK // 128):
            out[i * 2 + h] = gram[i * 8 : i * 8 + 8, h * 128 : h * 128 + 128]


def column_kernel(where, power, mom, grad, after, keep, send, mom_here, grad_here, full, sems):
    copies = []
    for j in range(NX):
        copies.append(
            buffer_copies(columns(where[0], -j), mom, grad, mom_here, grad_here, sems, j)
        )
        for copy in copies[j]:
            copy.start()
    for j in range(NX):
        for copy in copies[j]:
            copy.wait()
        part = dot(buffer_chunk(mom_here, grad_here, columns(where[0], -j)), power[...], 0, 0)
        full[j] = part.reshape(NZ, NC, SHARD, RANK)
        copies[j] = [
            pltpu.make_async_copy(full.at[j, :, 1 - where[1]], send.at[j], sems.at[j, 2]),
            pltpu.make_async_copy(full.at[j, :, where[1]], keep.at[j], sems.at[j, 3]),
        ]
        for copy in copies[j]:
            copy.start()
    for j in range(NX):
        for copy in copies[j]:
            copy.wait()


def sum_kernel(a, b, c, d, after, out, token):
    token[...] = jnp.zeros_like(token)
    out[...] = (a[...] + b[...]) + (c[...] + d[...])


def column_mine_kernel(pieces, after, mine, copies):
    total = jnp.sum(pieces[...], axis=0)
    mine[...] = total
    for i in range(NZ):
        copies[i] = total


def eliminate(a, blocks):
    row = lax.broadcasted_iota(jnp.int32, (BLOCK, BLOCK), 0)
    col = lax.broadcasted_iota(jnp.int32, (BLOCK, BLOCK), 1)
    eye = (row == col).astype(f32)
    wide = lax.broadcasted_iota(jnp.int32, (BLOCK, RANK), 1)
    for k in blocks:
        lo, hi = k * BLOCK, (k + 1) * BLOCK
        d = a[lo:hi, lo:hi]
        for j in range(BLOCK - 1):
            column = jnp.broadcast_to(d[:, j : j + 1], (BLOCK, BLOCK))
            pivot = jnp.broadcast_to(1.0 / column[j : j + 1, :], (BLOCK, BLOCK))
            line = jnp.broadcast_to(d[j : j + 1, :], (BLOCK, BLOCK))
            line = jnp.where(col == j, 1.0, line)
            rest = jnp.where(col == j, 0.0, d)
            d = jnp.where(row > j, rest - column * (line * pivot), d)
        diagonal = jnp.sum(d * eye, axis=1, keepdims=True)
        inner = (jnp.where(row > col, d, 0.0) + eye) * lax.rsqrt(diagonal)
        panel = a[lo:hi, :]
        panel = jnp.where((wide >= lo) & (wide < hi), 0.0, panel)
        panel = dot(inner, panel, 1, 0)
        a[lo:hi, :] = panel
        a[lo:hi, lo:hi] = inner
        panel = a[lo:hi, :]
        if hi < RANK:
            change = dot(panel, panel, 0, 0)
            a[hi:, lo:hi] = jnp.zeros((RANK - hi, BLOCK), f32)
            a[hi:, :] = a[hi:, :] - change[hi:, :]


def first_half_kernel(gram, a):
    for i in range(RANK // 8):
        for h in range(RANK // 128):
            a[i * 8 : i * 8 + 8, h * 128 : h * 128 + 128] = gram[i * 2 + h]
    eliminate(a, range(0, RANK // BLOCK // 2))


def second_half_kernel(half, after, a):
    a[...] = half[...]
    eliminate(a, range(RANK // BLOCK // 2, RANK // BLOCK))
    row = lax.broadcasted_iota(jnp.int32, (RANK, RANK), 0)
    col = lax.broadcasted_iota(jnp.int32, (RANK, RANK), 1)
    a[...] = jnp.where(col <= row, a[...], 0.0)


def squares_kernel(column_mine, inverse, after, factor_mine, squares):
    c = dot(column_mine[...], inverse[...], 1, 1)
    factor_mine[...] = c
    squares[...] = jnp.sum(c * c, axis=0, keepdims=True)


def ortho_kernel(power, inverse, row_factor, weights):
    o = dot(power[...], inverse[...], 1, 1)
    row_factor[...] = o * math.sqrt(ROWS)
    weights[...] = 0.05 * dot(o, inverse[...], 1, 0)


def new_right_kernel(pieces, factor_mine, out):
    squares = jnp.sum(pieces[...], axis=0)
    out[...] = factor_mine[...] / jnp.sqrt(squares / COLS + 1e-06)


def split(value):
    high = value.astype(bf16)
    return high, (value - high.astype(f32)).astype(bf16)


def momentum_kernel(where, *refs):
    pieces, (weights, mom, grad, out, mom_here, grad_here, full, sems, done) = refs[:8], refs[8:]
    copies = gathered_copies(where, pieces, mom, grad, mom_here, grad_here, full, sems)
    high, low = split(weights[...])
    for j in range(NX):
        for copy in copies[j]:
            copy.wait()
        fh, fl = split(full[j].reshape(CHUNK, RANK))
        change = dot(high, fh, 1, 1, None) + (dot(high, fl, 1, 1, None) + dot(low, fh, 1, 1, None))
        cols = columns(where[0], j)
        mom_here[:, cols] = buffer_chunk(mom_here, grad_here, cols) - change
        copies[j] = pltpu.make_async_copy(mom_here.at[:, cols], out.at[:, cols], done.at[j])
        copies[j].start()
    for j in range(NX):
        copies[j].wait()


def spread(value, axis, size):
    copies = jnp.broadcast_to(value[None], (size,) + value.shape)
    return swap(copies, axis)


def swap(pieces, axis):
    return lax.all_to_all(pieces, axis, 0, 0)


def other_core(value):
    return lax.ppermute(value, "c", [(0, 1), (1, 0)])


def shift(value, by):
    return lax.ppermute(value, "x", [(i, (i + by) % NX) for i in range(NX)])


def gather_rest(block):
    own = [block] + [shift(block, d) for d in (1, 2, 3)]
    return own + [other_core(piece) for piece in own]


def shards(momentum, gradient, right_factor):
    where = jnp.stack([lax.axis_index("x"), lax.axis_index("c")]).astype(jnp.int32)
    momentum = pltpu.with_memory_space_constraint(momentum, pltpu.HBM)
    gradient = pltpu.with_memory_space_constraint(gradient, pltpu.HBM)
    fsdp = ("x", "z", "c")

    pieces = gather_rest(spread(right_factor, "z", NZ))
    partial_power = call(
        power_kernel, shape(MY_ROWS, RANK), [SMEM] + [HBM] * 10,
        BUFFER_SCRATCH + FULL + SEMS, None, 12 * MACS, 7_000_000,
    )(where, *pieces, momentum, gradient)

    pieces = swap(partial_power.reshape(NY, MY_ROWS // NY, RANK), "y")
    copies = call(sum_spread_kernel, shape(NY, MY_ROWS // NY, RANK), [VMEM])(pieces)
    power = swap(copies, "y").reshape(MY_ROWS, RANK)

    gram, token = call(gram_kernel, [shape(64, 8, 128), TOKEN], [VMEM])(power)
    gram = swap(gram, fsdp)
    keep, send = call(
        column_kernel, [in_hbm(NX, NZ, SHARD, RANK)] * 2, [SMEM, VMEM, HBM, HBM, ANY],
        BUFFER_SCRATCH + FULL + SEMS, [HBM, HBM], 12 * MACS, 7_000_000,
    )(where, power, momentum, gradient, token)
    gram = call(sum_spread_kernel, shape(64, 8, 128), [VMEM])(gram)
    send, gram = lax.optimization_barrier((send, gram))
    arrived = other_core(send)
    sums = [keep[d] + arrived[d] for d in range(NX)]
    gram, *sums[1:] = lax.optimization_barrier((gram, *sums[1:]))
    parts = [sums[0]] + [shift(sums[d], d) for d in (1, 2, 3)]
    half = call(first_half_kernel, shape(RANK, RANK), [VMEM], flops=15_000_000_000)(
        swap(gram, fsdp)
    )
    by_z, token = call(
        sum_kernel, [shape(NZ, SHARD, RANK), TOKEN], [VMEM] * 4 + [ANY], nbytes=3_000_000
    )(*parts, half)
    swapped = swap(by_z, "z")
    inverse = call(
        second_half_kernel, shape(RANK, RANK), [VMEM, ANY], flops=15_000_000_000
    )(half, token)
    column_mine, copies = call(
        column_mine_kernel, [shape(SHARD, RANK), shape(NZ, SHARD, RANK)], [VMEM, ANY]
    )(swapped, inverse)

    gathered = swap(copies, "z")
    factor_mine, squares = call(
        squares_kernel, [shape(SHARD, RANK), shape(1, RANK)], [VMEM, VMEM, ANY]
    )(column_mine, inverse, copies)
    squares = squares + other_core(squares)
    for bit in (1, 2):
        squares = squares + lax.ppermute(squares, "x", [(i, i ^ bit) for i in range(NX)])
    row_factor, weights = call(
        ortho_kernel, [shape(MY_ROWS, RANK)] * 2, [VMEM, VMEM]
    )(power, inverse)
    gathered, squares, weights = lax.optimization_barrier((gathered, squares, weights))
    squares = swap(jnp.broadcast_to(squares[None], (64, 1, RANK)), ("z", "y"))
    own = [gathered] + [shift(gathered, d) for d in (1, 2, 3)]
    squares, *own[1:] = lax.optimization_barrier((squares, *own[1:]))
    pieces = own + [other_core(piece) for piece in own]
    new_right = call(new_right_kernel, shape(SHARD, RANK), [VMEM, VMEM])(squares, factor_mine)
    new_momentum = call(
        momentum_kernel, in_hbm(MY_ROWS, MY_COLS), [SMEM] + [HBM] * 8 + [VMEM, HBM, HBM],
        BUFFER_SCRATCH + FULL + SEMS + [pltpu.SemaphoreType.DMA((NX,))],
        HBM, 6 * MACS, 9_000_000,
    )(where, *pieces, weights, momentum, gradient)
    return (new_momentum, new_right, row_factor)


def solution(mesh):
    devices = np.asarray(mesh.devices).reshape(NX, NZ, NC, NY)
    grid = Mesh(devices, ("x", "z", "c", "y"))
    fsdp = ("x", "z", "c")
    return jax.shard_map(
        shards,
        mesh=grid,
        in_specs=(P(fsdp, "y"), P(fsdp, "y"), P(("y",) + fsdp, None)),
        out_specs=(P(fsdp, "y"), P(("y",) + fsdp, None), P(fsdp, None)),
        check_vma=False,
    )
```

time: 253 us -> 249 us (0.984)
  starting transfers between devices: 57.7 us -> 112 us
  blocking collectives: 95.1 us -> 50.1 us
  waiting for transfers between devices: 41.7 us -> 28 us
  other arithmetic: 0.01 us -> 2.6 us
    all_to_all x5 -> x3, blocking collectives: 95.1 us -> 50.1 us  [swap(): return lax.all_to_all(pieces, axis, 0, 0)]
    ppermute x3 -> x11, starting transfers between devices: 6.29 us -> 39.2 us  [the longest x9 31.1 us: shift(): return lax.ppermute(value, 'x', [(i, (i + by) % NX) for i in range(NX)])]
    ppermute x3 -> x10, starting transfers between devices: 16.3 us -> 40.8 us  [other_core(): return lax.ppermute(value, 'c', [(0, 1), (1, 0)])]
    all_to_all x6 -> x5, waiting for transfers between devices: 26.5 us -> 12.1 us  [swap(): return lax.all_to_all(pieces, axis, 0, 0)]
    all_to_all x6 -> x5, starting transfers between devices: 35.1 us -> 31.9 us  [swap(): return lax.all_to_all(pieces, axis, 0, 0)]
    ppermute x3 -> x10, waiting for transfers between devices: 3.52 us -> 6.55 us  [other_core(): return lax.ppermute(value, 'c', [(0, 1), (1, 0)])]
    ppermute x3 -> x11, waiting for transfers between devices: 11.7 us -> 9.39 us  [the longest x9 7.23 us: shift(): return lax.ppermute(value, 'x', [(i, (i + by) % NX) for i in range(NX)])]
    pallas_call x9 -> x7, Pallas kernels: 38.8 us -> 36.6 us  [the longest x1 13.3 us: shards(): call(first_half_kernel, shape(RANK, RANK), [VMEM], flops=15000000000)]
  transfers between devices with their start and end apart: 12 -> 26, of which waited for: 9 -> 13; matrix products, arithmetic and copies ran while one was open for 0% -> 0% of each run, Pallas kernels for 18% -> 15%
where the time goes in v2:
time: 249 us; the launch traced here: 248 us
  starting transfers between devices  112 us (45%)
  Pallas kernels  52.8 us (21%)
  blocking collectives  50.1 us (20%)
  waiting for transfers between devices  28 us (11%)
  other arithmetic  2.6 us (1%)
    all_to_all x3, blocking collectives, swap(): return lax.all_to_all(pieces, axis, 0, 0)  50.1 us
    ppermute x10, starting transfers between devices, other_core(): return lax.ppermute(value, 'c', [(0, 1), (1, 0)])  40.8 us
    all_to_all x5, starting transfers between devices, swap(): return lax.all_to_all(pieces, axis, 0, 0)  31.9 us
    ppermute x9, starting transfers between devices, shift(): return lax.ppermute(value, 'x', [(i, (i + by) % NX) for i in range(NX)])  31.1 us
    pallas_call x1, Pallas kernels, shards(): call(first_half_kernel, shape(RANK, RANK), [VMEM], flops=15000000000)  13.3 us
    pallas_call x1, Pallas kernels, shards(): call(second_half_kernel, shape(RANK, RANK), [VMEM, ANY], flops=15000000000)  12.7 us
    all_to_all x5, waiting for transfers between devices, swap(): return lax.all_to_all(pieces, axis, 0, 0)  12.1 us
    pallas_call x1, Pallas kernels, shards(): call(column_kernel, [in_hbm(NX, NZ, SHARD, RANK)] * 2, [SMEM, VMEM, HBM,...  9.17 us
  transfers between devices with their start and end apart: 26, of which 13 were waited for; matrix products, arithmetic and copies ran while one was open for 0% of the time, Pallas kernels for 15%

profile of v2, /device:TPU:1, one launch (start us, length us, event | category | flops | bytes accessed | tf_op | source)
XLA Modules:
  0.0 247.9 jit_solution(15067214750497405026)
XLA Ops:
  1.5 25.2 %all_to_all.40.refs_0_ = f32[8,56,256]{2,1,0:T(8,128)S(1)} all-to-all(f32[8,56,256]{2,1,0:T(8,128)S(1)} %broadcast_in_dim.6), channel_id=1, replica_groups=mesh['x'=4,'z'=8,'c'=2,'y'=8] {'z'}, dimensions={0} | all-to-all | bytes 917504 | tf_op jit(solution)/shard_map/all_to_all | solution.py:253
  26.7 4.4 %collective-permute-start.2 = (f32[8,56,256]{2,1,0:T(8,128)S(1)}, f32[8,56,256]{2,1,0:T(8,128)S(1)}, u32[]{:S(2)}, u32[]{:S(2)}) collective-permute-start(f32[8,56,256]{2,1,0:T(8,128)S(1)} %all_to_all.40.refs_0_), channel_id=1, source_target_pairs={{0,384},{128,0},{256,128},{384,256},{1,385},{129,1},{257,129},{385... | collective-permute-start | bytes 1376264 | tf_op jit(solution)/shard_map/ppermute | solution.py:261
  36.0 5.3 %collective-permute-start.3 = (f32[8,56,256]{2,1,0:T(8,128)S(1)}, f32[8,56,256]{2,1,0:T(8,128)S(1)}, u32[]{:S(2)}, u32[]{:S(2)}) collective-permute-start(f32[8,56,256]{2,1,0:T(8,128)S(1)} %all_to_all.40.refs_0_), channel_id=1, source_target_pairs={{0,8},{8,0},{1,9},{9,1},{2,10},{10,2},{3,11},{11,3},{4,12},{12,4},... | collective-permute-start | bytes 1376264 | tf_op jit(solution)/shard_map/ppermute | solution.py:257
  41.3 12.2 %collective-permute-start.6 = (f32[8,56,256]{2,1,0:T(8,128)S(1)}, f32[8,56,256]{2,1,0:T(8,128)S(1)}, u32[]{:S(2)}, u32[]{:S(2)}) collective-permute-start(f32[8,56,256]{2,1,0:T(8,128)S(1)} %collective-permute-done.2.refs_3_), channel_id=1, source_target_pairs={{0,8},{8,0},{1,9},{9,1},{2,10},{10,2},{3,11},{11,3},{4,12},{12,4},... | collective-permute-start | bytes 1376264 | tf_op jit(solution)/shard_map/ppermute | solution.py:257
  60.7 5.9 %shard_map.58 = f32[128,256]{1,0:T(8,128)S(1)} custom-call(s32[2]{0:T(128)S(1)} %pad_add_fusion.where, f32[8,56,256]{2,1,0:T(8,128)S(1)} %all_to_all.40.refs_0_, f32[8,56,256]{2,1,0:T(8,128)S(1)} %collective-permute-done.refs_1_, f32[8,56,256]{2,1,0:T(8,128)S(1)} %collective-permute-done.1.refs_2_, f32[8,56,256]{2,1,0:T(8,128)S(1)} %collective-permute-done.2.refs_3_, ...), custom_call_target="tpu_custom_call" | custom-call | flops 1409286144 | bytes 7000000 | tf_op jit(solution)/shard_map/pallas_call | solution.py:276
  66.6 14.5 %all_to_all.41.pieces = f32[8,16,256]{2,1,0:T(8,128)S(1)} all-to-all(f32[8,16,256]{2,1,0:T(8,128)S(1)} %bitcast.16), channel_id=1, replica_groups=mesh['x'=4,'z'=8,'c'=2,'y'=8] {'y'}, dimensions={0} | all-to-all | bytes 262144 | tf_op jit(solution)/shard_map/all_to_all | solution.py:253
  81.1 10.4 %all_to_all.42 = f32[8,16,256]{2,1,0:T(8,128)S(1)} all-to-all(f32[8,16,256]{2,1,0:T(8,128)S(1)} %shard_map.59), channel_id=1, replica_groups=mesh['x'=4,'z'=8,'c'=2,'y'=8] {'y'}, dimensions={0} | all-to-all | bytes 262144 | tf_op jit(solution)/shard_map/all_to_all | solution.py:253
  92.6 8.8 %all-to-all-start.3 = ((f32[64,8,128]{2,1,0:T(8,128)}), f32[64,8,128]{2,1,0:T(8,128)S(1)}, u32[]{:S(2)}, u32[]{:S(2)}) async-start(f32[64,8,128]{2,1,0:T(8,128)} %get-tuple-element.31), calls=%async_computation.3 | async-start | bytes 524288 | tf_op jit(solution)/shard_map/all_to_all | solution.py:253
  101.4 9.2 %shard_map.61 = (f32[4,8,56,256]{3,2,1,0:T(8,128)}, f32[4,8,56,256]{3,2,1,0:T(8,128)}) custom-call(s32[2]{0:T(128)S(1)} %pad_add_fusion.where, f32[128,256]{1,0:T(8,128)S(1)} %bitcast.14, f32[128,3584]{1,0:T(8,128)} %refs_9_.3, bf16[128,3584]{1,0:T(8,128)(2,1)} %refs_10_.1, f32[8,128]{1,0:T(8,128)S(1)} %get-tuple-element.28.after), custom_call_target="tpu_custom_call" | custom-call | flops 1409286144 | bytes 7000000 | tf_op jit(solution)/shard_map/pallas_call | solution.py:287
  116.6 3.6 %collective-permute-done.7 = f32[4,8,56,256]{3,2,1,0:T(8,128)S(1)} collective-permute-done((f32[4,8,56,256]{3,2,1,0:T(8,128)}, f32[4,8,56,256]{3,2,1,0:T(8,128)S(1)}, u32[]{:S(2)}, u32[]{:S(2)}) %collective-permute-start.7) | collective-permute-done | bytes 1835040 | tf_op jit(solution)/shard_map/ppermute | solution.py:257
  122.7 7.4 %all-to-all-start.4 = ((f32[64,8,128]{2,1,0:T(8,128)}), f32[64,8,128]{2,1,0:T(8,128)S(1)}, u32[]{:S(2)}, u32[]{:S(2)}) async-start(f32[64,8,128]{2,1,0:T(8,128)} %shard_map.62), calls=%async_computation.4 | async-start | bytes 524288 | tf_op jit(solution)/shard_map/all_to_all | solution.py:253
  133.4 4.5 %collective-permute-start.9 = (f32[8,56,256]{2,1,0:T(8,128)S(1)}, f32[8,56,256]{2,1,0:T(8,128)S(1)}, u32[]{:S(2)}, u32[]{:S(2)}) collective-permute-start(f32[8,56,256]{2,1,0:T(8,128)S(1)} %get-tuple-element.35), channel_id=1, source_target_pairs={{0,256},{128,384},{256,0},{384,128},{1,257},{129,385},{257,1},{385... | collective-permute-start | bytes 1376264 | tf_op jit(solution)/shard_map/ppermute | solution.py:261
  142.1 13.3 %shard_map.63.after.half = f32[256,256]{1,0:T(8,128)S(1)} custom-call(f32[64,8,128]{2,1,0:T(8,128)S(1)} %all-to-all-done.4.gram), custom_call_target="tpu_custom_call" | custom-call | flops 15000000512 | bytes 100000 | tf_op jit(solution)/shard_map/pallas_call | solution.py:297
  159.4 5.4 %all-to-all-start.5 = ((f32[8,56,256]{2,1,0:T(8,128)}), f32[8,56,256]{2,1,0:T(8,128)S(1)}, u32[]{:S(2)}, u32[]{:S(2)}) async-start(f32[8,56,256]{2,1,0:T(8,128)} %get-tuple-element.38), calls=%async_computation.5 | async-start | bytes 917504 | tf_op jit(solution)/shard_map/all_to_all | solution.py:253
  164.8 12.7 %shard_map.65.after.inverse = f32[256,256]{1,0:T(8,128)S(1)} custom-call(f32[256,256]{1,0:T(8,128)S(1)} %shard_map.63.after.half, f32[8,128]{1,0:T(8,128)S(1)} %get-tuple-element.39.after), custom_call_target="tpu_custom_call" | custom-call | flops 15000000512 | bytes 100000 | tf_op jit(solution)/shard_map/pallas_call | solution.py:304
  180.4 4.6 %all-to-all-start.6 = ((f32[8,56,256]{2,1,0:T(8,128)}), f32[8,56,256]{2,1,0:T(8,128)S(1)}, u32[]{:S(2)}, u32[]{:S(2)}) async-start(f32[8,56,256]{2,1,0:T(8,128)} %get-tuple-element.40.after), calls=%async_computation.6 | async-start | bytes 917504 | tf_op jit(solution)/shard_map/all_to_all | solution.py:253
  185.4 3.8 %collective-permute-start.11 = (f32[1,256]{1,0:T(1,128)S(1)}, f32[1,256]{1,0:T(1,128)S(1)}, u32[]{:S(2)}, u32[]{:S(2)}) collective-permute-start(f32[1,256]{1,0:T(1,128)S(1)} %get-tuple-element.42), channel_id=1, source_target_pairs={{0,8},{8,0},{1,9},{9,1},{2,10},{10,2},{3,11},{11,3},{4,12},{12,4},... | collective-permute-start | bytes 3080 | tf_op jit(solution)/shard_map/ppermute | solution.py:257
  190.0 4.1 %collective-permute-start.12 = (f32[1,256]{1,0:T(1,128)S(1)}, f32[1,256]{1,0:T(1,128)S(1)}, u32[]{:S(2)}, u32[]{:S(2)}) collective-permute-start(f32[1,256]{1,0:T(1,128)S(1)} %add.40), channel_id=1, source_target_pairs={{0,128},{128,0},{256,384},{384,256},{1,129},{129,1},{257,385},{385... | collective-permute-start | bytes 3080 | tf_op jit(solution)/shard_map/ppermute | solution.py:317
  195.4 4.0 %collective-permute-start.13 = (f32[1,256]{1,0:T(1,128)S(1)}, f32[1,256]{1,0:T(1,128)S(1)}, u32[]{:S(2)}, u32[]{:S(2)}) collective-permute-start(f32[1,256]{1,0:T(1,128)S(1)} %add.41), channel_id=1, source_target_pairs={{0,256},{128,384},{256,0},{384,128},{1,257},{129,385},{257,1},{385... | collective-permute-start | bytes 3080 | tf_op jit(solution)/shard_map/ppermute | solution.py:317
  201.5 5.5 %collective-permute-start.16 = (f32[8,56,256]{2,1,0:T(8,128)S(1)}, f32[8,56,256]{2,1,0:T(8,128)S(1)}, u32[]{:S(2)}, u32[]{:S(2)}) collective-permute-start(f32[8,56,256]{2,1,0:T(8,128)S(1)} %all-to-all-done.6.refs_0_), channel_id=1, source_target_pairs={{0,384},{128,0},{256,128},{384,256},{1,385},{129,1},{257,129},{385... | collective-permute-start | bytes 1376264 | tf_op jit(solution)/shard_map/ppermute | solution.py:261
  213.2 5.6 %all-to-all-start.7 = ((f32[64,1,256]{2,1,0:T(1,128)}), f32[64,1,256]{2,1,0:T(1,128)S(1)}, u32[]{:S(2)}, u32[]{:S(2)}) async-start(f32[64,1,256]{2,1,0:T(1,128)} %broadcast_in_dim.16), calls=%async_computation.7 | async-start | bytes 131072 | tf_op jit(solution)/shard_map/all_to_all | solution.py:253
  218.8 5.1 %collective-permute-start.17 = (f32[8,56,256]{2,1,0:T(8,128)S(1)}, f32[8,56,256]{2,1,0:T(8,128)S(1)}, u32[]{:S(2)}, u32[]{:S(2)}) collective-permute-start(f32[8,56,256]{2,1,0:T(8,128)S(1)} %all-to-all-done.6.refs_0_), channel_id=1, source_target_pairs={{0,8},{8,0},{1,9},{9,1},{2,10},{10,2},{3,11},{11,3},{4,12},{12,4},... | collective-permute-start | bytes 1376264 | tf_op jit(solution)/shard_map/ppermute | solution.py:257
  223.9 6.0 %all-to-all-done.7.pieces = f32[64,1,256]{2,1,0:T(1,128)S(1)} async-done(((f32[64,1,256]{2,1,0:T(1,128)}), f32[64,1,256]{2,1,0:T(1,128)S(1)}, u32[]{:S(2)}, u32[]{:S(2)}) %all-to-all-start.7) | async-done | bytes 65568 | tf_op jit(solution)/shard_map/all_to_all | solution.py:253
  241.9 5.8 %shard_map.69 = f32[128,3584]{1,0:T(8,128)} custom-call(s32[2]{0:T(128)S(1)} %pad_add_fusion.where, f32[8,56,256]{2,1,0:T(8,128)S(1)} %all-to-all-done.6.refs_0_, f32[8,56,256]{2,1,0:T(8,128)S(1)} %collective-permute-done.14.refs_1_, f32[8,56,256]{2,1,0:T(8,128)S(1)} %collective-permute-done.15.refs_2_, f32[8,56,256]{2,1,0:T(8,128)S(1)} %collective-permute-done.16.refs_3_, ...), custom_call_target="tpu_custom_call" | custom-call | flops 704643072 | bytes 9000000 | tf_op jit(solution)/shard_map/pallas_call | solution.py:327
  (51 shorter events, 59.4 us)
Async XLA Ops:
  26.7 14.6 %collective-permute-start.2 = (f32[8,56,256]{2,1,0:T(8,128)S(1)}, f32[8,56,256]{2,1,0:T(8,128)S(1)}, u32[]{:S(2)}, u32[]{:S(2)}) collective-permute-start(f32[8,56,256]{2,1,0:T(8,128)S(1)} %all_to_all.40.refs_0_), channel_id=1, source_target_pairs={{0,384},{128,0},{256,128},{384,256},{1,385},{129,1},{257,129},{385... | collective-permute-start | bytes 1376264 | tf_op jit(solution)/shard_map/ppermute | solution.py:261
  31.0 22.5 %collective-permute-start.1 = (f32[8,56,256]{2,1,0:T(8,128)S(1)}, f32[8,56,256]{2,1,0:T(8,128)S(1)}, u32[]{:S(2)}, u32[]{:S(2)}) collective-permute-start(f32[8,56,256]{2,1,0:T(8,128)S(1)} %all_to_all.40.refs_0_), channel_id=1, source_target_pairs={{0,256},{128,384},{256,0},{384,128},{1,257},{129,385},{257,1},{385... | collective-permute-start | bytes 1376264 | tf_op jit(solution)/shard_map/ppermute | solution.py:261
  33.5 23.2 %collective-permute-start = (f32[8,56,256]{2,1,0:T(8,128)S(1)}, f32[8,56,256]{2,1,0:T(8,128)S(1)}, u32[]{:S(2)}, u32[]{:S(2)}) collective-permute-start(f32[8,56,256]{2,1,0:T(8,128)S(1)} %all_to_all.40.refs_0_), channel_id=1, source_target_pairs={{0,128},{128,256},{256,384},{384,0},{1,129},{129,257},{257,385},{3... | collective-permute-start | bytes 1376264 | tf_op jit(solution)/shard_map/ppermute | solution.py:261
  36.0 23.2 %collective-permute-start.3 = (f32[8,56,256]{2,1,0:T(8,128)S(1)}, f32[8,56,256]{2,1,0:T(8,128)S(1)}, u32[]{:S(2)}, u32[]{:S(2)}) collective-permute-start(f32[8,56,256]{2,1,0:T(8,128)S(1)} %all_to_all.40.refs_0_), channel_id=1, source_target_pairs={{0,8},{8,0},{1,9},{9,1},{2,10},{10,2},{3,11},{11,3},{4,12},{12,4},... | collective-permute-start | bytes 1376264 | tf_op jit(solution)/shard_map/ppermute | solution.py:257
  41.3 17.9 %collective-permute-start.6 = (f32[8,56,256]{2,1,0:T(8,128)S(1)}, f32[8,56,256]{2,1,0:T(8,128)S(1)}, u32[]{:S(2)}, u32[]{:S(2)}) collective-permute-start(f32[8,56,256]{2,1,0:T(8,128)S(1)} %collective-permute-done.2.refs_3_), channel_id=1, source_target_pairs={{0,8},{8,0},{1,9},{9,1},{2,10},{10,2},{3,11},{11,3},{4,12},{12,4},... | collective-permute-start | bytes 1376264 | tf_op jit(solution)/shard_map/ppermute | solution.py:257
  53.5 5.7 %collective-permute-start.5 = (f32[8,56,256]{2,1,0:T(8,128)S(1)}, f32[8,56,256]{2,1,0:T(8,128)S(1)}, u32[]{:S(2)}, u32[]{:S(2)}) collective-permute-start(f32[8,56,256]{2,1,0:T(8,128)S(1)} %collective-permute-done.1.refs_2_), channel_id=1, source_target_pairs={{0,8},{8,0},{1,9},{9,1},{2,10},{10,2},{3,11},{11,3},{4,12},{12,4},... | collective-permute-start | bytes 1376264 | tf_op jit(solution)/shard_map/ppermute | solution.py:257
  92.6 20.8 %all-to-all-start.3 = ((f32[64,8,128]{2,1,0:T(8,128)}), f32[64,8,128]{2,1,0:T(8,128)S(1)}, u32[]{:S(2)}, u32[]{:S(2)}) async-start(f32[64,8,128]{2,1,0:T(8,128)} %get-tuple-element.31), calls=%async_computation.3 | async-start | bytes 524288 | tf_op jit(solution)/shard_map/all_to_all | solution.py:253
  114.2 6.0 %collective-permute-start.7 = (f32[4,8,56,256]{3,2,1,0:T(8,128)}, f32[4,8,56,256]{3,2,1,0:T(8,128)S(1)}, u32[]{:S(2)}, u32[]{:S(2)}) collective-permute-start(f32[4,8,56,256]{3,2,1,0:T(8,128)} %get-tuple-element.32), channel_id=1, source_target_pairs={{0,8},{8,0},{1,9},{9,1},{2,10},{10,2},{3,11},{11,3},{4,12},{12,4},... | collective-permute-start | bytes 5505032 | tf_op jit(solution)/shard_map/ppermute | solution.py:257
  122.7 19.4 %all-to-all-start.4 = ((f32[64,8,128]{2,1,0:T(8,128)}), f32[64,8,128]{2,1,0:T(8,128)S(1)}, u32[]{:S(2)}, u32[]{:S(2)}) async-start(f32[64,8,128]{2,1,0:T(8,128)} %shard_map.62), calls=%async_computation.4 | async-start | bytes 524288 | tf_op jit(solution)/shard_map/all_to_all | solution.py:253
  130.1 25.3 %collective-permute-start.8 = (f32[8,56,256]{2,1,0:T(8,128)}, f32[8,56,256]{2,1,0:T(8,128)S(1)}, u32[]{:S(2)}, u32[]{:S(2)}) collective-permute-start(f32[8,56,256]{2,1,0:T(8,128)} %get-tuple-element.34), channel_id=1, source_target_pairs={{0,128},{128,256},{256,384},{384,0},{1,129},{129,257},{257,385},{3... | collective-permute-start | bytes 1376264 | tf_op jit(solution)/shard_map/ppermute | solution.py:261
  133.4 25.1 %collective-permute-start.9 = (f32[8,56,256]{2,1,0:T(8,128)S(1)}, f32[8,56,256]{2,1,0:T(8,128)S(1)}, u32[]{:S(2)}, u32[]{:S(2)}) collective-permute-start(f32[8,56,256]{2,1,0:T(8,128)S(1)} %get-tuple-element.35), channel_id=1, source_target_pairs={{0,256},{128,384},{256,0},{384,128},{1,257},{129,385},{257,1},{385... | collective-permute-start | bytes 1376264 | tf_op jit(solution)/shard_map/ppermute | solution.py:261
  137.9 20.6 %collective-permute-start.10 = (f32[8,56,256]{2,1,0:T(8,128)S(1)}, f32[8,56,256]{2,1,0:T(8,128)S(1)}, u32[]{:S(2)}, u32[]{:S(2)}) collective-permute-start(f32[8,56,256]{2,1,0:T(8,128)S(1)} %get-tuple-element.36), channel_id=1, source_target_pairs={{0,384},{128,0},{256,128},{384,256},{1,385},{129,1},{257,129},{385... | collective-permute-start | bytes 1376264 | tf_op jit(solution)/shard_map/ppermute | solution.py:261
  159.4 20.2 %all-to-all-start.5 = ((f32[8,56,256]{2,1,0:T(8,128)}), f32[8,56,256]{2,1,0:T(8,128)S(1)}, u32[]{:S(2)}, u32[]{:S(2)}) async-start(f32[8,56,256]{2,1,0:T(8,128)} %get-tuple-element.38), calls=%async_computation.5 | async-start | bytes 917504 | tf_op jit(solution)/shard_map/all_to_all | solution.py:253
  180.4 21.1 %all-to-all-start.6 = ((f32[8,56,256]{2,1,0:T(8,128)}), f32[8,56,256]{2,1,0:T(8,128)S(1)}, u32[]{:S(2)}, u32[]{:S(2)}) async-start(f32[8,56,256]{2,1,0:T(8,128)} %get-tuple-element.40.after), calls=%async_computation.6 | async-start | bytes 917504 | tf_op jit(solution)/shard_map/all_to_all | solution.py:253
  185.4 4.6 %collective-permute-start.11 = (f32[1,256]{1,0:T(1,128)S(1)}, f32[1,256]{1,0:T(1,128)S(1)}, u32[]{:S(2)}, u32[]{:S(2)}) collective-permute-start(f32[1,256]{1,0:T(1,128)S(1)} %get-tuple-element.42), channel_id=1, source_target_pairs={{0,8},{8,0},{1,9},{9,1},{2,10},{10,2},{3,11},{11,3},{4,12},{12,4},... | collective-permute-start | bytes 3080 | tf_op jit(solution)/shard_map/ppermute | solution.py:257
  190.0 5.4 %collective-permute-start.12 = (f32[1,256]{1,0:T(1,128)S(1)}, f32[1,256]{1,0:T(1,128)S(1)}, u32[]{:S(2)}, u32[]{:S(2)}) collective-permute-start(f32[1,256]{1,0:T(1,128)S(1)} %add.40), channel_id=1, source_target_pairs={{0,128},{128,0},{256,384},{384,256},{1,129},{129,1},{257,385},{385... | collective-permute-start | bytes 3080 | tf_op jit(solution)/shard_map/ppermute | solution.py:317
  195.4 6.1 %collective-permute-start.13 = (f32[1,256]{1,0:T(1,128)S(1)}, f32[1,256]{1,0:T(1,128)S(1)}, u32[]{:S(2)}, u32[]{:S(2)}) collective-permute-start(f32[1,256]{1,0:T(1,128)S(1)} %add.41), channel_id=1, source_target_pairs={{0,256},{128,384},{256,0},{384,128},{1,257},{129,385},{257,1},{385... | collective-permute-start | bytes 3080 | tf_op jit(solution)/shard_map/ppermute | solution.py:317
  201.5 28.4 %collective-permute-start.16 = (f32[8,56,256]{2,1,0:T(8,128)S(1)}, f32[8,56,256]{2,1,0:T(8,128)S(1)}, u32[]{:S(2)}, u32[]{:S(2)}) collective-permute-start(f32[8,56,256]{2,1,0:T(8,128)S(1)} %all-to-all-done.6.refs_0_), channel_id=1, source_target_pairs={{0,384},{128,0},{256,128},{384,256},{1,385},{129,1},{257,129},{385... | collective-permute-start | bytes 1376264 | tf_op jit(solution)/shard_map/ppermute | solution.py:261
  207.1 22.8 %collective-permute-start.15 = (f32[8,56,256]{2,1,0:T(8,128)S(1)}, f32[8,56,256]{2,1,0:T(8,128)S(1)}, u32[]{:S(2)}, u32[]{:S(2)}) collective-permute-start(f32[8,56,256]{2,1,0:T(8,128)S(1)} %all-to-all-done.6.refs_0_), channel_id=1, source_target_pairs={{0,256},{128,384},{256,0},{384,128},{1,257},{129,385},{257,1},{385... | collective-permute-start | bytes 1376264 | tf_op jit(solution)/shard_map/ppermute | solution.py:261
  210.6 22.2 %collective-permute-start.14 = (f32[8,56,256]{2,1,0:T(8,128)S(1)}, f32[8,56,256]{2,1,0:T(8,128)S(1)}, u32[]{:S(2)}, u32[]{:S(2)}) collective-permute-start(f32[8,56,256]{2,1,0:T(8,128)S(1)} %all-to-all-done.6.refs_0_), channel_id=1, source_target_pairs={{0,128},{128,256},{256,384},{384,0},{1,129},{129,257},{257,385},{3... | collective-permute-start | bytes 1376264 | tf_op jit(solution)/shard_map/ppermute | solution.py:261
  213.2 16.7 %all-to-all-start.7 = ((f32[64,1,256]{2,1,0:T(1,128)}), f32[64,1,256]{2,1,0:T(1,128)S(1)}, u32[]{:S(2)}, u32[]{:S(2)}) async-start(f32[64,1,256]{2,1,0:T(1,128)} %broadcast_in_dim.16), calls=%async_computation.7 | async-start | bytes 131072 | tf_op jit(solution)/shard_map/all_to_all | solution.py:253
  218.8 22.4 %collective-permute-start.17 = (f32[8,56,256]{2,1,0:T(8,128)S(1)}, f32[8,56,256]{2,1,0:T(8,128)S(1)}, u32[]{:S(2)}, u32[]{:S(2)}) collective-permute-start(f32[8,56,256]{2,1,0:T(8,128)S(1)} %all-to-all-done.6.refs_0_), channel_id=1, source_target_pairs={{0,8},{8,0},{1,9},{9,1},{2,10},{10,2},{3,11},{11,3},{4,12},{12,4},... | collective-permute-start | bytes 1376264 | tf_op jit(solution)/shard_map/ppermute | solution.py:257
  232.7 8.5 %collective-permute-start.18 = (f32[8,56,256]{2,1,0:T(8,128)S(1)}, f32[8,56,256]{2,1,0:T(8,128)S(1)}, u32[]{:S(2)}, u32[]{:S(2)}) collective-permute-start(f32[8,56,256]{2,1,0:T(8,128)S(1)} %collective-permute-done.14.refs_1_), channel_id=1, source_target_pairs={{0,8},{8,0},{1,9},{9,1},{2,10},{10,2},{3,11},{11,3},{4,12},{12,4},... | collective-permute-start | bytes 1376264 | tf_op jit(solution)/shard_map/ppermute | solution.py:257
  236.1 5.1 %collective-permute-start.19 = (f32[8,56,256]{2,1,0:T(8,128)S(1)}, f32[8,56,256]{2,1,0:T(8,128)S(1)}, u32[]{:S(2)}, u32[]{:S(2)}) collective-permute-start(f32[8,56,256]{2,1,0:T(8,128)S(1)} %collective-permute-done.15.refs_2_), channel_id=1, source_target_pairs={{0,8},{8,0},{1,9},{9,1},{2,10},{10,2},{3,11},{11,3},{4,12},{12,4},... | collective-permute-start | bytes 1376264 | tf_op jit(solution)/shard_map/ppermute | solution.py:257
  (2 other events, 7.8 us)

commit v3 on v2

v3 whole, which is shorter than its diff:
```python
import math

import jax
import jax.numpy as jnp
import numpy as np
from jax import lax
from jax.experimental import pallas as pl
from jax.experimental.pallas import tpu as pltpu
from jax.sharding import Mesh, PartitionSpec as P

ROWS = 8192
COLS = 28672
RANK = 256
NX, NZ, NC, NY = 4, 8, 2, 8
MY_ROWS = 128
MY_COLS = 3584
SHARD = 56
CHUNK = NZ * NC * SHARD
HALF = 128
GROUP = 8
PER_SHARD = SHARD // GROUP
PER_X = NZ * PER_SHARD
MACS = MY_ROWS * MY_COLS * RANK

highest = lax.Precision.HIGHEST
f32 = jnp.float32
bf16 = jnp.bfloat16
VMEM = pl.BlockSpec(memory_space=pltpu.VMEM)
SMEM = pl.BlockSpec(memory_space=pltpu.SMEM)
ANY = pl.BlockSpec(memory_space=pl.ANY)
HBM = pl.BlockSpec(memory_space=pltpu.HBM)


def dot(a, b, ca, cb, precision=highest):
    return lax.dot_general(
        a, b, (((ca,), (cb,)), ((), ())), precision=precision, preferred_element_type=f32
    )


def shape(*dims):
    return jax.ShapeDtypeStruct(dims, f32)


def in_hbm(*dims):
    return pltpu.HBM(dims, f32)


TOKEN = shape(8, 128)


def call(kernel, out_shape, in_specs, scratch=(), out_specs=None, flops=1_000_000, nbytes=100_000, limit=12):
    return pl.pallas_call(
        kernel,
        out_shape=out_shape,
        in_specs=in_specs,
        out_specs=out_specs or jax.tree.map(lambda _: VMEM, out_shape),
        scratch_shapes=scratch,
        compiler_params=pltpu.CompilerParams(vmem_limit_bytes=limit * 2**20),
        cost_estimate=pl.CostEstimate(
            flops=flops, bytes_accessed=nbytes, transcendentals=0
        ),
    )


def columns(j):
    return pl.ds(j * CHUNK, CHUNK)


def buffer_copies(mom, grad, mom_here, grad_here, sems, j):
    cols = columns(j)
    return [
        pltpu.make_async_copy(mom.at[:, cols], mom_here.at[:, cols], sems.at[j, 0]),
        pltpu.make_async_copy(grad.at[:, cols], grad_here.at[:, cols], sems.at[j, 1]),
    ]


def gathered_copies(where, own, other, mom, grad, mom_here, grad_here, full, sems):
    core = where[1]
    copies = []
    for j in range(NX):
        copies.append(
            [
                pltpu.make_async_copy(own.at[j], full.at[j, :, core], sems.at[j, 2]),
                pltpu.make_async_copy(other.at[j], full.at[j, :, 1 - core], sems.at[j, 3]),
            ]
            + buffer_copies(mom, grad, mom_here, grad_here, sems, j)
        )
        for copy in copies[j]:
            copy.start()
    return copies


def buffer_chunk(mom, grad, j):
    return mom[:, columns(j)] + grad[:, columns(j)].astype(f32)


BUFFER_SCRATCH = [pltpu.VMEM((MY_ROWS, MY_COLS), f32), pltpu.VMEM((MY_ROWS, MY_COLS), bf16)]
SEMS = [pltpu.SemaphoreType.DMA((NX, 4))]
FULL = [pltpu.VMEM((NX, NZ, NC, SHARD, RANK), f32)]


def power_kernel(where, own, other, mom, grad, out, mom_here, grad_here, full, sems):
    copies = gathered_copies(where, own, other, mom, grad, mom_here, grad_here, full, sems)
    total = None
    for j in range(NX):
        for copy in copies[j]:
            copy.wait()
        part = dot(buffer_chunk(mom_here, grad_here, j), full[j].reshape(CHUNK, RANK), 1, 0)
        total = part if total is None else total + part
    out[...] = total


def sum_spread_kernel(pieces, out):
    total = jnp.sum(pieces[...], axis=0)
    for i in range(out.shape[0]):
        out[i] = total


def column_kernel(where, power, mom, grad, keep, send, mom_here, grad_here, full, gram, sems, outs):
    copies = []
    for j in range(NX):
        copies.append(buffer_copies(mom, grad, mom_here, grad_here, sems, j))
        for copy in copies[j]:
            copy.start()
    gram[...] = dot(power[...], power[...], 0, 0).reshape(RANK // GROUP, GROUP, RANK)
    core = where[1]
    waits = []
    for j in range(NX):
        for copy in copies[j]:
            copy.wait()
        for q in range(CHUNK // HALF):
            cols = pl.ds(j * CHUNK + q * HALF, HALF)
            part = mom_here[:, cols] + grad_here[:, cols].astype(f32)
            part = dot(part, power[...], 0, 0)
            full[pl.ds((j * CHUNK + q * HALF) // GROUP, HALF // GROUP)] = part.reshape(
                HALF // GROUP, GROUP, RANK
            )
        for side, (out, c) in enumerate(((send, 1 - core), (keep, core))):
            for z in range(NZ):
                start = ((j * NZ + z) * NC + c) * PER_SHARD
                waits.append(
                    pltpu.make_async_copy(
                        full.at[pl.ds(start, PER_SHARD)],
                        out.at[j, pl.ds(z * PER_SHARD, PER_SHARD)],
                        outs.at[j, z, side],
                    )
                )
            waits.append(
                pltpu.make_async_copy(
                    gram.at[pl.ds(where[2] * NX + j, 1)],
                    out.at[j, pl.ds(PER_X, 1)],
                    outs.at[j, NZ, side],
                )
            )
        for copy in waits[-2 * (NZ + 1) :]:
            copy.start()
    for copy in waits:
        copy.wait()


def sum_x_kernel(pieces, out):
    total = (pieces[0] + pieces[1]) + (pieces[2] + pieces[3])
    for z in range(NZ):
        out[z, 0:PER_SHARD] = total[z * PER_SHARD : (z + 1) * PER_SHARD]
        out[z, PER_SHARD] = total[PER_X]


def sum_z_kernel(pieces, mine, copies, gram):
    total = jnp.sum(pieces[...], axis=0)
    column = total[0:PER_SHARD].reshape(SHARD, RANK)
    mine[...] = column
    for i in range(NZ):
        copies[i] = column
    for i in range(NX * NY):
        gram[i] = total[PER_SHARD]


def copies_kernel(value, after, out):
    for i in range(out.shape[0]):
        out[i] = value[...]


def inverse_factor(d):
    row = lax.broadcasted_iota(jnp.int32, (GROUP, HALF), 0)
    col = lax.broadcasted_iota(jnp.int32, (GROUP, HALF), 1)
    groups = [d[g * GROUP : (g + 1) * GROUP] for g in range(HALF // GROUP)]
    for j in range(0, HALF - 2, 2):
        g0, i = divmod(j, GROUP)
        column0 = [None] * len(groups)
        column1 = [None] * len(groups)
        for g in range(g0, len(groups)):
            column0[g] = jnp.broadcast_to(groups[g][:, j : j + 1], (GROUP, HALF))
            column1[g] = jnp.broadcast_to(groups[g][:, j + 1 : j + 2], (GROUP, HALF))
        p = column0[g0][i : i + 1]
        b = column0[g0][i + 1 : i + 2]
        q = column1[g0][i + 1 : i + 2]
        over_p = 1.0 / p
        ratio = b * over_p
        over_q = 1.0 / (q - ratio * b)
        first, second = col[0:1] == j, col[0:1] == j + 1
        line0 = jnp.where(first, 1.0, jnp.where(second, 0.0, groups[g0][i : i + 1]))
        line1 = jnp.where(first, 0.0, jnp.where(second, 1.0, groups[g0][i + 1 : i + 2]))
        line1 = over_q * (line1 - ratio * line0)
        line0 = over_p * line0 - ratio * line1
        line0 = jnp.broadcast_to(line0, (GROUP, HALF))
        line1 = jnp.broadcast_to(line1, (GROUP, HALF))
        pivots = (col == j) | (col == j + 1)
        for g in range(g0, len(groups)):
            rest = jnp.where(pivots, 0.0, groups[g])
            rest = rest - column0[g] * line0 - column1[g] * line1
            groups[g] = jnp.where(row > i + 1, rest, groups[g]) if g == g0 else rest
    odd = row % 2 == 1
    for g in range(len(groups)):
        at = row + g * GROUP
        d = groups[g]
        diagonal = jnp.sum(jnp.where(col == at, d, 0.0), axis=1, keepdims=True)
        diagonal = jnp.broadcast_to(diagonal, (GROUP, HALF))
        below = jnp.sum(jnp.where(col == at - 1, d, 0.0), axis=1, keepdims=True)
        below = jnp.broadcast_to(below, (GROUP, HALF))
        ratio = jnp.where(odd, below / pltpu.roll(diagonal, 1, 0), 0.0)
        scale = lax.rsqrt(diagonal - ratio * below)
        unit = jnp.where(col == at, 1.0, jnp.where(col < at - at % 2, d, 0.0))
        groups[g] = scale * (unit - ratio * pltpu.roll(unit, 1, 0))
    return jnp.concatenate(groups, axis=0)


def first_half_kernel(gram, out):
    inner = inverse_factor(gram[0:HALF, 0:HALF])
    upper = dot(inner, gram[0:HALF, HALF:], 1, 0)
    out[0] = inner
    out[1] = gram[HALF:, HALF:] - dot(upper, upper, 0, 0)
    out[2] = -dot(upper, inner, 0, 0)


def second_half_kernel(half, out):
    inner = inverse_factor(half[1])
    out[0:HALF, 0:HALF] = half[0]
    out[0:HALF, HALF:] = jnp.zeros((HALF, HALF), f32)
    out[HALF:, 0:HALF] = dot(inner, half[2], 1, 0)
    out[HALF:, HALF:] = inner


def squares_kernel(own, column_mine, inverse, factor_mine, squares):
    factor_mine[...] = dot(column_mine[...], inverse[...], 1, 1)
    total = jnp.zeros((1, RANK), f32)
    for x in range(NX):
        c = dot(own[x].reshape(NZ * SHARD, RANK), inverse[...], 1, 1)
        total = total + jnp.sum(c * c, axis=0, keepdims=True)
    for i in range(NY * NC):
        squares[i] = total


def ortho_kernel(power, inverse, row_factor, weights):
    o = dot(power[...], inverse[...], 1, 1)
    row_factor[...] = o * math.sqrt(ROWS)
    weights[...] = 0.05 * dot(o, inverse[...], 1, 0)


def new_right_kernel(pieces, factor_mine, after, out):
    squares = jnp.sum(pieces[...], axis=0)
    out[...] = factor_mine[...] / jnp.sqrt(squares / COLS + 1e-06)


def split(value):
    high = value.astype(bf16)
    return high, (value - high.astype(f32)).astype(bf16)


def momentum_kernel(
    where, own, other, weights, mom, grad, out, token, mom_here, grad_here, full, sems, done
):
    copies = gathered_copies(where, own, other, mom, grad, mom_here, grad_here, full, sems)
    high, low = split(weights[...])
    token[...] = jnp.zeros_like(token)
    for j in range(NX):
        for copy in copies[j]:
            copy.wait()
        fh, fl = split(full[j].reshape(CHUNK, RANK))
        change = dot(high, fh, 1, 1, None) + (dot(high, fl, 1, 1, None) + dot(low, fh, 1, 1, None))
        mom_here[:, columns(j)] = buffer_chunk(mom_here, grad_here, j) - change
        copies[j] = pltpu.make_async_copy(
            mom_here.at[:, columns(j)], out.at[:, columns(j)], done.at[j]
        )
        copies[j].start()
    for j in range(NX):
        copies[j].wait()


def spread(value, axis, size):
    copies = jnp.broadcast_to(value[None], (size,) + value.shape)
    return swap(copies, axis)


def swap(pieces, axis):
    return lax.all_to_all(pieces, axis, 0, 0)


def other_core(value):
    return lax.ppermute(value, "c", [(0, 1), (1, 0)])


def shards(momentum, gradient, right_factor):
    where = jnp.stack([lax.axis_index(a) for a in ("x", "c", "y")]).astype(jnp.int32)
    momentum = pltpu.with_memory_space_constraint(momentum, pltpu.HBM)
    gradient = pltpu.with_memory_space_constraint(gradient, pltpu.HBM)

    own = spread(spread(right_factor, "z", NZ), "x", NX)
    partial_power = call(
        power_kernel, shape(MY_ROWS, RANK), [SMEM] + [HBM] * 4,
        BUFFER_SCRATCH + FULL + SEMS, None, 12 * MACS, 7_000_000,
    )(where, own, other_core(own), momentum, gradient)

    pieces = swap(partial_power.reshape(NY, MY_ROWS // NY, RANK), "y")
    copies = call(sum_spread_kernel, shape(NY, MY_ROWS // NY, RANK), [VMEM])(pieces)
    power = swap(copies, "y").reshape(MY_ROWS, RANK)

    keep, send = call(
        column_kernel, [in_hbm(NX, PER_X + 1, GROUP, RANK)] * 2, [SMEM, VMEM, HBM, HBM],
        BUFFER_SCRATCH
        + [pltpu.VMEM((MY_COLS // GROUP, GROUP, RANK), f32)]
        + [pltpu.VMEM((RANK // GROUP, GROUP, RANK), f32)]
        + [pltpu.SemaphoreType.DMA((NX, 2)), pltpu.SemaphoreType.DMA((NX, NZ + 1, 2))],
        [HBM, HBM], 12 * MACS, 7_000_000,
    )(where, power, momentum, gradient)
    by_x = swap(keep + other_core(send), "x")
    by_z = call(
        sum_x_kernel, shape(NZ, PER_SHARD + 1, GROUP, RANK), [VMEM], nbytes=3_000_000
    )(by_x)
    column_mine, copies, gram = call(
        sum_z_kernel,
        [shape(SHARD, RANK), shape(NZ, SHARD, RANK), shape(NX * NY, GROUP, RANK)],
        [VMEM],
    )(swap(by_z, "z"))

    gram = swap(gram, ("y", "x")).reshape(RANK, RANK)
    gram, copies = lax.optimization_barrier((gram, copies))
    half = call(first_half_kernel, shape(3, HALF, HALF), [VMEM], flops=10_000_000_000)(gram)
    copies = call(
        copies_kernel, shape(NX, NZ, SHARD, RANK), [VMEM, ANY], nbytes=3_000_000
    )(swap(copies, "z"), half)
    half, copies = lax.optimization_barrier((half, copies))
    inverse = call(second_half_kernel, shape(RANK, RANK), [VMEM], flops=10_000_000_000)(half)
    own = swap(copies, "x")
    own, inverse = lax.optimization_barrier((own, inverse))
    factor_mine, squares = call(
        squares_kernel, [shape(SHARD, RANK), shape(NY * NC, 1, RANK)], [VMEM] * 3, (), None,
        6 * MACS, 2_000_000,
    )(own, column_mine, inverse)
    squares = swap(squares, ("y", "c"))
    row_factor, weights = call(
        ortho_kernel, [shape(MY_ROWS, RANK)] * 2, [VMEM, VMEM]
    )(power, inverse)
    new_momentum, token = call(
        momentum_kernel, [in_hbm(MY_ROWS, MY_COLS), TOKEN], [SMEM, HBM, HBM, VMEM, HBM, HBM],
        BUFFER_SCRATCH + FULL + SEMS + [pltpu.SemaphoreType.DMA((NX,))],
        [HBM, VMEM], 6 * MACS, 9_000_000,
    )(where, own, other_core(own), weights, momentum, gradient)
    new_right = call(new_right_kernel, shape(SHARD, RANK), [VMEM, VMEM, ANY])(
        squares, factor_mine, token
    )
    return (new_momentum, new_right, row_factor)


def solution(mesh):
    devices = np.asarray(mesh.devices).reshape(NX, NZ, NC, NY)
    grid = Mesh(devices, ("x", "z", "c", "y"))
    fsdp = ("x", "z", "c")
    return jax.shard_map(
        shards,
        mesh=grid,
        in_specs=(P(fsdp, "y"), P(fsdp, "y"), P(("y",) + fsdp, None)),
        out_specs=(P(fsdp, "y"), P(("y",) + fsdp, None), P(fsdp, None)),
        check_vma=False,
    )
```

time: 249 us -> 230 us (0.924)
  blocking collectives: 50.1 us -> 132 us
  starting transfers between devices: 112 us -> 33.1 us
  Pallas kernels: 52.8 us -> 40.5 us
  waiting for transfers between devices: 28 us -> 20.3 us
    all_to_all x3 -> x7, blocking collectives: 50.1 us -> 132 us  [swap(): return lax.all_to_all(pieces, axis, 0, 0)]
    ppermute x11 -> x0, starting transfers between devices: 39.2 us -> none  [the longest x9 31.1 us: shift(): return lax.ppermute(value, 'x', [(i, (i + by) % NX) for i in range(NX)])]
    ppermute x10 -> x3, starting transfers between devices: 40.8 us -> 20.4 us  [other_core(): return lax.ppermute(value, 'c', [(0, 1), (1, 0)])]
    all_to_all x5 -> x3, starting transfers between devices: 31.9 us -> 12.7 us  [swap(): return lax.all_to_all(pieces, axis, 0, 0)]
    pallas_call x11 -> x10, Pallas kernels: 51.6 us -> 39.3 us  [the longest x1 7.46 us: shards(): call(first_half_kernel, shape(3, HALF, HALF), [VMEM], flops=10000000000)]
    ppermute x11 -> x0, waiting for transfers between devices: 9.39 us -> none  [the longest x9 7.23 us: shift(): return lax.ppermute(value, 'x', [(i, (i + by) % NX) for i in range(NX)])]
    all_to_all x5 -> x3, waiting for transfers between devices: 12.1 us -> 13.2 us  [swap(): return lax.all_to_all(pieces, axis, 0, 0)]
    ppermute x10 -> x3, waiting for transfers between devices: 6.55 us -> 7.09 us  [other_core(): return lax.ppermute(value, 'c', [(0, 1), (1, 0)])]
  transfers between devices with their start and end apart: 26 -> 6, of which waited for: 13 -> 5; matrix products, arithmetic and copies ran while one was open for 0% -> 0% of each run, Pallas kernels for 15% -> 11%
where the time goes in v3:
time: 230 us; the launch traced here: 229 us
  blocking collectives  132 us (57%)
  Pallas kernels  40.5 us (18%)
  starting transfers between devices  33.1 us (14%)
  waiting for transfers between devices  20.3 us (9%)
    all_to_all x7, blocking collectives, swap(): return lax.all_to_all(pieces, axis, 0, 0)  132 us
    ppermute x3, starting transfers between devices, other_core(): return lax.ppermute(value, 'c', [(0, 1), (1, 0)])  20.4 us
    all_to_all x3, waiting for transfers between devices, swap(): return lax.all_to_all(pieces, axis, 0, 0)  13.2 us
    all_to_all x3, starting transfers between devices, swap(): return lax.all_to_all(pieces, axis, 0, 0)  12.7 us
    pallas_call x1, Pallas kernels, shards(): call(first_half_kernel, shape(3, HALF, HALF), [VMEM], flops=10000000000)  7.46 us
    pallas_call x1, Pallas kernels, shards(): call(column_kernel, [in_hbm(NX, PER_X + 1, GROUP, RANK)] * 2, [SMEM, VMEM...  7.41 us
    pallas_call x1, Pallas kernels, shards(): call(second_half_kernel, shape(RANK, RANK), [VMEM], flops=10000000000)(half)  7.16 us
    ppermute x3, waiting for transfers between devices, other_core(): return lax.ppermute(value, 'c', [(0, 1), (1, 0)])  7.09 us
  transfers between devices with their start and end apart: 6, of which 5 were waited for; matrix products, arithmetic and copies ran while one was open for 0% of the time, Pallas kernels for 11%

profile of v3, /device:TPU:1, one launch (start us, length us, event | category | flops | bytes accessed | tf_op | source)
XLA Modules:
  0.0 229.1 jit_solution(16992773559261486334)
XLA Ops:
  1.5 25.2 %all_to_all.50 = f32[8,56,256]{2,1,0:T(8,128)S(1)} all-to-all(f32[8,56,256]{2,1,0:T(8,128)S(1)} %broadcast_in_dim.4), channel_id=1, replica_groups=mesh['x'=4,'z'=8,'c'=2,'y'=8] {'z'}, dimensions={0} | all-to-all | bytes 917504 | tf_op jit(solution)/shard_map/all_to_all | solution.py:295
  26.8 24.3 %all_to_all.51.own = f32[4,8,56,256]{3,2,1,0:T(8,128)S(1)} all-to-all(f32[4,8,56,256]{3,2,1,0:T(8,128)S(1)} %broadcast_in_dim.5), channel_id=1, replica_groups=mesh['x'=4,'z'=8,'c'=2,'y'=8] {'x'}, dimensions={0} | all-to-all | bytes 3670016 | tf_op jit(solution)/shard_map/all_to_all | solution.py:295
  51.1 5.9 %collective-permute-start = (f32[4,8,56,256]{3,2,1,0:T(8,128)S(1)}, f32[4,8,56,256]{3,2,1,0:T(8,128)}, u32[]{:S(2)}, u32[]{:S(2)}) collective-permute-start(f32[4,8,56,256]{3,2,1,0:T(8,128)S(1)} %all_to_all.51.own), channel_id=1, source_target_pairs={{0,8},{8,0},{1,9},{9,1},{2,10},{10,2},{3,11},{11,3},{4,12},{12,4},... | collective-permute-start | bytes 5505032 | tf_op jit(solution)/shard_map/ppermute | solution.py:299
  57.1 3.4 %collective-permute-done.other = f32[4,8,56,256]{3,2,1,0:T(8,128)} collective-permute-done((f32[4,8,56,256]{3,2,1,0:T(8,128)S(1)}, f32[4,8,56,256]{3,2,1,0:T(8,128)}, u32[]{:S(2)}, u32[]{:S(2)}) %collective-permute-start) | collective-permute-done | bytes 1835040 | tf_op jit(solution)/shard_map/ppermute | solution.py:299
  60.5 5.9 %shard_map.58 = f32[128,256]{1,0:T(8,128)S(1)} custom-call(s32[3]{0:T(128)S(1)} %pad_add_fusion.where, f32[4,8,56,256]{3,2,1,0:T(8,128)S(1)} %all_to_all.51.own, f32[4,8,56,256]{3,2,1,0:T(8,128)} %collective-permute-done.other, f32[128,3584]{1,0:T(8,128)} %mom.5, bf16[128,3584]{1,0:T(8,128)(2,1)} %grad.5), custom_call_target="tpu_custom_call" | custom-call | flops 1409286144 | bytes 7000000 | tf_op jit(solution)/shard_map/pallas_call | solution.py:308
  66.5 14.5 %all_to_all.52.pieces = f32[8,16,256]{2,1,0:T(8,128)S(1)} all-to-all(f32[8,16,256]{2,1,0:T(8,128)S(1)} %bitcast.8), channel_id=1, replica_groups=mesh['x'=4,'z'=8,'c'=2,'y'=8] {'y'}, dimensions={0} | all-to-all | bytes 262144 | tf_op jit(solution)/shard_map/all_to_all | solution.py:295
  81.0 10.4 %all_to_all.53 = f32[8,16,256]{2,1,0:T(8,128)S(1)} all-to-all(f32[8,16,256]{2,1,0:T(8,128)S(1)} %shard_map.59), channel_id=1, replica_groups=mesh['x'=4,'z'=8,'c'=2,'y'=8] {'y'}, dimensions={0} | all-to-all | bytes 262144 | tf_op jit(solution)/shard_map/all_to_all | solution.py:295
  91.4 7.4 %shard_map.60 = (f32[4,57,8,256]{3,2,1,0:T(8,128)}, f32[4,57,8,256]{3,2,1,0:T(8,128)}) custom-call(s32[3]{0:T(128)S(1)} %pad_add_fusion.where, f32[128,256]{1,0:T(8,128)S(1)} %bitcast.6, f32[128,3584]{1,0:T(8,128)} %mom.5, bf16[128,3584]{1,0:T(8,128)(2,1)} %grad.5), custom_call_target="tpu_custom_call" | custom-call | flops 1409286144 | bytes 7000000 | tf_op jit(solution)/shard_map/pallas_call | solution.py:317
  98.8 5.1 %collective-permute-start.1 = (f32[4,57,8,256]{3,2,1,0:T(8,128)}, f32[4,57,8,256]{3,2,1,0:T(8,128)S(1)}, u32[]{:S(2)}, u32[]{:S(2)}) collective-permute-start(f32[4,57,8,256]{3,2,1,0:T(8,128)} %get-tuple-element.21), channel_id=1, source_target_pairs={{0,8},{8,0},{1,9},{9,1},{2,10},{10,2},{3,11},{11,3},{4,12},{12,4},... | collective-permute-start | bytes 5603336 | tf_op jit(solution)/shard_map/ppermute | solution.py:299
  103.9 3.6 %collective-permute-done.1 = f32[4,57,8,256]{3,2,1,0:T(8,128)S(1)} collective-permute-done((f32[4,57,8,256]{3,2,1,0:T(8,128)}, f32[4,57,8,256]{3,2,1,0:T(8,128)S(1)}, u32[]{:S(2)}, u32[]{:S(2)}) %collective-permute-start.1) | collective-permute-done | bytes 1867808 | tf_op jit(solution)/shard_map/ppermute | solution.py:299
  107.6 1.7 add.3
  109.3 25.9 %all_to_all.54.pieces = f32[4,57,8,256]{3,2,1,0:T(8,128)S(1)} all-to-all(f32[4,57,8,256]{3,2,1,0:T(8,128)S(1)} %add.3), channel_id=1, replica_groups=mesh['x'=4,'z'=8,'c'=2,'y'=8] {'x'}, dimensions={0} | all-to-all | bytes 3735552 | tf_op jit(solution)/shard_map/all_to_all | solution.py:295
  135.3 17.8 %all_to_all.55.pieces = f32[8,8,8,256]{3,2,1,0:T(8,128)S(1)} all-to-all(f32[8,8,8,256]{3,2,1,0:T(8,128)S(1)} %shard_map.61), channel_id=1, replica_groups=mesh['x'=4,'z'=8,'c'=2,'y'=8] {'z'}, dimensions={0} | all-to-all | bytes 1048576 | tf_op jit(solution)/shard_map/all_to_all | solution.py:295
  154.0 13.5 %all_to_all.56 = f32[32,8,256]{2,1,0:T(8,128)S(1)} all-to-all(f32[32,8,256]{2,1,0:T(8,128)S(1)} %get-tuple-element.22), channel_id=1, replica_groups=mesh['x'=4,'z'=8,'c'=2,'y'=8] {'y','x'}, dimensions={0} | all-to-all | bytes 524288 | tf_op jit(solution)/shard_map/all_to_all | solution.py:295
  167.5 3.7 %all-to-all-start.7 = ((f32[8,56,256]{2,1,0:T(8,128)}), f32[8,56,256]{2,1,0:T(8,128)S(1)}, u32[]{:S(2)}, u32[]{:S(2)}) async-start(f32[8,56,256]{2,1,0:T(8,128)} %get-tuple-element.25), calls=%async_computation.7 | async-start | bytes 917504 | tf_op jit(solution)/shard_map/all_to_all | solution.py:295
  171.2 7.5 %shard_map.63.after.half = f32[3,128,128]{2,1,0:T(8,128)S(1)} custom-call(f32[256,256]{1,0:T(8,128)S(1)} %bitcast.9), custom_call_target="tpu_custom_call" | custom-call | flops 10000000000 | bytes 100000 | tf_op jit(solution)/shard_map/pallas_call | solution.py:337
  178.6 3.2 %all-to-all-done.7.value = f32[8,56,256]{2,1,0:T(8,128)S(1)} async-done(((f32[8,56,256]{2,1,0:T(8,128)}), f32[8,56,256]{2,1,0:T(8,128)S(1)}, u32[]{:S(2)}, u32[]{:S(2)}) %all-to-all-start.7) | async-done | bytes 458784 | tf_op jit(solution)/shard_map/all_to_all | solution.py:295
  183.2 3.6 %all-to-all-start.8 = ((f32[4,8,56,256]{3,2,1,0:T(8,128)}), f32[4,8,56,256]{3,2,1,0:T(8,128)S(1)}, u32[]{:S(2)}, u32[]{:S(2)}) async-start(f32[4,8,56,256]{3,2,1,0:T(8,128)} %shard_map.64), calls=%async_computation.8 | async-start | bytes 3670016 | tf_op jit(solution)/shard_map/all_to_all | solution.py:295
  186.8 7.2 %shard_map.65.inverse = f32[256,256]{1,0:T(8,128)S(1)} custom-call(f32[3,128,128]{2,1,0:T(8,128)S(1)} %shard_map.63.after.half), custom_call_target="tpu_custom_call" | custom-call | flops 10000000000 | bytes 100000 | tf_op jit(solution)/shard_map/pallas_call | solution.py:342
  193.9 9.8 %all-to-all-done.8.own = f32[4,8,56,256]{3,2,1,0:T(8,128)S(1)} async-done(((f32[4,8,56,256]{3,2,1,0:T(8,128)}), f32[4,8,56,256]{3,2,1,0:T(8,128)S(1)}, u32[]{:S(2)}, u32[]{:S(2)}) %all-to-all-start.8) | async-done | bytes 1835040 | tf_op jit(solution)/shard_map/all_to_all | solution.py:295
  203.7 9.4 %collective-permute-start.2 = (f32[4,8,56,256]{3,2,1,0:T(8,128)S(1)}, f32[4,8,56,256]{3,2,1,0:T(8,128)}, u32[]{:S(2)}, u32[]{:S(2)}) collective-permute-start(f32[4,8,56,256]{3,2,1,0:T(8,128)S(1)} %all-to-all-done.8.own), channel_id=1, source_target_pairs={{0,8},{8,0},{1,9},{9,1},{2,10},{10,2},{3,11},{11,3},{4,12},{12,4},... | collective-permute-start | bytes 5505032 | tf_op jit(solution)/shard_map/ppermute | solution.py:299
  213.1 2.5 %shard_map.68 = (f32[56,256]{1,0:T(8,128)S(1)}, f32[16,1,256]{2,1,0:T(1,128)}) custom-call(f32[4,8,56,256]{3,2,1,0:T(8,128)S(1)} %all-to-all-done.8.own, f32[56,256]{1,0:T(8,128)S(1)} %get-tuple-element.32.column_mine, f32[256,256]{1,0:T(8,128)S(1)} %shard_map.65.inverse), custom_call_target="tpu_custom_call" | custom-call | flops 704643072 | bytes 2000000 | tf_op jit(solution)/shard_map/pallas_call | solution.py:345
  215.6 5.4 %all-to-all-start.9 = ((f32[16,1,256]{2,1,0:T(1,128)}), f32[16,1,256]{2,1,0:T(1,128)S(1)}, u32[]{:S(2)}, u32[]{:S(2)}) async-start(f32[16,1,256]{2,1,0:T(1,128)} %get-tuple-element.33), calls=%async_computation.9 | async-start | bytes 32768 | tf_op jit(solution)/shard_map/all_to_all | solution.py:295
  222.3 5.9 %shard_map.67 = (f32[128,3584]{1,0:T(8,128)}, f32[8,128]{1,0:T(8,128)S(1)}) custom-call(s32[3]{0:T(128)S(1)} %pad_add_fusion.where, f32[4,8,56,256]{3,2,1,0:T(8,128)S(1)} %all-to-all-done.8.own, f32[4,8,56,256]{3,2,1,0:T(8,128)} %collective-permute-done.2.other, f32[128,256]{1,0:T(8,128)S(1)} %get-tuple-element.30.weights, f32[128,3584]{1,0:T(8,128)} %mom.5, ...), custom_call_target="tpu_custom_call" | custom-call | flops 704643072 | bytes 9000000 | tf_op jit(solution)/shard_map/pallas_call | solution.py:353
  (11 shorter events, 5.4 us)
Async XLA Ops:
  51.1 9.5 %collective-permute-start = (f32[4,8,56,256]{3,2,1,0:T(8,128)S(1)}, f32[4,8,56,256]{3,2,1,0:T(8,128)}, u32[]{:S(2)}, u32[]{:S(2)}) collective-permute-start(f32[4,8,56,256]{3,2,1,0:T(8,128)S(1)} %all_to_all.51.own), channel_id=1, source_target_pairs={{0,8},{8,0},{1,9},{9,1},{2,10},{10,2},{3,11},{11,3},{4,12},{12,4},... | collective-permute-start | bytes 5505032 | tf_op jit(solution)/shard_map/ppermute | solution.py:299
  98.8 8.7 %collective-permute-start.1 = (f32[4,57,8,256]{3,2,1,0:T(8,128)}, f32[4,57,8,256]{3,2,1,0:T(8,128)S(1)}, u32[]{:S(2)}, u32[]{:S(2)}) collective-permute-start(f32[4,57,8,256]{3,2,1,0:T(8,128)} %get-tuple-element.21), channel_id=1, source_target_pairs={{0,8},{8,0},{1,9},{9,1},{2,10},{10,2},{3,11},{11,3},{4,12},{12,4},... | collective-permute-start | bytes 5603336 | tf_op jit(solution)/shard_map/ppermute | solution.py:299
  167.5 14.3 %all-to-all-start.7 = ((f32[8,56,256]{2,1,0:T(8,128)}), f32[8,56,256]{2,1,0:T(8,128)S(1)}, u32[]{:S(2)}, u32[]{:S(2)}) async-start(f32[8,56,256]{2,1,0:T(8,128)} %get-tuple-element.25), calls=%async_computation.7 | async-start | bytes 917504 | tf_op jit(solution)/shard_map/all_to_all | solution.py:295
  183.2 20.5 %all-to-all-start.8 = ((f32[4,8,56,256]{3,2,1,0:T(8,128)}), f32[4,8,56,256]{3,2,1,0:T(8,128)S(1)}, u32[]{:S(2)}, u32[]{:S(2)}) async-start(f32[4,8,56,256]{3,2,1,0:T(8,128)} %shard_map.64), calls=%async_computation.8 | async-start | bytes 3670016 | tf_op jit(solution)/shard_map/all_to_all | solution.py:295
  203.7 18.5 %collective-permute-start.2 = (f32[4,8,56,256]{3,2,1,0:T(8,128)S(1)}, f32[4,8,56,256]{3,2,1,0:T(8,128)}, u32[]{:S(2)}, u32[]{:S(2)}) collective-permute-start(f32[4,8,56,256]{3,2,1,0:T(8,128)S(1)} %all-to-all-done.8.own), channel_id=1, source_target_pairs={{0,8},{8,0},{1,9},{9,1},{2,10},{10,2},{3,11},{11,3},{4,12},{12,4},... | collective-permute-start | bytes 5505032 | tf_op jit(solution)/shard_map/ppermute | solution.py:299
  215.6 12.8 %all-to-all-start.9 = ((f32[16,1,256]{2,1,0:T(1,128)}), f32[16,1,256]{2,1,0:T(1,128)S(1)}, u32[]{:S(2)}, u32[]{:S(2)}) async-start(f32[16,1,256]{2,1,0:T(1,128)} %get-tuple-element.33), calls=%async_computation.9 | async-start | bytes 32768 | tf_op jit(solution)/shard_map/all_to_all | solution.py:295

commit v4 on v3

--- a/solution.py
+++ b/solution.py
@@ -20,6 +20,7 @@
 GROUP = 8
 PER_SHARD = SHARD // GROUP
 PER_X = NZ * PER_SHARD
+PER_CORE = MY_COLS // NC
 MACS = MY_ROWS * MY_COLS * RANK
 
 highest = lax.Precision.HIGHEST
@@ -99,14 +100,47 @@
 FULL = [pltpu.VMEM((NX, NZ, NC, SHARD, RANK), f32)]
 
 
-def power_kernel(where, own, other, mom, grad, out, mom_here, grad_here, full, sems):
-    copies = gathered_copies(where, own, other, mom, grad, mom_here, grad_here, full, sems)
+def layout_kernel(where, mom, grad, own, other, own_t, other_t):
+    first = where[1] == 0
+    for j in range(NX):
+        part = buffer_chunk(mom, grad, j).T.reshape(NZ, NC, SHARD, MY_ROWS)
+        rows = pl.ds(j * NZ * SHARD, NZ * SHARD)
+        own_t[rows] = jnp.where(first, part[:, 0], part[:, 1]).reshape(NZ * SHARD, MY_ROWS)
+        other_t[rows] = jnp.where(first, part[:, 1], part[:, 0]).reshape(NZ * SHARD, MY_ROWS)
+    for j in range(PER_CORE // CHUNK):
+        own[:, columns(j)] = own_t[columns(j)].T
+        other[:, columns(j)] = other_t[columns(j)].T
+
+
+def own_power_kernel(buffer, factor, out):
     total = None
-    for j in range(NX):
+    for j in range(PER_CORE // CHUNK):
+        part = factor[j * 2 : j * 2 + 2].reshape(CHUNK, RANK)
+        part = dot(buffer[:, columns(j)], part, 1, 0)
+        total = part if total is None else total + part
+    out[...] = total
+
+
+def power_kernel(buffer, factor, before, out, here, full, sems):
+    copies = []
+    for j in range(PER_CORE // CHUNK):
+        pair = pl.ds(j * 2, 2)
+        copies.append(
+            [
+                pltpu.make_async_copy(factor.at[pair], full.at[pair], sems.at[j, 0]),
+                pltpu.make_async_copy(
+                    buffer.at[:, columns(j)], here.at[:, columns(j)], sems.at[j, 1]
+                ),
+            ]
+        )
+        for copy in copies[j]:
+            copy.start()
+    total = before[...]
+    for j in range(PER_CORE // CHUNK):
         for copy in copies[j]:
             copy.wait()
-        part = dot(buffer_chunk(mom_here, grad_here, j), full[j].reshape(CHUNK, RANK), 1, 0)
-        total = part if total is None else total + part
+        part = full[j * 2 : j * 2 + 2].reshape(CHUNK, RANK)
+        total = total + dot(here[:, columns(j)], part, 1, 0)
     out[...] = total
 
 
@@ -116,46 +150,13 @@
         out[i] = total
 
 
-def column_kernel(where, power, mom, grad, keep, send, mom_here, grad_here, full, gram, sems, outs):
-    copies = []
-    for j in range(NX):
-        copies.append(buffer_copies(mom, grad, mom_here, grad_here, sems, j))
-        for copy in copies[j]:
-            copy.start()
+def column_kernel(where, power, buffer_t, after, out, token, gram):
+    token[...] = jnp.zeros_like(token)
     gram[...] = dot(power[...], power[...], 0, 0).reshape(RANK // GROUP, GROUP, RANK)
-    core = where[1]
-    waits = []
-    for j in range(NX):
-        for copy in copies[j]:
-            copy.wait()
-        for q in range(CHUNK // HALF):
-            cols = pl.ds(j * CHUNK + q * HALF, HALF)
-            part = mom_here[:, cols] + grad_here[:, cols].astype(f32)
-            part = dot(part, power[...], 0, 0)
-            full[pl.ds((j * CHUNK + q * HALF) // GROUP, HALF // GROUP)] = part.reshape(
-                HALF // GROUP, GROUP, RANK
-            )
-        for side, (out, c) in enumerate(((send, 1 - core), (keep, core))):
-            for z in range(NZ):
-                start = ((j * NZ + z) * NC + c) * PER_SHARD
-                waits.append(
-                    pltpu.make_async_copy(
-                        full.at[pl.ds(start, PER_SHARD)],
-                        out.at[j, pl.ds(z * PER_SHARD, PER_SHARD)],
-                        outs.at[j, z, side],
-                    )
-                )
-            waits.append(
-                pltpu.make_async_copy(
-                    gram.at[pl.ds(where[2] * NX + j, 1)],
-                    out.at[j, pl.ds(PER_X, 1)],
-                    outs.at[j, NZ, side],
-                )
-            )
-        for copy in waits[-2 * (NZ + 1) :]:
-            copy.start()
-    for copy in waits:
-        copy.wait()
+    for x in range(NX):
+        part = dot(buffer_t[pl.ds(x * NZ * SHARD, NZ * SHARD)], power[...], 1, 0)
+        out[x, 0:PER_X] = part.reshape(PER_X, GROUP, RANK)
+        out[x, pl.ds(PER_X, 1)] = gram[pl.ds(where[2] * NX + x, 1)]
 
 
 def sum_x_kernel(pieces, out):
@@ -240,14 +241,10 @@
     out[HALF:, HALF:] = inner
 
 
-def squares_kernel(own, column_mine, inverse, factor_mine, squares):
+def squares_kernel(gathered, column_mine, inverse, factor_mine, squares):
     factor_mine[...] = dot(column_mine[...], inverse[...], 1, 1)
-    total = jnp.zeros((1, RANK), f32)
-    for x in range(NX):
-        c = dot(own[x].reshape(NZ * SHARD, RANK), inverse[...], 1, 1)
-        total = total + jnp.sum(c * c, axis=0, keepdims=True)
-    for i in range(NY * NC):
-        squares[i] = total
+    c = dot(gathered[...].reshape(NZ * SHARD, RANK), inverse[...], 1, 1)
+    squares[...] = jnp.sum(c * c, axis=0, keepdims=True)
 
 
 def ortho_kernel(power, inverse, row_factor, weights):
@@ -304,25 +301,41 @@
     momentum = pltpu.with_memory_space_constraint(momentum, pltpu.HBM)
     gradient = pltpu.with_memory_space_constraint(gradient, pltpu.HBM)
 
-    own = spread(spread(right_factor, "z", NZ), "x", NX)
+    halves = [shape(MY_ROWS, PER_CORE)] * 2 + [shape(PER_CORE, MY_ROWS)] * 2
+    by_core = call(
+        layout_kernel, halves, [SMEM, VMEM, VMEM], (), None, 1_000_000_000, 9_000_000, 24
+    )(where, momentum, gradient)
+    gathered = spread(right_factor, "z", NZ)
+    gathered, *by_core = lax.optimization_barrier((gathered, *by_core))
+    buffer_own, buffer_other, own_t, other_t = by_core
+    own = spread(gathered, "x", NX)
+    own_power = call(
+        own_power_kernel, shape(MY_ROWS, RANK), [VMEM, VMEM], (), None, 6 * MACS, 3_000_000
+    )(buffer_own, own)
     partial_power = call(
-        power_kernel, shape(MY_ROWS, RANK), [SMEM] + [HBM] * 4,
-        BUFFER_SCRATCH + FULL + SEMS, None, 12 * MACS, 7_000_000,
-    )(where, own, other_core(own), momentum, gradient)
+        power_kernel, shape(MY_ROWS, RANK), [HBM, HBM, VMEM],
+        [
+            pltpu.VMEM((MY_ROWS, PER_CORE), f32),
+            pltpu.VMEM((NX, NZ, SHARD, RANK), f32),
+            pltpu.SemaphoreType.DMA((PER_CORE // CHUNK, 2)),
+        ],
+        None, 6 * MACS, 3_000_000,
+    )(buffer_other, other_core(own), own_power)
 
     pieces = swap(partial_power.reshape(NY, MY_ROWS // NY, RANK), "y")
     copies = call(sum_spread_kernel, shape(NY, MY_ROWS // NY, RANK), [VMEM])(pieces)
     power = swap(copies, "y").reshape(MY_ROWS, RANK)
 
-    keep, send = call(
-        column_kernel, [in_hbm(NX, PER_X + 1, GROUP, RANK)] * 2, [SMEM, VMEM, HBM, HBM],
-        BUFFER_SCRATCH
-        + [pltpu.VMEM((MY_COLS // GROUP, GROUP, RANK), f32)]
-        + [pltpu.VMEM((RANK // GROUP, GROUP, RANK), f32)]
-        + [pltpu.SemaphoreType.DMA((NX, 2)), pltpu.SemaphoreType.DMA((NX, NZ + 1, 2))],
-        [HBM, HBM], 12 * MACS, 7_000_000,
-    )(where, power, momentum, gradient)
-    by_x = swap(keep + other_core(send), "x")
+    def columns_of(buffer_t, after):
+        return call(
+            column_kernel, [shape(NX, PER_X + 1, GROUP, RANK), TOKEN], [SMEM, VMEM, VMEM, ANY],
+            [pltpu.VMEM((RANK // GROUP, GROUP, RANK), f32)], None, 6 * MACS, 3_000_000,
+        )(where, power, buffer_t, after)
+
+    send, token = columns_of(other_t, where)
+    arrived = other_core(send)
+    keep, token = columns_of(own_t, token)
+    by_x = swap(keep + arrived, "x")
     by_z = call(
         sum_x_kernel, shape(NZ, PER_SHARD + 1, GROUP, RANK), [VMEM], nbytes=3_000_000
     )(by_x)
@@ -335,21 +348,23 @@
     gram = swap(gram, ("y", "x")).reshape(RANK, RANK)
     gram, copies = lax.optimization_barrier((gram, copies))
     half = call(first_half_kernel, shape(3, HALF, HALF), [VMEM], flops=10_000_000_000)(gram)
+    gathered = swap(copies, "z")
     copies = call(
         copies_kernel, shape(NX, NZ, SHARD, RANK), [VMEM, ANY], nbytes=3_000_000
-    )(swap(copies, "z"), half)
+    )(gathered, half)
     half, copies = lax.optimization_barrier((half, copies))
+    own = swap(copies, "x")
     inverse = call(second_half_kernel, shape(RANK, RANK), [VMEM], flops=10_000_000_000)(half)
-    own = swap(copies, "x")
-    own, inverse = lax.optimization_barrier((own, inverse))
     factor_mine, squares = call(
-        squares_kernel, [shape(SHARD, RANK), shape(NY * NC, 1, RANK)], [VMEM] * 3, (), None,
-        6 * MACS, 2_000_000,
-    )(own, column_mine, inverse)
-    squares = swap(squares, ("y", "c"))
+        squares_kernel, [shape(SHARD, RANK), shape(1, RANK)], [VMEM] * 3, (), None, 2 * MACS
+    )(gathered, column_mine, inverse)
+    for bit in (1, 2):
+        squares = squares + lax.ppermute(squares, "x", [(i, i ^ bit) for i in range(NX)])
     row_factor, weights = call(
         ortho_kernel, [shape(MY_ROWS, RANK)] * 2, [VMEM, VMEM]
     )(power, inverse)
+    own, squares, weights = lax.optimization_barrier((own, squares, weights))
+    squares = swap(jnp.broadcast_to(squares[None], (NY * NC, 1, RANK)), ("y", "c"))
     new_momentum, token = call(
         momentum_kernel, [in_hbm(MY_ROWS, MY_COLS), TOKEN], [SMEM, HBM, HBM, VMEM, HBM, HBM],
         BUFFER_SCRATCH + FULL + SEMS + [pltpu.SemaphoreType.DMA((NX,))],

time: 230 us -> 227 us (0.987)
  blocking collectives: 132 us -> 109 us
  starting transfers between devices: 33.1 us -> 49.3 us
  waiting for transfers between devices: 20.3 us -> 26.9 us
  Pallas kernels: 40.5 us -> 36.5 us
    all_to_all x7 -> x6, blocking collectives: 132 us -> 109 us  [swap(): return lax.all_to_all(pieces, axis, 0, 0)]
    all_to_all x3 -> x4, starting transfers between devices: 12.7 us -> 23.9 us  [swap(): return lax.all_to_all(pieces, axis, 0, 0)]
    ppermute x0 -> x2, starting transfers between devices: none -> 7.61 us  [shards(): lax.ppermute(squares, 'x', [(i, i ^ bit) for i in range(NX)])]
    ppermute x0 -> x2, waiting for transfers between devices: none -> 6.14 us  [shards(): lax.ppermute(squares, 'x', [(i, i ^ bit) for i in range(NX)])]
    all_to_all x3 -> x4, waiting for transfers between devices: 13.2 us -> 17.4 us  [swap(): return lax.all_to_all(pieces, axis, 0, 0)]
    pallas_call x3 -> x6, Pallas kernels: 15.8 us -> 11.8 us  [the longest x2 4.7 us: columns_of(): call(column_kernel, [shape(NX, PER_X + 1, GROUP, RANK), TOKEN], [SMEM, VM...]
    ppermute x3, waiting for transfers between devices: 7.09 us -> 3.29 us  [other_core(): return lax.ppermute(value, 'c', [(0, 1), (1, 0)])]
    ppermute x3, starting transfers between devices: 20.4 us -> 17.8 us  [other_core(): return lax.ppermute(value, 'c', [(0, 1), (1, 0)])]
  transfers between devices with their start and end apart: 6 -> 9, of which waited for: 5 -> 7; matrix products, arithmetic and copies ran while one was open for 0% -> 0% of each run, Pallas kernels for 11% -> 13%
where the time goes in v4:
time: 227 us; the launch traced here: 226 us
  blocking collectives  109 us (48%)
  starting transfers between devices  49.3 us (22%)
  Pallas kernels  36.5 us (16%)
  waiting for transfers between devices  26.9 us (12%)
  local copies, waits for them, and re-layouts  3.3 us (1%)
    all_to_all x6, blocking collectives, swap(): return lax.all_to_all(pieces, axis, 0, 0)  109 us
    all_to_all x4, starting transfers between devices, swap(): return lax.all_to_all(pieces, axis, 0, 0)  23.9 us
    ppermute x3, starting transfers between devices, other_core(): return lax.ppermute(value, 'c', [(0, 1), (1, 0)])  17.8 us
    all_to_all x4, waiting for transfers between devices, swap(): return lax.all_to_all(pieces, axis, 0, 0)  17.4 us
    ppermute x2, starting transfers between devices, shards(): lax.ppermute(squares, 'x', [(i, i ^ bit) for i in range(NX)])  7.61 us
    pallas_call x1, Pallas kernels, shards(): call(first_half_kernel, shape(3, HALF, HALF), [VMEM], flops=10000000000)  7.46 us
    pallas_call x1, Pallas kernels, shards(): call(second_half_kernel, shape(RANK, RANK), [VMEM], flops=10000000000)(half)  7.16 us
    ppermute x2, waiting for transfers between devices, shards(): lax.ppermute(squares, 'x', [(i, i ^ bit) for i in range(NX)])  6.14 us
  transfers between devices with their start and end apart: 9, of which 7 were waited for; matrix products, arithmetic and copies ran while one was open for 0% of the time, Pallas kernels for 13%

profile of v4, /device:TPU:1, one launch (start us, length us, event | category | flops | bytes accessed | tf_op | source)
XLA Modules:
  0.0 225.8 jit_solution(10475020264441338547)
XLA Ops:
  2.2 10.9 %all-to-all-start = ((f32[8,56,256]{2,1,0:T(8,128)}), f32[8,56,256]{2,1,0:T(8,128)S(1)}, u32[]{:S(2)}, u32[]{:S(2)}) async-start(f32[8,56,256]{2,1,0:T(8,128)} %broadcast_in_dim.8), calls=%async_computation | async-start | bytes 917504 | tf_op jit(solution)/shard_map/all_to_all | solution.py:292
  13.2 2.7 %shard_map.58 = (f32[128,1792]{1,0:T(8,128)S(1)}, f32[128,1792]{1,0:T(8,128)S(1)}, f32[1792,128]{1,0:T(8,128)S(1)}, f32[1792,128]{1,0:T(8,128)S(1)}) custom-call(s32[3]{0:T(128)S(1)} %pad_add_fusion.where.after, f32[128,3584]{1,0:T(8,128)} %mom.3, bf16[128,3584]{1,0:T(8,128)(2,1)} %grad.3), custom_call_target="tpu_custom_call" | custom-call | flops 1000000000 | bytes 9000000 | tf_op jit(solution)/shard_map/pallas_call | solution.py:305
  16.9 12.7 %all-to-all-done = f32[8,56,256]{2,1,0:T(8,128)S(1)} async-done(((f32[8,56,256]{2,1,0:T(8,128)}), f32[8,56,256]{2,1,0:T(8,128)S(1)}, u32[]{:S(2)}, u32[]{:S(2)}) %all-to-all-start) | async-done | bytes 458784 | tf_op jit(solution)/shard_map/all_to_all | solution.py:292
  29.7 26.5 %all_to_all.50.factor = f32[4,8,56,256]{3,2,1,0:T(8,128)S(1)} all-to-all(f32[4,8,56,256]{3,2,1,0:T(8,128)S(1)} %broadcast_in_dim.9), channel_id=1, replica_groups=mesh['x'=4,'z'=8,'c'=2,'y'=8] {'x'}, dimensions={0} | all-to-all | bytes 3670016 | tf_op jit(solution)/shard_map/all_to_all | solution.py:292
  56.2 3.7 %collective-permute-start = (f32[4,8,56,256]{3,2,1,0:T(8,128)S(1)}, f32[4,8,56,256]{3,2,1,0:T(8,128)S(1)}, u32[]{:S(2)}, u32[]{:S(2)}) collective-permute-start(f32[4,8,56,256]{3,2,1,0:T(8,128)S(1)} %all_to_all.50.factor), channel_id=1, source_target_pairs={{0,8},{8,0},{1,9},{9,1},{2,10},{10,2},{3,11},{11,3},{4,12},{12,4},... | collective-permute-start | bytes 5505032 | tf_op jit(solution)/shard_map/ppermute | solution.py:296
  63.3 2.4 %shard_map.60 = f32[128,256]{1,0:T(8,128)S(1)} custom-call(f32[128,1792]{1,0:T(8,128)S(1)} %get-tuple-element.35.buffer, f32[4,8,56,256]{3,2,1,0:T(8,128)S(1)} %collective-permute-done.factor, f32[128,256]{1,0:T(8,128)S(1)} %shard_map.59.before), custom_call_target="tpu_custom_call" | custom-call | flops 704643072 | bytes 3000000 | tf_op jit(solution)/shard_map/pallas_call | solution.py:315
  65.8 14.5 %all_to_all.51.pieces = f32[8,16,256]{2,1,0:T(8,128)S(1)} all-to-all(f32[8,16,256]{2,1,0:T(8,128)S(1)} %bitcast.10), channel_id=1, replica_groups=mesh['x'=4,'z'=8,'c'=2,'y'=8] {'y'}, dimensions={0} | all-to-all | bytes 262144 | tf_op jit(solution)/shard_map/all_to_all | solution.py:292
  80.3 10.4 %all_to_all.52 = f32[8,16,256]{2,1,0:T(8,128)S(1)} all-to-all(f32[8,16,256]{2,1,0:T(8,128)S(1)} %shard_map.61), channel_id=1, replica_groups=mesh['x'=4,'z'=8,'c'=2,'y'=8] {'y'}, dimensions={0} | all-to-all | bytes 262144 | tf_op jit(solution)/shard_map/all_to_all | solution.py:292
  93.1 5.1 %collective-permute-start.1 = (f32[4,57,8,256]{3,2,1,0:T(8,128)S(1)}, f32[4,57,8,256]{3,2,1,0:T(8,128)S(1)}, u32[]{:S(2)}, u32[]{:S(2)}) collective-permute-start(f32[4,57,8,256]{3,2,1,0:T(8,128)S(1)} %get-tuple-element.42), channel_id=1, source_target_pairs={{0,8},{8,0},{1,9},{9,1},{2,10},{10,2},{3,11},{11,3},{4,12},{12,4},... | collective-permute-start | bytes 5603336 | tf_op jit(solution)/shard_map/ppermute | solution.py:296
  98.2 2.4 %shard_map.63 = (f32[4,57,8,256]{3,2,1,0:T(8,128)S(1)}, f32[8,128]{1,0:T(8,128)}) custom-call(s32[3]{0:T(128)S(1)} %pad_add_fusion.where.after, f32[128,256]{1,0:T(8,128)S(1)} %bitcast.8, f32[1792,128]{1,0:T(8,128)S(1)} %get-tuple-element.38.buffer_t, f32[8,128]{1,0:T(8,128)S(1)} %get-tuple-element.40.after), custom_call_target="tpu_custom_call" | custom-call | flops 704643072 | bytes 3000000 | tf_op jit(solution)/shard_map/pallas_call | solution.py:330
  101.8 25.9 %all_to_all.53.pieces = f32[4,57,8,256]{3,2,1,0:T(8,128)S(1)} all-to-all(f32[4,57,8,256]{3,2,1,0:T(8,128)S(1)} %add.9), channel_id=1, replica_groups=mesh['x'=4,'z'=8,'c'=2,'y'=8] {'x'}, dimensions={0} | all-to-all | bytes 3735552 | tf_op jit(solution)/shard_map/all_to_all | solution.py:292
  127.8 17.9 %all_to_all.54.pieces = f32[8,8,8,256]{3,2,1,0:T(8,128)S(1)} all-to-all(f32[8,8,8,256]{3,2,1,0:T(8,128)S(1)} %shard_map.64), channel_id=1, replica_groups=mesh['x'=4,'z'=8,'c'=2,'y'=8] {'z'}, dimensions={0} | all-to-all | bytes 1048576 | tf_op jit(solution)/shard_map/all_to_all | solution.py:292
  146.6 13.6 %all_to_all.55 = f32[32,8,256]{2,1,0:T(8,128)S(1)} all-to-all(f32[32,8,256]{2,1,0:T(8,128)S(1)} %get-tuple-element.43), channel_id=1, replica_groups=mesh['x'=4,'z'=8,'c'=2,'y'=8] {'y','x'}, dimensions={0} | all-to-all | bytes 524288 | tf_op jit(solution)/shard_map/all_to_all | solution.py:292
  160.1 3.7 %all-to-all-start.7 = ((f32[8,56,256]{2,1,0:T(8,128)}), f32[8,56,256]{2,1,0:T(8,128)S(1)}, u32[]{:S(2)}, u32[]{:S(2)}) async-start(f32[8,56,256]{2,1,0:T(8,128)} %get-tuple-element.46), calls=%async_computation.7 | async-start | bytes 917504 | tf_op jit(solution)/shard_map/all_to_all | solution.py:292
  163.8 7.5 %shard_map.66.after.half = f32[3,128,128]{2,1,0:T(8,128)S(1)} custom-call(f32[256,256]{1,0:T(8,128)S(1)} %bitcast.11), custom_call_target="tpu_custom_call" | custom-call | flops 10000000000 | bytes 100000 | tf_op jit(solution)/shard_map/pallas_call | solution.py:350
  171.2 3.3 %all-to-all-done.7.value.gathered = f32[8,56,256]{2,1,0:T(8,128)S(1)} async-done(((f32[8,56,256]{2,1,0:T(8,128)}), f32[8,56,256]{2,1,0:T(8,128)S(1)}, u32[]{:S(2)}, u32[]{:S(2)}) %all-to-all-start.7) | async-done | bytes 458784 | tf_op jit(solution)/shard_map/all_to_all | solution.py:292
  175.9 4.2 %all-to-all-start.8 = ((f32[4,8,56,256]{3,2,1,0:T(8,128)}), f32[4,8,56,256]{3,2,1,0:T(8,128)S(1)}, u32[]{:S(2)}, u32[]{:S(2)}) async-start(f32[4,8,56,256]{3,2,1,0:T(8,128)} %shard_map.67), calls=%async_computation.8 | async-start | bytes 3670016 | tf_op jit(solution)/shard_map/all_to_all | solution.py:292
  180.1 7.2 %shard_map.68.inverse = f32[256,256]{1,0:T(8,128)S(1)} custom-call(f32[3,128,128]{2,1,0:T(8,128)S(1)} %shard_map.66.after.half), custom_call_target="tpu_custom_call" | custom-call | flops 10000000000 | bytes 100000 | tf_op jit(solution)/shard_map/pallas_call | solution.py:357
  188.1 3.4 %collective-permute-start.2 = (f32[1,256]{1,0:T(1,128)S(1)}, f32[1,256]{1,0:T(1,128)S(1)}, u32[]{:S(2)}, u32[]{:S(2)}) collective-permute-start(f32[1,256]{1,0:T(1,128)S(1)} %get-tuple-element.50), channel_id=1, source_target_pairs={{0,128},{128,0},{256,384},{384,256},{1,129},{129,1},{257,385},{385... | collective-permute-start | bytes 3080 | tf_op jit(solution)/shard_map/ppermute | solution.py:362
  191.5 5.4 %collective-permute-done.2 = f32[1,256]{1,0:T(1,128)S(1)} collective-permute-done((f32[1,256]{1,0:T(1,128)S(1)}, f32[1,256]{1,0:T(1,128)S(1)}, u32[]{:S(2)}, u32[]{:S(2)}) %collective-permute-start.2) | collective-permute-done | bytes 1056 | tf_op jit(solution)/shard_map/ppermute | solution.py:362
  196.9 4.2 %collective-permute-start.3 = (f32[1,256]{1,0:T(1,128)S(1)}, f32[1,256]{1,0:T(1,128)S(1)}, u32[]{:S(2)}, u32[]{:S(2)}) collective-permute-start(f32[1,256]{1,0:T(1,128)S(1)} %add.10), channel_id=1, source_target_pairs={{0,256},{128,384},{256,0},{384,128},{1,257},{129,385},{257,1},{385... | collective-permute-start | bytes 3080 | tf_op jit(solution)/shard_map/ppermute | solution.py:362
  203.1 9.0 %collective-permute-start.4 = (f32[4,8,56,256]{3,2,1,0:T(8,128)S(1)}, f32[4,8,56,256]{3,2,1,0:T(8,128)}, u32[]{:S(2)}, u32[]{:S(2)}) collective-permute-start(f32[4,8,56,256]{3,2,1,0:T(8,128)S(1)} %all-to-all-done.8.own), channel_id=1, source_target_pairs={{0,8},{8,0},{1,9},{9,1},{2,10},{10,2},{3,11},{11,3},{4,12},{12,4},... | collective-permute-start | bytes 5505032 | tf_op jit(solution)/shard_map/ppermute | solution.py:296
  212.7 5.1 %all-to-all-start.9 = ((f32[16,1,256]{2,1,0:T(1,128)}), f32[16,1,256]{2,1,0:T(1,128)S(1)}, u32[]{:S(2)}, u32[]{:S(2)}) async-start(f32[16,1,256]{2,1,0:T(1,128)} %broadcast_in_dim.11), calls=%async_computation.9 | async-start | bytes 32768 | tf_op jit(solution)/shard_map/all_to_all | solution.py:292
  217.8 5.9 %shard_map.71 = (f32[128,3584]{1,0:T(8,128)}, f32[8,128]{1,0:T(8,128)S(1)}) custom-call(s32[3]{0:T(128)S(1)} %pad_add_fusion.where.after, f32[4,8,56,256]{3,2,1,0:T(8,128)S(1)} %all-to-all-done.8.own, f32[4,8,56,256]{3,2,1,0:T(8,128)} %collective-permute-done.4.other, f32[128,256]{1,0:T(8,128)S(1)} %get-tuple-element.53.weights, f32[128,3584]{1,0:T(8,128)} %mom.3, ...), custom_call_target="tpu_custom_call" | custom-call | flops 704643072 | bytes 9000000 | tf_op jit(solution)/shard_map/pallas_call | solution.py:368
  (26 shorter events, 17.5 us)
Async XLA Ops:
  2.2 27.3 %all-to-all-start = ((f32[8,56,256]{2,1,0:T(8,128)}), f32[8,56,256]{2,1,0:T(8,128)S(1)}, u32[]{:S(2)}, u32[]{:S(2)}) async-start(f32[8,56,256]{2,1,0:T(8,128)} %broadcast_in_dim.8), calls=%async_computation | async-start | bytes 917504 | tf_op jit(solution)/shard_map/all_to_all | solution.py:292
  15.9 0.9 copy-start
  56.2 7.1 %collective-permute-start = (f32[4,8,56,256]{3,2,1,0:T(8,128)S(1)}, f32[4,8,56,256]{3,2,1,0:T(8,128)S(1)}, u32[]{:S(2)}, u32[]{:S(2)}) collective-permute-start(f32[4,8,56,256]{3,2,1,0:T(8,128)S(1)} %all_to_all.50.factor), channel_id=1, source_target_pairs={{0,8},{8,0},{1,9},{9,1},{2,10},{10,2},{3,11},{11,3},{4,12},{12,4},... | collective-permute-start | bytes 5505032 | tf_op jit(solution)/shard_map/ppermute | solution.py:296
  61.1 29.6 %copy-start.1 = (f32[1792,128]{1,0:T(8,128)S(1)}, f32[1792,128]{1,0:T(8,128)}, u32[]{:S(2)}) copy-start(f32[1792,128]{1,0:T(8,128)} %copy-done) | copy-start | bytes 2752516
  93.1 8.5 %collective-permute-start.1 = (f32[4,57,8,256]{3,2,1,0:T(8,128)S(1)}, f32[4,57,8,256]{3,2,1,0:T(8,128)S(1)}, u32[]{:S(2)}, u32[]{:S(2)}) collective-permute-start(f32[4,57,8,256]{3,2,1,0:T(8,128)S(1)} %get-tuple-element.42), channel_id=1, source_target_pairs={{0,8},{8,0},{1,9},{9,1},{2,10},{10,2},{3,11},{11,3},{4,12},{12,4},... | collective-permute-start | bytes 5603336 | tf_op jit(solution)/shard_map/ppermute | solution.py:296
  160.1 14.5 %all-to-all-start.7 = ((f32[8,56,256]{2,1,0:T(8,128)}), f32[8,56,256]{2,1,0:T(8,128)S(1)}, u32[]{:S(2)}, u32[]{:S(2)}) async-start(f32[8,56,256]{2,1,0:T(8,128)} %get-tuple-element.46), calls=%async_computation.7 | async-start | bytes 917504 | tf_op jit(solution)/shard_map/all_to_all | solution.py:292
  175.9 27.1 %all-to-all-start.8 = ((f32[4,8,56,256]{3,2,1,0:T(8,128)}), f32[4,8,56,256]{3,2,1,0:T(8,128)S(1)}, u32[]{:S(2)}, u32[]{:S(2)}) async-start(f32[4,8,56,256]{3,2,1,0:T(8,128)} %shard_map.67), calls=%async_computation.8 | async-start | bytes 3670016 | tf_op jit(solution)/shard_map/all_to_all | solution.py:292
  188.1 8.8 %collective-permute-start.2 = (f32[1,256]{1,0:T(1,128)S(1)}, f32[1,256]{1,0:T(1,128)S(1)}, u32[]{:S(2)}, u32[]{:S(2)}) collective-permute-start(f32[1,256]{1,0:T(1,128)S(1)} %get-tuple-element.50), channel_id=1, source_target_pairs={{0,128},{128,0},{256,384},{384,256},{1,129},{129,1},{257,385},{385... | collective-permute-start | bytes 3080 | tf_op jit(solution)/shard_map/ppermute | solution.py:362
  196.9 6.2 %collective-permute-start.3 = (f32[1,256]{1,0:T(1,128)S(1)}, f32[1,256]{1,0:T(1,128)S(1)}, u32[]{:S(2)}, u32[]{:S(2)}) collective-permute-start(f32[1,256]{1,0:T(1,128)S(1)} %add.10), channel_id=1, source_target_pairs={{0,256},{128,384},{256,0},{384,128},{1,257},{129,385},{257,1},{385... | collective-permute-start | bytes 3080 | tf_op jit(solution)/shard_map/ppermute | solution.py:362
  203.1 14.8 %collective-permute-start.4 = (f32[4,8,56,256]{3,2,1,0:T(8,128)S(1)}, f32[4,8,56,256]{3,2,1,0:T(8,128)}, u32[]{:S(2)}, u32[]{:S(2)}) collective-permute-start(f32[4,8,56,256]{3,2,1,0:T(8,128)S(1)} %all-to-all-done.8.own), channel_id=1, source_target_pairs={{0,8},{8,0},{1,9},{9,1},{2,10},{10,2},{3,11},{11,3},{4,12},{12,4},... | collective-permute-start | bytes 5505032 | tf_op jit(solution)/shard_map/ppermute | solution.py:296
  212.7 12.5 %all-to-all-start.9 = ((f32[16,1,256]{2,1,0:T(1,128)}), f32[16,1,256]{2,1,0:T(1,128)S(1)}, u32[]{:S(2)}, u32[]{:S(2)}) async-start(f32[16,1,256]{2,1,0:T(1,128)} %broadcast_in_dim.11), calls=%async_computation.9 | async-start | bytes 32768 | tf_op jit(solution)/shard_map/all_to_all | solution.py:292

commit v5 on v4

--- a/solution.py
+++ b/solution.py
@@ -18,8 +18,7 @@
 CHUNK = NZ * NC * SHARD
 HALF = 128
 GROUP = 8
-PER_SHARD = SHARD // GROUP
-PER_X = NZ * PER_SHARD
+SOME = RANK // NY
 PER_CORE = MY_COLS // NC
 MACS = MY_ROWS * MY_COLS * RANK
 
@@ -150,30 +149,33 @@
         out[i] = total
 
 
-def column_kernel(where, power, buffer_t, after, out, token, gram):
-    token[...] = jnp.zeros_like(token)
-    gram[...] = dot(power[...], power[...], 0, 0).reshape(RANK // GROUP, GROUP, RANK)
+def column_product(power, buffer_t, out):
     for x in range(NX):
         part = dot(buffer_t[pl.ds(x * NZ * SHARD, NZ * SHARD)], power[...], 1, 0)
-        out[x, 0:PER_X] = part.reshape(PER_X, GROUP, RANK)
-        out[x, pl.ds(PER_X, 1)] = gram[pl.ds(where[2] * NX + x, 1)]
+        out[x] = part.reshape(NZ, SHARD, RANK)
+
+
+def send_kernel(where, power, buffer_t, out, some, gram):
+    gram[...] = dot(power[...], power[...], 0, 0)
+    some[...] = gram[pl.ds(pl.multiple_of(where[2] * SOME, 8), SOME), :]
+    column_product(power, buffer_t, out)
+
+
+def keep_kernel(power, buffer_t, after, out):
+    column_product(power, buffer_t, out)
 
 
 def sum_x_kernel(pieces, out):
-    total = (pieces[0] + pieces[1]) + (pieces[2] + pieces[3])
-    for z in range(NZ):
-        out[z, 0:PER_SHARD] = total[z * PER_SHARD : (z + 1) * PER_SHARD]
-        out[z, PER_SHARD] = total[PER_X]
-
-
-def sum_z_kernel(pieces, mine, copies, gram):
-    total = jnp.sum(pieces[...], axis=0)
-    column = total[0:PER_SHARD].reshape(SHARD, RANK)
+    out[...] = (pieces[0] + pieces[1]) + (pieces[2] + pieces[3])
+
+
+def sum_z_kernel(pieces, some, mine, copies, gram):
+    column = jnp.sum(pieces[...], axis=0)
     mine[...] = column
     for i in range(NZ):
         copies[i] = column
-    for i in range(NX * NY):
-        gram[i] = total[PER_SHARD]
+    for i in range(NY):
+        gram[i] = some[...]
 
 
 def copies_kernel(value, after, out):
@@ -241,10 +243,14 @@
     out[HALF:, HALF:] = inner
 
 
-def squares_kernel(gathered, column_mine, inverse, factor_mine, squares):
+def squares_kernel(own, column_mine, inverse, factor_mine, squares):
     factor_mine[...] = dot(column_mine[...], inverse[...], 1, 1)
-    c = dot(gathered[...].reshape(NZ * SHARD, RANK), inverse[...], 1, 1)
-    squares[...] = jnp.sum(c * c, axis=0, keepdims=True)
+    total = jnp.zeros((1, RANK), f32)
+    for x in range(NX):
+        c = dot(own[x].reshape(NZ * SHARD, RANK), inverse[...], 1, 1)
+        total = total + jnp.sum(c * c, axis=0, keepdims=True)
+    for i in range(NY * NC):
+        squares[i] = total
 
 
 def ortho_kernel(power, inverse, row_factor, weights):
@@ -273,8 +279,8 @@
         for copy in copies[j]:
             copy.wait()
         fh, fl = split(full[j].reshape(CHUNK, RANK))
-        change = dot(high, fh, 1, 1, None) + (dot(high, fl, 1, 1, None) + dot(low, fh, 1, 1, None))
-        mom_here[:, columns(j)] = buffer_chunk(mom_here, grad_here, j) - change
+        change = dot(fh, high, 1, 1, None) + (dot(fh, low, 1, 1, None) + dot(fl, high, 1, 1, None))
+        mom_here[:, columns(j)] = buffer_chunk(mom_here, grad_here, j) - change.T
         copies[j] = pltpu.make_async_copy(
             mom_here.at[:, columns(j)], out.at[:, columns(j)], done.at[j]
         )
@@ -294,6 +300,14 @@
 
 def other_core(value):
     return lax.ppermute(value, "c", [(0, 1), (1, 0)])
+
+
+def sum_along(value, axis, size):
+    bit = 1
+    while bit < size:
+        value = value + lax.ppermute(value, axis, [(i, i ^ bit) for i in range(size)])
+        bit *= 2
+    return value
 
 
 def shards(momentum, gradient, right_factor):
@@ -326,26 +340,32 @@
     copies = call(sum_spread_kernel, shape(NY, MY_ROWS // NY, RANK), [VMEM])(pieces)
     power = swap(copies, "y").reshape(MY_ROWS, RANK)
 
-    def columns_of(buffer_t, after):
-        return call(
-            column_kernel, [shape(NX, PER_X + 1, GROUP, RANK), TOKEN], [SMEM, VMEM, VMEM, ANY],
-            [pltpu.VMEM((RANK // GROUP, GROUP, RANK), f32)], None, 6 * MACS, 3_000_000,
-        )(where, power, buffer_t, after)
-
-    send, token = columns_of(other_t, where)
+    full = shape(NX, NZ, SHARD, RANK)
+    send, some = call(
+        send_kernel, [full, shape(SOME, RANK)], [SMEM, VMEM, VMEM],
+        [pltpu.VMEM((RANK, RANK), f32)], None, 6 * MACS, 3_000_000,
+    )(where, power, other_t)
     arrived = other_core(send)
-    keep, token = columns_of(own_t, token)
-    by_x = swap(keep + arrived, "x")
-    by_z = call(
-        sum_x_kernel, shape(NZ, PER_SHARD + 1, GROUP, RANK), [VMEM], nbytes=3_000_000
-    )(by_x)
+    keep = call(keep_kernel, full, [VMEM, VMEM, ANY], (), None, 6 * MACS, 3_000_000)(
+        power, own_t, some
+    )
+    sums = keep + arrived
+    some = some + other_core(some)
+    sums, some = lax.optimization_barrier((sums, some))
+    by_x = swap(sums, "x")
+    some = sum_along(some, "z", NZ)
+    by_x, some = lax.optimization_barrier((by_x, some))
+    by_z = call(sum_x_kernel, shape(NZ, SHARD, RANK), [VMEM], nbytes=3_000_000)(by_x)
+    by_z, some = lax.optimization_barrier((by_z, some))
+    swapped = swap(by_z, "z")
+    some = sum_along(some, "x", NX)
     column_mine, copies, gram = call(
         sum_z_kernel,
-        [shape(SHARD, RANK), shape(NZ, SHARD, RANK), shape(NX * NY, GROUP, RANK)],
-        [VMEM],
-    )(swap(by_z, "z"))
-
-    gram = swap(gram, ("y", "x")).reshape(RANK, RANK)
+        [shape(SHARD, RANK), shape(NZ, SHARD, RANK), shape(NY, SOME, RANK)],
+        [VMEM, VMEM],
+    )(swapped, some)
+
+    gram = swap(gram, "y").reshape(RANK, RANK)
     gram, copies = lax.optimization_barrier((gram, copies))
     half = call(first_half_kernel, shape(3, HALF, HALF), [VMEM], flops=10_000_000_000)(gram)
     gathered = swap(copies, "z")
@@ -355,16 +375,15 @@
     half, copies = lax.optimization_barrier((half, copies))
     own = swap(copies, "x")
     inverse = call(second_half_kernel, shape(RANK, RANK), [VMEM], flops=10_000_000_000)(half)
-    factor_mine, squares = call(
-        squares_kernel, [shape(SHARD, RANK), shape(1, RANK)], [VMEM] * 3, (), None, 2 * MACS
-    )(gathered, column_mine, inverse)
-    for bit in (1, 2):
-        squares = squares + lax.ppermute(squares, "x", [(i, i ^ bit) for i in range(NX)])
     row_factor, weights = call(
         ortho_kernel, [shape(MY_ROWS, RANK)] * 2, [VMEM, VMEM]
     )(power, inverse)
-    own, squares, weights = lax.optimization_barrier((own, squares, weights))
-    squares = swap(jnp.broadcast_to(squares[None], (NY * NC, 1, RANK)), ("y", "c"))
+    own, weights, inverse = lax.optimization_barrier((own, weights, inverse))
+    factor_mine, squares = call(
+        squares_kernel, [shape(SHARD, RANK), shape(NY * NC, 1, RANK)], [VMEM] * 3, (), None,
+        6 * MACS, 2_000_000,
+    )(own, column_mine, inverse)
+    squares = swap(squares, ("y", "c"))
     new_momentum, token = call(
         momentum_kernel, [in_hbm(MY_ROWS, MY_COLS), TOKEN], [SMEM, HBM, HBM, VMEM, HBM, HBM],
         BUFFER_SCRATCH + FULL + SEMS + [pltpu.SemaphoreType.DMA((NX,))],

time: 227 us -> 222 us (0.978)
  blocking collectives: 109 us -> 63.3 us
  waiting for transfers between devices: 26.9 us -> 54.6 us
  starting transfers between devices: 49.3 us -> 59.4 us
  Pallas kernels: 36.5 us -> 38.9 us
    all_to_all x6 -> x4, blocking collectives: 109 us -> 63.3 us  [swap(): return lax.all_to_all(pieces, axis, 0, 0)]
    all_to_all x4 -> x6, waiting for transfers between devices: 17.4 us -> 32.4 us  [swap(): return lax.all_to_all(pieces, axis, 0, 0)]
    ppermute x2 -> x5, waiting for transfers between devices: 6.14 us -> 20.1 us  [sum_along(): lax.ppermute(value, axis, [(i, i ^ bit) for i in range(size)])]
    all_to_all x4 -> x6, starting transfers between devices: 23.9 us -> 28.6 us  [swap(): return lax.all_to_all(pieces, axis, 0, 0)]
    ppermute x2 -> x5, starting transfers between devices: 7.61 us -> 10.4 us  [sum_along(): lax.ppermute(value, axis, [(i, i ^ bit) for i in range(size)])]
    ppermute x3 -> x4, starting transfers between devices: 17.8 us -> 20.4 us  [other_core(): return lax.ppermute(value, 'c', [(0, 1), (1, 0)])]
  transfers between devices with their start and end apart: 9 -> 15, of which waited for: 7 -> 12; matrix products, arithmetic and copies ran while one was open for 0% -> 0% of each run, Pallas kernels for 13% -> 14%
where the time goes in v5:
time: 222 us; the launch traced here: 221 us
  blocking collectives  63.3 us (29%)
  starting transfers between devices  59.4 us (27%)
  waiting for transfers between devices  54.6 us (25%)
  Pallas kernels  38.9 us (18%)
  local copies, waits for them, and re-layouts  2.71 us (1%)
    all_to_all x4, blocking collectives, swap(): return lax.all_to_all(pieces, axis, 0, 0)  63.3 us
    all_to_all x6, waiting for transfers between devices, swap(): return lax.all_to_all(pieces, axis, 0, 0)  32.4 us
    all_to_all x6, starting transfers between devices, swap(): return lax.all_to_all(pieces, axis, 0, 0)  28.6 us
    ppermute x4, starting transfers between devices, other_core(): return lax.ppermute(value, 'c', [(0, 1), (1, 0)])  20.4 us
    ppermute x5, waiting for transfers between devices, sum_along(): lax.ppermute(value, axis, [(i, i ^ bit) for i in range(size)])  20.1 us
    ppermute x5, starting transfers between devices, sum_along(): lax.ppermute(value, axis, [(i, i ^ bit) for i in range(size)])  10.4 us
    pallas_call x1, Pallas kernels, shards(): call(first_half_kernel, shape(3, HALF, HALF), [VMEM], flops=10000000000)  7.46 us
    pallas_call x1, Pallas kernels, shards(): call(second_half_kernel, shape(RANK, RANK), [VMEM], flops=10000000000)(half)  7.16 us
  transfers between devices with their start and end apart: 15, of which 12 were waited for; matrix products, arithmetic and copies ran while one was open for 0% of the time, Pallas kernels for 14%

profile of v5, /device:TPU:1, one launch (start us, length us, event | category | flops | bytes accessed | tf_op | source)
XLA Modules:
  0.0 221.3 jit_solution(6956812093013477233)
XLA Ops:
  2.3 10.9 %all-to-all-start = ((f32[8,56,256]{2,1,0:T(8,128)}), f32[8,56,256]{2,1,0:T(8,128)S(1)}, u32[]{:S(2)}, u32[]{:S(2)}) async-start(f32[8,56,256]{2,1,0:T(8,128)} %broadcast_in_dim.4), calls=%async_computation | async-start | bytes 917504 | tf_op jit(solution)/shard_map/all_to_all | solution.py:298
  16.9 12.7 %all-to-all-done = f32[8,56,256]{2,1,0:T(8,128)S(1)} async-done(((f32[8,56,256]{2,1,0:T(8,128)}), f32[8,56,256]{2,1,0:T(8,128)S(1)}, u32[]{:S(2)}, u32[]{:S(2)}) %all-to-all-start) | async-done | bytes 458784 | tf_op jit(solution)/shard_map/all_to_all | solution.py:298
  29.8 26.5 %all_to_all.50.factor = f32[4,8,56,256]{3,2,1,0:T(8,128)S(1)} all-to-all(f32[4,8,56,256]{3,2,1,0:T(8,128)S(1)} %broadcast_in_dim.5), channel_id=1, replica_groups=mesh['x'=4,'z'=8,'c'=2,'y'=8] {'x'}, dimensions={0} | all-to-all | bytes 3670016 | tf_op jit(solution)/shard_map/all_to_all | solution.py:298
  56.2 3.7 %collective-permute-start = (f32[4,8,56,256]{3,2,1,0:T(8,128)S(1)}, f32[4,8,56,256]{3,2,1,0:T(8,128)S(1)}, u32[]{:S(2)}, u32[]{:S(2)}) collective-permute-start(f32[4,8,56,256]{3,2,1,0:T(8,128)S(1)} %all_to_all.50.factor), channel_id=1, source_target_pairs={{0,8},{8,0},{1,9},{9,1},{2,10},{10,2},{3,11},{11,3},{4,12},{12,4},... | collective-permute-start | bytes 5505032 | tf_op jit(solution)/shard_map/ppermute | solution.py:302
  65.8 14.5 %all_to_all.51.pieces = f32[8,16,256]{2,1,0:T(8,128)S(1)} all-to-all(f32[8,16,256]{2,1,0:T(8,128)S(1)} %bitcast.9), channel_id=1, replica_groups=mesh['x'=4,'z'=8,'c'=2,'y'=8] {'y'}, dimensions={0} | all-to-all | bytes 262144 | tf_op jit(solution)/shard_map/all_to_all | solution.py:298
  80.3 10.4 %all_to_all.52 = f32[8,16,256]{2,1,0:T(8,128)S(1)} all-to-all(f32[8,16,256]{2,1,0:T(8,128)S(1)} %shard_map.61), channel_id=1, replica_groups=mesh['x'=4,'z'=8,'c'=2,'y'=8] {'y'}, dimensions={0} | all-to-all | bytes 262144 | tf_op jit(solution)/shard_map/all_to_all | solution.py:298
  93.1 5.1 %collective-permute-start.1 = (f32[4,8,56,256]{3,2,1,0:T(8,128)S(1)}, f32[4,8,56,256]{3,2,1,0:T(8,128)S(1)}, u32[]{:S(2)}, u32[]{:S(2)}) collective-permute-start(f32[4,8,56,256]{3,2,1,0:T(8,128)S(1)} %get-tuple-element.46), channel_id=1, source_target_pairs={{0,8},{8,0},{1,9},{9,1},{2,10},{10,2},{3,11},{11,3},{4,12},{12,4},... | collective-permute-start | bytes 5505032 | tf_op jit(solution)/shard_map/ppermute | solution.py:302
  103.2 3.6 %all-to-all-start.4 = ((f32[4,8,56,256]{3,2,1,0:T(8,128)}), f32[4,8,56,256]{3,2,1,0:T(8,128)S(1)}, u32[]{:S(2)}, u32[]{:S(2)}) async-start(f32[4,8,56,256]{3,2,1,0:T(8,128)} %add.21), calls=%async_computation.4 | async-start | bytes 3670016 | tf_op jit(solution)/shard_map/all_to_all | solution.py:298
  113.7 4.0 %collective-permute-done.4 = f32[32,256]{1,0:T(8,128)S(1)} collective-permute-done((f32[32,256]{1,0:T(8,128)S(1)}, f32[32,256]{1,0:T(8,128)S(1)}, u32[]{:S(2)}, u32[]{:S(2)}) %collective-permute-start.4) | collective-permute-done | bytes 32800 | tf_op jit(solution)/shard_map/ppermute | solution.py:308
  119.6 6.6 %collective-permute-done.5 = f32[32,256]{1,0:T(8,128)S(1)} collective-permute-done((f32[32,256]{1,0:T(8,128)S(1)}, f32[32,256]{1,0:T(8,128)S(1)}, u32[]{:S(2)}, u32[]{:S(2)}) %collective-permute-start.5) | collective-permute-done | bytes 32800 | tf_op jit(solution)/shard_map/ppermute | solution.py:308
  126.3 3.6 %all-to-all-done.4.pieces = f32[4,8,56,256]{3,2,1,0:T(8,128)S(1)} async-done(((f32[4,8,56,256]{3,2,1,0:T(8,128)}), f32[4,8,56,256]{3,2,1,0:T(8,128)S(1)}, u32[]{:S(2)}, u32[]{:S(2)}) %all-to-all-start.4) | async-done | bytes 1835040 | tf_op jit(solution)/shard_map/all_to_all | solution.py:298
  130.8 3.5 %all-to-all-start.5 = ((f32[8,56,256]{2,1,0:T(8,128)}), f32[8,56,256]{2,1,0:T(8,128)S(1)}, u32[]{:S(2)}, u32[]{:S(2)}) async-start(f32[8,56,256]{2,1,0:T(8,128)} %shard_map.64), calls=%async_computation.5 | async-start | bytes 917504 | tf_op jit(solution)/shard_map/all_to_all | solution.py:298
  141.4 3.9 %collective-permute-done.7 = f32[32,256]{1,0:T(8,128)S(1)} collective-permute-done((f32[32,256]{1,0:T(8,128)S(1)}, f32[32,256]{1,0:T(8,128)S(1)}, u32[]{:S(2)}, u32[]{:S(2)}) %collective-permute-start.7) | collective-permute-done | bytes 32800 | tf_op jit(solution)/shard_map/ppermute | solution.py:308
  145.4 3.6 %all-to-all-done.5.pieces = f32[8,56,256]{2,1,0:T(8,128)S(1)} async-done(((f32[8,56,256]{2,1,0:T(8,128)}), f32[8,56,256]{2,1,0:T(8,128)S(1)}, u32[]{:S(2)}, u32[]{:S(2)}) %all-to-all-start.5) | async-done | bytes 458784 | tf_op jit(solution)/shard_map/all_to_all | solution.py:298
  149.8 11.9 %all_to_all.53 = f32[8,32,256]{2,1,0:T(8,128)S(1)} all-to-all(f32[8,32,256]{2,1,0:T(8,128)S(1)} %get-tuple-element.53), channel_id=1, replica_groups=mesh['x'=4,'z'=8,'c'=2,'y'=8] {'y'}, dimensions={0} | all-to-all | bytes 524288 | tf_op jit(solution)/shard_map/all_to_all | solution.py:298
  161.7 3.7 %all-to-all-start.7 = ((f32[8,56,256]{2,1,0:T(8,128)}), f32[8,56,256]{2,1,0:T(8,128)S(1)}, u32[]{:S(2)}, u32[]{:S(2)}) async-start(f32[8,56,256]{2,1,0:T(8,128)} %get-tuple-element.56), calls=%async_computation.7 | async-start | bytes 917504 | tf_op jit(solution)/shard_map/all_to_all | solution.py:298
  165.3 7.5 %shard_map.66.after.half = f32[3,128,128]{2,1,0:T(8,128)S(1)} custom-call(f32[256,256]{1,0:T(8,128)S(1)} %bitcast.10), custom_call_target="tpu_custom_call" | custom-call | flops 10000000000 | bytes 100000 | tf_op jit(solution)/shard_map/pallas_call | solution.py:370
  172.8 3.2 %all-to-all-done.7.value = f32[8,56,256]{2,1,0:T(8,128)S(1)} async-done(((f32[8,56,256]{2,1,0:T(8,128)}), f32[8,56,256]{2,1,0:T(8,128)S(1)}, u32[]{:S(2)}, u32[]{:S(2)}) %all-to-all-start.7) | async-done | bytes 458784 | tf_op jit(solution)/shard_map/all_to_all | solution.py:298
  177.4 3.6 %all-to-all-start.8 = ((f32[4,8,56,256]{3,2,1,0:T(8,128)}), f32[4,8,56,256]{3,2,1,0:T(8,128)S(1)}, u32[]{:S(2)}, u32[]{:S(2)}) async-start(f32[4,8,56,256]{3,2,1,0:T(8,128)} %shard_map.67), calls=%async_computation.8 | async-start | bytes 3670016 | tf_op jit(solution)/shard_map/all_to_all | solution.py:298
  181.0 7.2 %shard_map.68.inverse = f32[256,256]{1,0:T(8,128)S(1)} custom-call(f32[3,128,128]{2,1,0:T(8,128)S(1)} %shard_map.66.after.half), custom_call_target="tpu_custom_call" | custom-call | flops 10000000000 | bytes 100000 | tf_op jit(solution)/shard_map/pallas_call | solution.py:377
  189.3 8.4 %all-to-all-done.8.own = f32[4,8,56,256]{3,2,1,0:T(8,128)S(1)} async-done(((f32[4,8,56,256]{3,2,1,0:T(8,128)}), f32[4,8,56,256]{3,2,1,0:T(8,128)S(1)}, u32[]{:S(2)}, u32[]{:S(2)}) %all-to-all-start.8) | async-done | bytes 1835040 | tf_op jit(solution)/shard_map/all_to_all | solution.py:298
  197.7 9.6 %collective-permute-start.8 = (f32[4,8,56,256]{3,2,1,0:T(8,128)S(1)}, f32[4,8,56,256]{3,2,1,0:T(8,128)}, u32[]{:S(2)}, u32[]{:S(2)}) collective-permute-start(f32[4,8,56,256]{3,2,1,0:T(8,128)S(1)} %all-to-all-done.8.own), channel_id=1, source_target_pairs={{0,8},{8,0},{1,9},{9,1},{2,10},{10,2},{3,11},{11,3},{4,12},{12,4},... | collective-permute-start | bytes 5505032 | tf_op jit(solution)/shard_map/ppermute | solution.py:302
  209.9 3.4 %all-to-all-start.9 = ((f32[16,1,256]{2,1,0:T(1,128)}), f32[16,1,256]{2,1,0:T(1,128)S(1)}, u32[]{:S(2)}, u32[]{:S(2)}) async-start(f32[16,1,256]{2,1,0:T(1,128)} %get-tuple-element.65), calls=%async_computation.9 | async-start | bytes 32768 | tf_op jit(solution)/shard_map/all_to_all | solution.py:298
  213.3 6.5 %shard_map.70 = (f32[128,3584]{1,0:T(8,128)}, f32[8,128]{1,0:T(8,128)S(1)}) custom-call(s32[3]{0:T(128)S(1)} %pad_add_fusion.where, f32[4,8,56,256]{3,2,1,0:T(8,128)S(1)} %all-to-all-done.8.own, f32[4,8,56,256]{3,2,1,0:T(8,128)} %collective-permute-done.8.other, f32[128,256]{1,0:T(8,128)S(1)} %get-tuple-element.61.weights, f32[128,3584]{1,0:T(8,128)} %mom.3, ...), custom_call_target="tpu_custom_call" | custom-call | flops 704643072 | bytes 9000000 | tf_op jit(solution)/shard_map/pallas_call | solution.py:387
  (39 shorter events, 42.9 us)
Async XLA Ops:
  2.3 27.3 %all-to-all-start = ((f32[8,56,256]{2,1,0:T(8,128)}), f32[8,56,256]{2,1,0:T(8,128)S(1)}, u32[]{:S(2)}, u32[]{:S(2)}) async-start(f32[8,56,256]{2,1,0:T(8,128)} %broadcast_in_dim.4), calls=%async_computation | async-start | bytes 917504 | tf_op jit(solution)/shard_map/all_to_all | solution.py:298
  16.0 0.9 copy-start
  56.2 7.1 %collective-permute-start = (f32[4,8,56,256]{3,2,1,0:T(8,128)S(1)}, f32[4,8,56,256]{3,2,1,0:T(8,128)S(1)}, u32[]{:S(2)}, u32[]{:S(2)}) collective-permute-start(f32[4,8,56,256]{3,2,1,0:T(8,128)S(1)} %all_to_all.50.factor), channel_id=1, source_target_pairs={{0,8},{8,0},{1,9},{9,1},{2,10},{10,2},{3,11},{11,3},{4,12},{12,4},... | collective-permute-start | bytes 5505032 | tf_op jit(solution)/shard_map/ppermute | solution.py:302
  61.2 29.5 %copy-start.1 = (f32[1792,128]{1,0:T(8,128)S(1)}, f32[1792,128]{1,0:T(8,128)}, u32[]{:S(2)}) copy-start(f32[1792,128]{1,0:T(8,128)} %copy-done) | copy-start | bytes 2752516
  93.1 8.6 %collective-permute-start.1 = (f32[4,8,56,256]{3,2,1,0:T(8,128)S(1)}, f32[4,8,56,256]{3,2,1,0:T(8,128)S(1)}, u32[]{:S(2)}, u32[]{:S(2)}) collective-permute-start(f32[4,8,56,256]{3,2,1,0:T(8,128)S(1)} %get-tuple-element.46), channel_id=1, source_target_pairs={{0,8},{8,0},{1,9},{9,1},{2,10},{10,2},{3,11},{11,3},{4,12},{12,4},... | collective-permute-start | bytes 5505032 | tf_op jit(solution)/shard_map/ppermute | solution.py:302
  98.2 3.5 %collective-permute-start.2 = (f32[32,256]{1,0:T(8,128)S(1)}, f32[32,256]{1,0:T(8,128)S(1)}, u32[]{:S(2)}, u32[]{:S(2)}) collective-permute-start(f32[32,256]{1,0:T(8,128)S(1)} %get-tuple-element.45.after), channel_id=1, source_target_pairs={{0,8},{8,0},{1,9},{9,1},{2,10},{10,2},{3,11},{11,3},{4,12},{12,4},... | collective-permute-start | bytes 98312 | tf_op jit(solution)/shard_map/ppermute | solution.py:302
  103.2 26.7 %all-to-all-start.4 = ((f32[4,8,56,256]{3,2,1,0:T(8,128)}), f32[4,8,56,256]{3,2,1,0:T(8,128)S(1)}, u32[]{:S(2)}, u32[]{:S(2)}) async-start(f32[4,8,56,256]{3,2,1,0:T(8,128)} %add.21), calls=%async_computation.4 | async-start | bytes 3670016 | tf_op jit(solution)/shard_map/all_to_all | solution.py:298
  106.8 5.0 %collective-permute-start.3 = (f32[32,256]{1,0:T(8,128)S(1)}, f32[32,256]{1,0:T(8,128)S(1)}, u32[]{:S(2)}, u32[]{:S(2)}) collective-permute-start(f32[32,256]{1,0:T(8,128)S(1)} %add.22), channel_id=1, source_target_pairs={{0,16},{16,0},{32,48},{48,32},{64,80},{80,64},{96,112},{112,96},{1... | collective-permute-start | bytes 98312 | tf_op jit(solution)/shard_map/ppermute | solution.py:308
  111.8 5.9 %collective-permute-start.4 = (f32[32,256]{1,0:T(8,128)S(1)}, f32[32,256]{1,0:T(8,128)S(1)}, u32[]{:S(2)}, u32[]{:S(2)}) collective-permute-start(f32[32,256]{1,0:T(8,128)S(1)} %add.23), channel_id=1, source_target_pairs={{0,32},{16,48},{32,0},{48,16},{64,96},{80,112},{96,64},{112,80},{1... | collective-permute-start | bytes 98312 | tf_op jit(solution)/shard_map/ppermute | solution.py:308
  117.7 8.6 %collective-permute-start.5 = (f32[32,256]{1,0:T(8,128)S(1)}, f32[32,256]{1,0:T(8,128)S(1)}, u32[]{:S(2)}, u32[]{:S(2)}) collective-permute-start(f32[32,256]{1,0:T(8,128)S(1)} %add.24), channel_id=1, source_target_pairs={{0,64},{16,80},{32,96},{48,112},{64,0},{80,16},{96,32},{112,48},{1... | collective-permute-start | bytes 98312 | tf_op jit(solution)/shard_map/ppermute | solution.py:308
  130.8 18.2 %all-to-all-start.5 = ((f32[8,56,256]{2,1,0:T(8,128)}), f32[8,56,256]{2,1,0:T(8,128)S(1)}, u32[]{:S(2)}, u32[]{:S(2)}) async-start(f32[8,56,256]{2,1,0:T(8,128)} %shard_map.64), calls=%async_computation.5 | async-start | bytes 917504 | tf_op jit(solution)/shard_map/all_to_all | solution.py:298
  134.3 4.7 %collective-permute-start.6 = (f32[32,256]{1,0:T(8,128)S(1)}, f32[32,256]{1,0:T(8,128)S(1)}, u32[]{:S(2)}, u32[]{:S(2)}) collective-permute-start(f32[32,256]{1,0:T(8,128)S(1)} %add.25), channel_id=1, source_target_pairs={{0,128},{128,0},{256,384},{384,256},{1,129},{129,1},{257,385},{385... | collective-permute-start | bytes 98312 | tf_op jit(solution)/shard_map/ppermute | solution.py:308
  138.9 6.4 %collective-permute-start.7 = (f32[32,256]{1,0:T(8,128)S(1)}, f32[32,256]{1,0:T(8,128)S(1)}, u32[]{:S(2)}, u32[]{:S(2)}) collective-permute-start(f32[32,256]{1,0:T(8,128)S(1)} %add.26), channel_id=1, source_target_pairs={{0,256},{128,384},{256,0},{384,128},{1,257},{129,385},{257,1},{385... | collective-permute-start | bytes 98312 | tf_op jit(solution)/shard_map/ppermute | solution.py:308
  161.7 14.4 %all-to-all-start.7 = ((f32[8,56,256]{2,1,0:T(8,128)}), f32[8,56,256]{2,1,0:T(8,128)S(1)}, u32[]{:S(2)}, u32[]{:S(2)}) async-start(f32[8,56,256]{2,1,0:T(8,128)} %get-tuple-element.56), calls=%async_computation.7 | async-start | bytes 917504 | tf_op jit(solution)/shard_map/all_to_all | solution.py:298
  177.4 20.3 %all-to-all-start.8 = ((f32[4,8,56,256]{3,2,1,0:T(8,128)}), f32[4,8,56,256]{3,2,1,0:T(8,128)S(1)}, u32[]{:S(2)}, u32[]{:S(2)}) async-start(f32[4,8,56,256]{3,2,1,0:T(8,128)} %shard_map.67), calls=%async_computation.8 | async-start | bytes 3670016 | tf_op jit(solution)/shard_map/all_to_all | solution.py:298
  197.7 15.6 %collective-permute-start.8 = (f32[4,8,56,256]{3,2,1,0:T(8,128)S(1)}, f32[4,8,56,256]{3,2,1,0:T(8,128)}, u32[]{:S(2)}, u32[]{:S(2)}) collective-permute-start(f32[4,8,56,256]{3,2,1,0:T(8,128)S(1)} %all-to-all-done.8.own), channel_id=1, source_target_pairs={{0,8},{8,0},{1,9},{9,1},{2,10},{10,2},{3,11},{11,3},{4,12},{12,4},... | collective-permute-start | bytes 5505032 | tf_op jit(solution)/shard_map/ppermute | solution.py:302
  209.9 10.7 %all-to-all-start.9 = ((f32[16,1,256]{2,1,0:T(1,128)}), f32[16,1,256]{2,1,0:T(1,128)S(1)}, u32[]{:S(2)}, u32[]{:S(2)}) async-start(f32[16,1,256]{2,1,0:T(1,128)} %get-tuple-element.65), calls=%async_computation.9 | async-start | bytes 32768 | tf_op jit(solution)/shard_map/all_to_all | solution.py:298

commit v6 on v5

--- a/solution.py
+++ b/solution.py
@@ -18,7 +18,8 @@
 CHUNK = NZ * NC * SHARD
 HALF = 128
 GROUP = 8
-SOME = RANK // NY
+SOME = RANK // NZ
+ORDER = (0, 4, 2, 6, 1, 5, 3, 7)
 PER_CORE = MY_COLS // NC
 MACS = MY_ROWS * MY_COLS * RANK
 
@@ -155,9 +156,8 @@
         out[x] = part.reshape(NZ, SHARD, RANK)
 
 
-def send_kernel(where, power, buffer_t, out, some, gram):
+def send_kernel(power, buffer_t, out, gram):
     gram[...] = dot(power[...], power[...], 0, 0)
-    some[...] = gram[pl.ds(pl.multiple_of(where[2] * SOME, 8), SOME), :]
     column_product(power, buffer_t, out)
 
 
@@ -169,18 +169,19 @@
     out[...] = (pieces[0] + pieces[1]) + (pieces[2] + pieces[3])
 
 
-def sum_z_kernel(pieces, some, mine, copies, gram):
+def sum_z_kernel(pieces, gram, mine, copies):
     column = jnp.sum(pieces[...], axis=0)
     mine[...] = column
     for i in range(NZ):
-        copies[i] = column
-    for i in range(NY):
-        gram[i] = some[...]
-
-
-def copies_kernel(value, after, out):
-    for i in range(out.shape[0]):
-        out[i] = value[...]
+        copies[i, 0:SHARD] = column
+        copies[i, SHARD:] = gram[...]
+
+
+def copies_kernel(pieces, out, gram):
+    for i in range(NX):
+        out[i] = pieces[:, 0:SHARD]
+    for i, z in enumerate(ORDER):
+        gram[i * SOME : (i + 1) * SOME] = pieces[z, SHARD:]
 
 
 def inverse_factor(d):
@@ -274,13 +275,15 @@
 ):
     copies = gathered_copies(where, own, other, mom, grad, mom_here, grad_here, full, sems)
     high, low = split(weights[...])
+    both = jnp.concatenate([high, low], axis=0)
     token[...] = jnp.zeros_like(token)
     for j in range(NX):
         for copy in copies[j]:
             copy.wait()
         fh, fl = split(full[j].reshape(CHUNK, RANK))
-        change = dot(fh, high, 1, 1, None) + (dot(fh, low, 1, 1, None) + dot(fl, high, 1, 1, None))
-        mom_here[:, columns(j)] = buffer_chunk(mom_here, grad_here, j) - change.T
+        change = dot(both, fh, 1, 1, None)
+        change = change[0:MY_ROWS] + (change[MY_ROWS:] + dot(high, fl, 1, 1, None))
+        mom_here[:, columns(j)] = buffer_chunk(mom_here, grad_here, j) - change
         copies[j] = pltpu.make_async_copy(
             mom_here.at[:, columns(j)], out.at[:, columns(j)], done.at[j]
         )
@@ -307,6 +310,17 @@
     while bit < size:
         value = value + lax.ppermute(value, axis, [(i, i ^ bit) for i in range(size)])
         bit *= 2
+    return value
+
+
+def halve_along_z(value):
+    z = lax.axis_index("z")
+    for bit in (1, 2, 4):
+        size = value.shape[0] // 2
+        side = (z // bit) % 2
+        mine = lax.dynamic_slice_in_dim(value, side * size, size)
+        theirs = lax.dynamic_slice_in_dim(value, (1 - side) * size, size)
+        value = mine + lax.ppermute(theirs, "z", [(i, i ^ bit) for i in range(NZ)])
     return value
 
 
@@ -341,38 +355,31 @@
     power = swap(copies, "y").reshape(MY_ROWS, RANK)
 
     full = shape(NX, NZ, SHARD, RANK)
-    send, some = call(
-        send_kernel, [full, shape(SOME, RANK)], [SMEM, VMEM, VMEM],
-        [pltpu.VMEM((RANK, RANK), f32)], None, 6 * MACS, 3_000_000,
-    )(where, power, other_t)
+    send, gram = call(
+        send_kernel, [full, shape(RANK, RANK)], [VMEM, VMEM], (), None, 6 * MACS, 3_000_000
+    )(power, other_t)
     arrived = other_core(send)
     keep = call(keep_kernel, full, [VMEM, VMEM, ANY], (), None, 6 * MACS, 3_000_000)(
-        power, own_t, some
+        power, own_t, gram
     )
     sums = keep + arrived
-    some = some + other_core(some)
-    sums, some = lax.optimization_barrier((sums, some))
+    gram = gram + other_core(gram)
+    sums, gram = lax.optimization_barrier((sums, gram))
     by_x = swap(sums, "x")
-    some = sum_along(some, "z", NZ)
-    by_x, some = lax.optimization_barrier((by_x, some))
+    gram = halve_along_z(gram)
+    by_x, gram = lax.optimization_barrier((by_x, gram))
     by_z = call(sum_x_kernel, shape(NZ, SHARD, RANK), [VMEM], nbytes=3_000_000)(by_x)
-    by_z, some = lax.optimization_barrier((by_z, some))
+    by_z, gram = lax.optimization_barrier((by_z, gram))
     swapped = swap(by_z, "z")
-    some = sum_along(some, "x", NX)
-    column_mine, copies, gram = call(
-        sum_z_kernel,
-        [shape(SHARD, RANK), shape(NZ, SHARD, RANK), shape(NY, SOME, RANK)],
-        [VMEM, VMEM],
-    )(swapped, some)
-
-    gram = swap(gram, "y").reshape(RANK, RANK)
-    gram, copies = lax.optimization_barrier((gram, copies))
+    gram = sum_along(gram, "x", NX)
+    column_mine, copies = call(
+        sum_z_kernel, [shape(SHARD, RANK), shape(NZ, SHARD + SOME, RANK)], [VMEM, VMEM]
+    )(swapped, gram)
+
+    copies, gram = call(
+        copies_kernel, [in_hbm(NX, NZ, SHARD, RANK), shape(RANK, RANK)], [VMEM], nbytes=3_000_000
+    )(swap(copies, "z"))
     half = call(first_half_kernel, shape(3, HALF, HALF), [VMEM], flops=10_000_000_000)(gram)
-    gathered = swap(copies, "z")
-    copies = call(
-        copies_kernel, shape(NX, NZ, SHARD, RANK), [VMEM, ANY], nbytes=3_000_000
-    )(gathered, half)
-    half, copies = lax.optimization_barrier((half, copies))
     own = swap(copies, "x")
     inverse = call(second_half_kernel, shape(RANK, RANK), [VMEM], flops=10_000_000_000)(half)
     row_factor, weights = call(

time: 222 us -> 215 us (0.968)
  waiting for transfers between devices: 54.6 us -> 44.8 us
  blocking collectives: 63.3 us -> 71.4 us
  Pallas kernels: 38.9 us -> 35.7 us
  starting transfers between devices: 59.4 us -> 56.4 us
    ppermute x0 -> x3, waiting for transfers between devices: none -> 16.2 us  [halve_along_z(): value = mine + lax.ppermute(theirs, 'z', [(i, i ^ bit) for i in range(NZ)])]
    ppermute x5 -> x2, waiting for transfers between devices: 20.1 us -> 5.35 us  [sum_along(): lax.ppermute(value, axis, [(i, i ^ bit) for i in range(size)])]
    all_to_all x6 -> x5, waiting for transfers between devices: 32.4 us -> 20.8 us  [swap(): return lax.all_to_all(pieces, axis, 0, 0)]
    all_to_all x4, blocking collectives: 63.3 us -> 71.4 us  [swap(): return lax.all_to_all(pieces, axis, 0, 0)]
    ppermute x0 -> x3, starting transfers between devices: none -> 5.76 us  [halve_along_z(): value = mine + lax.ppermute(theirs, 'z', [(i, i ^ bit) for i in range(NZ)])]
    ppermute x5 -> x2, starting transfers between devices: 10.4 us -> 5.74 us  [sum_along(): lax.ppermute(value, axis, [(i, i ^ bit) for i in range(size)])]
    all_to_all x6 -> x5, starting transfers between devices: 28.6 us -> 25.1 us  [swap(): return lax.all_to_all(pieces, axis, 0, 0)]
  transfers between devices with their start and end apart: 15 -> 14, of which waited for: 12 -> 12; matrix products, arithmetic and copies ran while one was open for 0% -> 0% of each run, Pallas kernels for 14% -> 13%
where the time goes in v6:
time: 215 us; the launch traced here: 214 us
  blocking collectives  71.4 us (33%)
  starting transfers between devices  56.4 us (26%)
  waiting for transfers between devices  44.8 us (21%)
  Pallas kernels  35.7 us (17%)
  local copies, waits for them, and re-layouts  2.75 us (1%)
    all_to_all x4, blocking collectives, swap(): return lax.all_to_all(pieces, axis, 0, 0)  71.4 us
    all_to_all x5, starting transfers between devices, swap(): return lax.all_to_all(pieces, axis, 0, 0)  25.1 us
    all_to_all x5, waiting for transfers between devices, swap(): return lax.all_to_all(pieces, axis, 0, 0)  20.8 us
    ppermute x4, starting transfers between devices, other_core(): return lax.ppermute(value, 'c', [(0, 1), (1, 0)])  19.8 us
    ppermute x3, waiting for transfers between devices, halve_along_z(): value = mine + lax.ppermute(theirs, 'z', [(i, i ^ bit) for i in range(NZ)])  16.2 us
    pallas_call x1, Pallas kernels, shards(): call(first_half_kernel, shape(3, HALF, HALF), [VMEM], flops=10000000000)  7.46 us
    pallas_call x1, Pallas kernels, shards(): call(second_half_kernel, shape(RANK, RANK), [VMEM], flops=10000000000)(half)  7.16 us
    ppermute x3, starting transfers between devices, halve_along_z(): value = mine + lax.ppermute(theirs, 'z', [(i, i ^ bit) for i in range(NZ)])  5.76 us
  transfers between devices with their start and end apart: 14, of which 12 were waited for; matrix products, arithmetic and copies ran while one was open for 0% of the time, Pallas kernels for 13%

profile of v6, /device:TPU:1, one launch (start us, length us, event | category | flops | bytes accessed | tf_op | source)
XLA Modules:
  0.0 213.6 jit_solution(8946731752301264032)
XLA Ops:
  2.3 10.9 %all-to-all-start = ((f32[8,56,256]{2,1,0:T(8,128)}), f32[8,56,256]{2,1,0:T(8,128)S(1)}, u32[]{:S(2)}, u32[]{:S(2)}) async-start(f32[8,56,256]{2,1,0:T(8,128)} %broadcast_in_dim.4), calls=%async_computation | async-start | bytes 917504 | tf_op jit(solution)/shard_map/all_to_all | solution.py:301
  13.2 2.7 %shard_map.58 = (f32[128,1792]{1,0:T(8,128)S(1)}, f32[128,1792]{1,0:T(8,128)S(1)}, f32[1792,128]{1,0:T(8,128)S(1)}, f32[1792,128]{1,0:T(8,128)S(1)}) custom-call(s32[3]{0:T(128)S(1)} %pad_add_fusion.where, f32[128,3584]{1,0:T(8,128)} %mom.3, bf16[128,3584]{1,0:T(8,128)(2,1)} %grad.3), custom_call_target="tpu_custom_call" | custom-call | flops 1000000000 | bytes 9000000 | tf_op jit(solution)/shard_map/pallas_call | solution.py:333
  16.9 12.7 %all-to-all-done = f32[8,56,256]{2,1,0:T(8,128)S(1)} async-done(((f32[8,56,256]{2,1,0:T(8,128)}), f32[8,56,256]{2,1,0:T(8,128)S(1)}, u32[]{:S(2)}, u32[]{:S(2)}) %all-to-all-start) | async-done | bytes 458784 | tf_op jit(solution)/shard_map/all_to_all | solution.py:301
  29.7 26.5 %all_to_all.45.factor = f32[4,8,56,256]{3,2,1,0:T(8,128)S(1)} all-to-all(f32[4,8,56,256]{3,2,1,0:T(8,128)S(1)} %broadcast_in_dim.5), channel_id=1, replica_groups=mesh['x'=4,'z'=8,'c'=2,'y'=8] {'x'}, dimensions={0} | all-to-all | bytes 3670016 | tf_op jit(solution)/shard_map/all_to_all | solution.py:301
  56.2 3.7 %collective-permute-start = (f32[4,8,56,256]{3,2,1,0:T(8,128)S(1)}, f32[4,8,56,256]{3,2,1,0:T(8,128)S(1)}, u32[]{:S(2)}, u32[]{:S(2)}) collective-permute-start(f32[4,8,56,256]{3,2,1,0:T(8,128)S(1)} %all_to_all.45.factor), channel_id=1, source_target_pairs={{0,8},{8,0},{1,9},{9,1},{2,10},{10,2},{3,11},{11,3},{4,12},{12,4},... | collective-permute-start | bytes 5505032 | tf_op jit(solution)/shard_map/ppermute | solution.py:305
  65.8 14.5 %all_to_all.46.pieces = f32[8,16,256]{2,1,0:T(8,128)S(1)} all-to-all(f32[8,16,256]{2,1,0:T(8,128)S(1)} %bitcast.8), channel_id=1, replica_groups=mesh['x'=4,'z'=8,'c'=2,'y'=8] {'y'}, dimensions={0} | all-to-all | bytes 262144 | tf_op jit(solution)/shard_map/all_to_all | solution.py:301
  80.3 10.4 %all_to_all.47 = f32[8,16,256]{2,1,0:T(8,128)S(1)} all-to-all(f32[8,16,256]{2,1,0:T(8,128)S(1)} %shard_map.61), channel_id=1, replica_groups=mesh['x'=4,'z'=8,'c'=2,'y'=8] {'y'}, dimensions={0} | all-to-all | bytes 262144 | tf_op jit(solution)/shard_map/all_to_all | solution.py:301
  92.5 5.1 %collective-permute-start.1 = (f32[4,8,56,256]{3,2,1,0:T(8,128)S(1)}, f32[4,8,56,256]{3,2,1,0:T(8,128)S(1)}, u32[]{:S(2)}, u32[]{:S(2)}) collective-permute-start(f32[4,8,56,256]{3,2,1,0:T(8,128)S(1)} %get-tuple-element.43), channel_id=1, source_target_pairs={{0,8},{8,0},{1,9},{9,1},{2,10},{10,2},{3,11},{11,3},{4,12},{12,4},... | collective-permute-start | bytes 5505032 | tf_op jit(solution)/shard_map/ppermute | solution.py:305
  102.9 3.6 %all-to-all-start.4 = ((f32[4,8,56,256]{3,2,1,0:T(8,128)}), f32[4,8,56,256]{3,2,1,0:T(8,128)S(1)}, u32[]{:S(2)}, u32[]{:S(2)}) async-start(f32[4,8,56,256]{3,2,1,0:T(8,128)} %add.52), calls=%async_computation.4 | async-start | bytes 3670016 | tf_op jit(solution)/shard_map/all_to_all | solution.py:301
  108.6 4.6 %collective-permute-done.3 = f32[128,256]{1,0:T(8,128)S(1)} collective-permute-done((f32[128,256]{1,0:T(8,128)S(1)}, f32[128,256]{1,0:T(8,128)S(1)}, u32[]{:S(2)}, u32[]{:S(2)}) %collective-permute-start.3) | collective-permute-done | bytes 131104 | tf_op jit(solution)/shard_map/ppermute | solution.py:323
  115.2 4.9 %collective-permute-done.4 = f32[64,256]{1,0:T(8,128)S(1)} collective-permute-done((f32[64,256]{1,0:T(8,128)S(1)}, f32[64,256]{1,0:T(8,128)S(1)}, u32[]{:S(2)}, u32[]{:S(2)}) %collective-permute-start.4) | collective-permute-done | bytes 65568 | tf_op jit(solution)/shard_map/ppermute | solution.py:323
  122.1 6.6 %collective-permute-done.5 = f32[32,256]{1,0:T(8,128)S(1)} collective-permute-done((f32[32,256]{1,0:T(8,128)S(1)}, f32[32,256]{1,0:T(8,128)S(1)}, u32[]{:S(2)}, u32[]{:S(2)}) %collective-permute-start.5) | collective-permute-done | bytes 32800 | tf_op jit(solution)/shard_map/ppermute | solution.py:323
  130.6 3.5 %all-to-all-start.5 = ((f32[8,56,256]{2,1,0:T(8,128)}), f32[8,56,256]{2,1,0:T(8,128)S(1)}, u32[]{:S(2)}, u32[]{:S(2)}) async-start(f32[8,56,256]{2,1,0:T(8,128)} %shard_map.64), calls=%async_computation.5 | async-start | bytes 917504 | tf_op jit(solution)/shard_map/all_to_all | solution.py:301
  138.8 3.5 %collective-permute-start.7 = (f32[32,256]{1,0:T(8,128)S(1)}, f32[32,256]{1,0:T(8,128)S(1)}, u32[]{:S(2)}, u32[]{:S(2)}) collective-permute-start(f32[32,256]{1,0:T(8,128)S(1)} %add.66), channel_id=1, source_target_pairs={{0,256},{128,384},{256,0},{384,128},{1,257},{129,385},{257,1},{385... | collective-permute-start | bytes 98312 | tf_op jit(solution)/shard_map/ppermute | solution.py:311
  142.3 2.9 %collective-permute-done.7 = f32[32,256]{1,0:T(8,128)S(1)} collective-permute-done((f32[32,256]{1,0:T(8,128)S(1)}, f32[32,256]{1,0:T(8,128)S(1)}, u32[]{:S(2)}, u32[]{:S(2)}) %collective-permute-start.7) | collective-permute-done | bytes 32800 | tf_op jit(solution)/shard_map/ppermute | solution.py:311
  145.2 3.1 %all-to-all-done.5.pieces = f32[8,56,256]{2,1,0:T(8,128)S(1)} async-done(((f32[8,56,256]{2,1,0:T(8,128)}), f32[8,56,256]{2,1,0:T(8,128)S(1)}, u32[]{:S(2)}, u32[]{:S(2)}) %all-to-all-start.5) | async-done | bytes 458784 | tf_op jit(solution)/shard_map/all_to_all | solution.py:301
  148.4 20.0 %all_to_all.48.pieces = f32[8,88,256]{2,1,0:T(8,128)S(1)} all-to-all(f32[8,88,256]{2,1,0:T(8,128)S(1)} %get-tuple-element.50), channel_id=1, replica_groups=mesh['x'=4,'z'=8,'c'=2,'y'=8] {'z'}, dimensions={0} | all-to-all | bytes 1441792 | tf_op jit(solution)/shard_map/all_to_all | solution.py:301
  169.7 3.8 %all-to-all-start.7 = ((f32[4,8,56,256]{3,2,1,0:T(8,128)}), f32[4,8,56,256]{3,2,1,0:T(8,128)S(1)}, u32[]{:S(2)}, u32[]{:S(2)}) async-start(f32[4,8,56,256]{3,2,1,0:T(8,128)} %get-tuple-element.51), calls=%async_computation.7 | async-start | bytes 3670016 | tf_op jit(solution)/shard_map/all_to_all | solution.py:301
  173.5 7.5 %shard_map.67.half = f32[3,128,128]{2,1,0:T(8,128)S(1)} custom-call(f32[256,256]{1,0:T(8,128)S(1)} %get-tuple-element.52.gram), custom_call_target="tpu_custom_call" | custom-call | flops 10000000000 | bytes 100000 | tf_op jit(solution)/shard_map/pallas_call | solution.py:382
  181.0 7.2 %shard_map.68.inverse = f32[256,256]{1,0:T(8,128)S(1)} custom-call(f32[3,128,128]{2,1,0:T(8,128)S(1)} %shard_map.67.half), custom_call_target="tpu_custom_call" | custom-call | flops 10000000000 | bytes 100000 | tf_op jit(solution)/shard_map/pallas_call | solution.py:384
  190.6 9.1 %collective-permute-start.8 = (f32[4,8,56,256]{3,2,1,0:T(8,128)S(1)}, f32[4,8,56,256]{3,2,1,0:T(8,128)}, u32[]{:S(2)}, u32[]{:S(2)}) collective-permute-start(f32[4,8,56,256]{3,2,1,0:T(8,128)S(1)} %all-to-all-done.7.own), channel_id=1, source_target_pairs={{0,8},{8,0},{1,9},{9,1},{2,10},{10,2},{3,11},{11,3},{4,12},{12,4},... | collective-permute-start | bytes 5505032 | tf_op jit(solution)/shard_map/ppermute | solution.py:305
  202.2 3.4 %all-to-all-start.8 = ((f32[16,1,256]{2,1,0:T(1,128)}), f32[16,1,256]{2,1,0:T(1,128)S(1)}, u32[]{:S(2)}, u32[]{:S(2)}) async-start(f32[16,1,256]{2,1,0:T(1,128)} %get-tuple-element.59), calls=%async_computation.8 | async-start | bytes 32768 | tf_op jit(solution)/shard_map/all_to_all | solution.py:301
  205.6 4.6 %shard_map.70 = (f32[128,3584]{1,0:T(8,128)}, f32[8,128]{1,0:T(8,128)S(1)}) custom-call(s32[3]{0:T(128)S(1)} %pad_add_fusion.where, f32[4,8,56,256]{3,2,1,0:T(8,128)S(1)} %all-to-all-done.7.own, f32[4,8,56,256]{3,2,1,0:T(8,128)} %collective-permute-done.8.other, f32[128,256]{1,0:T(8,128)S(1)} %get-tuple-element.55.weights, f32[128,3584]{1,0:T(8,128)} %mom.3, ...), custom_call_target="tpu_custom_call" | custom-call | flops 704643072 | bytes 9000000 | tf_op jit(solution)/shard_map/pallas_call | solution.py:394
  210.2 2.7 %all-to-all-done.8.pieces = f32[16,1,256]{2,1,0:T(1,128)S(1)} async-done(((f32[16,1,256]{2,1,0:T(1,128)}), f32[16,1,256]{2,1,0:T(1,128)S(1)}, u32[]{:S(2)}, u32[]{:S(2)}) %all-to-all-start.8) | async-done | bytes 16416 | tf_op jit(solution)/shard_map/all_to_all | solution.py:301
  (40 shorter events, 35.2 us)
Async XLA Ops:
  2.3 27.3 %all-to-all-start = ((f32[8,56,256]{2,1,0:T(8,128)}), f32[8,56,256]{2,1,0:T(8,128)S(1)}, u32[]{:S(2)}, u32[]{:S(2)}) async-start(f32[8,56,256]{2,1,0:T(8,128)} %broadcast_in_dim.4), calls=%async_computation | async-start | bytes 917504 | tf_op jit(solution)/shard_map/all_to_all | solution.py:301
  16.0 0.9 copy-start
  56.2 7.1 %collective-permute-start = (f32[4,8,56,256]{3,2,1,0:T(8,128)S(1)}, f32[4,8,56,256]{3,2,1,0:T(8,128)S(1)}, u32[]{:S(2)}, u32[]{:S(2)}) collective-permute-start(f32[4,8,56,256]{3,2,1,0:T(8,128)S(1)} %all_to_all.45.factor), channel_id=1, source_target_pairs={{0,8},{8,0},{1,9},{9,1},{2,10},{10,2},{3,11},{11,3},{4,12},{12,4},... | collective-permute-start | bytes 5505032 | tf_op jit(solution)/shard_map/ppermute | solution.py:305
  61.2 29.5 %copy-start.1 = (f32[1792,128]{1,0:T(8,128)S(1)}, f32[1792,128]{1,0:T(8,128)}, u32[]{:S(2)}) copy-start(f32[1792,128]{1,0:T(8,128)} %copy-done) | copy-start | bytes 2752516
  92.5 8.9 %collective-permute-start.1 = (f32[4,8,56,256]{3,2,1,0:T(8,128)S(1)}, f32[4,8,56,256]{3,2,1,0:T(8,128)S(1)}, u32[]{:S(2)}, u32[]{:S(2)}) collective-permute-start(f32[4,8,56,256]{3,2,1,0:T(8,128)S(1)} %get-tuple-element.43), channel_id=1, source_target_pairs={{0,8},{8,0},{1,9},{9,1},{2,10},{10,2},{3,11},{11,3},{4,12},{12,4},... | collective-permute-start | bytes 5505032 | tf_op jit(solution)/shard_map/ppermute | solution.py:305
  97.6 3.8 %collective-permute-start.2 = (f32[256,256]{1,0:T(8,128)S(1)}, f32[256,256]{1,0:T(8,128)S(1)}, u32[]{:S(2)}, u32[]{:S(2)}) collective-permute-start(f32[256,256]{1,0:T(8,128)S(1)} %get-tuple-element.42.after), channel_id=1, source_target_pairs={{0,8},{8,0},{1,9},{9,1},{2,10},{10,2},{3,11},{11,3},{4,12},{12,4},... | collective-permute-start | bytes 786440 | tf_op jit(solution)/shard_map/ppermute | solution.py:305
  102.9 26.8 %all-to-all-start.4 = ((f32[4,8,56,256]{3,2,1,0:T(8,128)}), f32[4,8,56,256]{3,2,1,0:T(8,128)S(1)}, u32[]{:S(2)}, u32[]{:S(2)}) async-start(f32[4,8,56,256]{3,2,1,0:T(8,128)} %add.52), calls=%async_computation.4 | async-start | bytes 3670016 | tf_op jit(solution)/shard_map/all_to_all | solution.py:301
  106.6 6.6 %collective-permute-start.3 = (f32[128,256]{1,0:T(8,128)S(1)}, f32[128,256]{1,0:T(8,128)S(1)}, u32[]{:S(2)}, u32[]{:S(2)}) collective-permute-start(f32[128,256]{1,0:T(8,128)S(1)} %constant_dynamic-slice_fusion.2), channel_id=1, source_target_pairs={{0,16},{16,0},{32,48},{48,32},{64,80},{80,64},{96,112},{112,96},{1... | collective-permute-start | bytes 393224 | tf_op jit(solution)/shard_map/ppermute | solution.py:323
  113.2 6.9 %collective-permute-start.4 = (f32[64,256]{1,0:T(8,128)S(1)}, f32[64,256]{1,0:T(8,128)S(1)}, u32[]{:S(2)}, u32[]{:S(2)}) collective-permute-start(f32[64,256]{1,0:T(8,128)S(1)} %constant_dynamic-slice_fusion.1), channel_id=1, source_target_pairs={{0,32},{16,48},{32,0},{48,16},{64,96},{80,112},{96,64},{112,80},{1... | collective-permute-start | bytes 196616 | tf_op jit(solution)/shard_map/ppermute | solution.py:323
  120.2 8.6 %collective-permute-start.5 = (f32[32,256]{1,0:T(8,128)S(1)}, f32[32,256]{1,0:T(8,128)S(1)}, u32[]{:S(2)}, u32[]{:S(2)}) collective-permute-start(f32[32,256]{1,0:T(8,128)S(1)} %constant_dynamic-slice_fusion), channel_id=1, source_target_pairs={{0,64},{16,80},{32,96},{48,112},{64,0},{80,16},{96,32},{112,48},{1... | collective-permute-start | bytes 98312 | tf_op jit(solution)/shard_map/ppermute | solution.py:323
  130.6 17.7 %all-to-all-start.5 = ((f32[8,56,256]{2,1,0:T(8,128)}), f32[8,56,256]{2,1,0:T(8,128)S(1)}, u32[]{:S(2)}, u32[]{:S(2)}) async-start(f32[8,56,256]{2,1,0:T(8,128)} %shard_map.64), calls=%async_computation.5 | async-start | bytes 917504 | tf_op jit(solution)/shard_map/all_to_all | solution.py:301
  134.1 4.7 %collective-permute-start.6 = (f32[32,256]{1,0:T(8,128)S(1)}, f32[32,256]{1,0:T(8,128)S(1)}, u32[]{:S(2)}, u32[]{:S(2)}) collective-permute-start(f32[32,256]{1,0:T(8,128)S(1)} %dynamic-slice_add_fusion.2), channel_id=1, source_target_pairs={{0,128},{128,0},{256,384},{384,256},{1,129},{129,1},{257,385},{385... | collective-permute-start | bytes 98312 | tf_op jit(solution)/shard_map/ppermute | solution.py:311
  138.8 6.4 %collective-permute-start.7 = (f32[32,256]{1,0:T(8,128)S(1)}, f32[32,256]{1,0:T(8,128)S(1)}, u32[]{:S(2)}, u32[]{:S(2)}) collective-permute-start(f32[32,256]{1,0:T(8,128)S(1)} %add.66), channel_id=1, source_target_pairs={{0,256},{128,384},{256,0},{384,128},{1,257},{129,385},{257,1},{385... | collective-permute-start | bytes 98312 | tf_op jit(solution)/shard_map/ppermute | solution.py:311
  169.7 20.9 %all-to-all-start.7 = ((f32[4,8,56,256]{3,2,1,0:T(8,128)}), f32[4,8,56,256]{3,2,1,0:T(8,128)S(1)}, u32[]{:S(2)}, u32[]{:S(2)}) async-start(f32[4,8,56,256]{3,2,1,0:T(8,128)} %get-tuple-element.51), calls=%async_computation.7 | async-start | bytes 3670016 | tf_op jit(solution)/shard_map/all_to_all | solution.py:301
  190.6 15.0 %collective-permute-start.8 = (f32[4,8,56,256]{3,2,1,0:T(8,128)S(1)}, f32[4,8,56,256]{3,2,1,0:T(8,128)}, u32[]{:S(2)}, u32[]{:S(2)}) collective-permute-start(f32[4,8,56,256]{3,2,1,0:T(8,128)S(1)} %all-to-all-done.7.own), channel_id=1, source_target_pairs={{0,8},{8,0},{1,9},{9,1},{2,10},{10,2},{3,11},{11,3},{4,12},{12,4},... | collective-permute-start | bytes 5505032 | tf_op jit(solution)/shard_map/ppermute | solution.py:305
  202.2 10.7 %all-to-all-start.8 = ((f32[16,1,256]{2,1,0:T(1,128)}), f32[16,1,256]{2,1,0:T(1,128)S(1)}, u32[]{:S(2)}, u32[]{:S(2)}) async-start(f32[16,1,256]{2,1,0:T(1,128)} %get-tuple-element.59), calls=%async_computation.8 | async-start | bytes 32768 | tf_op jit(solution)/shard_map/all_to_all | solution.py:301

commit v7 on v6

--- a/solution.py
+++ b/solution.py
@@ -161,8 +161,10 @@
     column_product(power, buffer_t, out)
 
 
-def keep_kernel(power, buffer_t, after, out):
-    column_product(power, buffer_t, out)
+def keep_kernel(power, buffer_t, arrived, out):
+    for x in range(NX):
+        part = dot(buffer_t[pl.ds(x * NZ * SHARD, NZ * SHARD)], power[...], 1, 0)
+        out[x] = part.reshape(NZ, SHARD, RANK) + arrived[x]
 
 
 def sum_x_kernel(pieces, out):
@@ -177,11 +179,17 @@
         copies[i, SHARD:] = gram[...]
 
 
-def copies_kernel(pieces, out, gram):
-    for i in range(NX):
-        out[i] = pieces[:, 0:SHARD]
+def copies_kernel(pieces, out, gram, sems):
+    copies = [
+        pltpu.make_async_copy(pieces.at[:, pl.ds(0, SHARD)], out.at[i], sems.at[i])
+        for i in range(NX)
+    ]
+    for copy in copies:
+        copy.start()
     for i, z in enumerate(ORDER):
         gram[i * SOME : (i + 1) * SOME] = pieces[z, SHARD:]
+    for copy in copies:
+        copy.wait()
 
 
 def inverse_factor(d):
@@ -359,10 +367,9 @@
         send_kernel, [full, shape(RANK, RANK)], [VMEM, VMEM], (), None, 6 * MACS, 3_000_000
     )(power, other_t)
     arrived = other_core(send)
-    keep = call(keep_kernel, full, [VMEM, VMEM, ANY], (), None, 6 * MACS, 3_000_000)(
-        power, own_t, gram
-    )
-    sums = keep + arrived
+    sums = call(
+        keep_kernel, in_hbm(NX, NZ, SHARD, RANK), [VMEM] * 3, (), None, 6 * MACS, 5_000_000
+    )(power, own_t, arrived)
     gram = gram + other_core(gram)
     sums, gram = lax.optimization_barrier((sums, gram))
     by_x = swap(sums, "x")
@@ -377,7 +384,8 @@
     )(swapped, gram)
 
     copies, gram = call(
-        copies_kernel, [in_hbm(NX, NZ, SHARD, RANK), shape(RANK, RANK)], [VMEM], nbytes=3_000_000
+        copies_kernel, [in_hbm(NX, NZ, SHARD, RANK), shape(RANK, RANK)], [VMEM],
+        [pltpu.SemaphoreType.DMA((NX,))], [HBM, VMEM], nbytes=3_000_000,
     )(swap(copies, "z"))
     half = call(first_half_kernel, shape(3, HALF, HALF), [VMEM], flops=10_000_000_000)(gram)
     own = swap(copies, "x")

time: 215 us -> 216 us (level)
  no operation moved by 1% of the time
where the time goes in v7:
time: 216 us; the launch traced here: 215 us
  blocking collectives  71.4 us (33%)
  starting transfers between devices  56.4 us (26%)
  waiting for transfers between devices  46.3 us (21%)
  Pallas kernels  36.8 us (17%)
  local copies, waits for them, and re-layouts  2.75 us (1%)
    all_to_all x4, blocking collectives, swap(): return lax.all_to_all(pieces, axis, 0, 0)  71.4 us
    all_to_all x5, starting transfers between devices, swap(): return lax.all_to_all(pieces, axis, 0, 0)  25.1 us
    all_to_all x5, waiting for transfers between devices, swap(): return lax.all_to_all(pieces, axis, 0, 0)  20.8 us
    ppermute x4, starting transfers between devices, other_core(): return lax.ppermute(value, 'c', [(0, 1), (1, 0)])  19.8 us
    ppermute x3, waiting for transfers between devices, halve_along_z(): value = mine + lax.ppermute(theirs, 'z', [(i, i ^ bit) for i in range(NZ)])  16.2 us
    pallas_call x1, Pallas kernels, shards(): call(first_half_kernel, shape(3, HALF, HALF), [VMEM], flops=10000000000)  7.46 us
    pallas_call x1, Pallas kernels, shards(): call(second_half_kernel, shape(RANK, RANK), [VMEM], flops=10000000000)(half)  7.16 us
    ppermute x3, starting transfers between devices, halve_along_z(): value = mine + lax.ppermute(theirs, 'z', [(i, i ^ bit) for i in range(NZ)])  5.76 us
  transfers between devices with their start and end apart: 14, of which 12 were waited for; matrix products, arithmetic and copies ran while one was open for 0% of the time, Pallas kernels for 13%

profile of v7, /device:TPU:1, one launch (start us, length us, event | category | flops | bytes accessed | tf_op | source)
XLA Modules:
  0.0 214.8 jit_solution(13140970235010203540)
XLA Ops:
  2.3 10.9 %all-to-all-start = ((f32[8,56,256]{2,1,0:T(8,128)}), f32[8,56,256]{2,1,0:T(8,128)S(1)}, u32[]{:S(2)}, u32[]{:S(2)}) async-start(f32[8,56,256]{2,1,0:T(8,128)} %broadcast_in_dim.4), calls=%async_computation | async-start | bytes 917504 | tf_op jit(solution)/shard_map/all_to_all | solution.py:309
  13.2 2.7 %shard_map.58 = (f32[128,1792]{1,0:T(8,128)S(1)}, f32[128,1792]{1,0:T(8,128)S(1)}, f32[1792,128]{1,0:T(8,128)S(1)}, f32[1792,128]{1,0:T(8,128)S(1)}) custom-call(s32[3]{0:T(128)S(1)} %pad_add_fusion.where, f32[128,3584]{1,0:T(8,128)} %mom.3, bf16[128,3584]{1,0:T(8,128)(2,1)} %grad.3), custom_call_target="tpu_custom_call" | custom-call | flops 1000000000 | bytes 9000000 | tf_op jit(solution)/shard_map/pallas_call | solution.py:341
  16.9 12.7 %all-to-all-done = f32[8,56,256]{2,1,0:T(8,128)S(1)} async-done(((f32[8,56,256]{2,1,0:T(8,128)}), f32[8,56,256]{2,1,0:T(8,128)S(1)}, u32[]{:S(2)}, u32[]{:S(2)}) %all-to-all-start) | async-done | bytes 458784 | tf_op jit(solution)/shard_map/all_to_all | solution.py:309
  29.7 26.5 %all_to_all.45.factor = f32[4,8,56,256]{3,2,1,0:T(8,128)S(1)} all-to-all(f32[4,8,56,256]{3,2,1,0:T(8,128)S(1)} %broadcast_in_dim.5), channel_id=1, replica_groups=mesh['x'=4,'z'=8,'c'=2,'y'=8] {'x'}, dimensions={0} | all-to-all | bytes 3670016 | tf_op jit(solution)/shard_map/all_to_all | solution.py:309
  56.2 3.7 %collective-permute-start = (f32[4,8,56,256]{3,2,1,0:T(8,128)S(1)}, f32[4,8,56,256]{3,2,1,0:T(8,128)S(1)}, u32[]{:S(2)}, u32[]{:S(2)}) collective-permute-start(f32[4,8,56,256]{3,2,1,0:T(8,128)S(1)} %all_to_all.45.factor), channel_id=1, source_target_pairs={{0,8},{8,0},{1,9},{9,1},{2,10},{10,2},{3,11},{11,3},{4,12},{12,4},... | collective-permute-start | bytes 5505032 | tf_op jit(solution)/shard_map/ppermute | solution.py:313
  65.8 14.5 %all_to_all.46.pieces = f32[8,16,256]{2,1,0:T(8,128)S(1)} all-to-all(f32[8,16,256]{2,1,0:T(8,128)S(1)} %bitcast.8), channel_id=1, replica_groups=mesh['x'=4,'z'=8,'c'=2,'y'=8] {'y'}, dimensions={0} | all-to-all | bytes 262144 | tf_op jit(solution)/shard_map/all_to_all | solution.py:309
  80.3 10.4 %all_to_all.47 = f32[8,16,256]{2,1,0:T(8,128)S(1)} all-to-all(f32[8,16,256]{2,1,0:T(8,128)S(1)} %shard_map.61), channel_id=1, replica_groups=mesh['x'=4,'z'=8,'c'=2,'y'=8] {'y'}, dimensions={0} | all-to-all | bytes 262144 | tf_op jit(solution)/shard_map/all_to_all | solution.py:309
  92.5 5.1 %collective-permute-start.1 = (f32[4,8,56,256]{3,2,1,0:T(8,128)S(1)}, f32[4,8,56,256]{3,2,1,0:T(8,128)S(1)}, u32[]{:S(2)}, u32[]{:S(2)}) collective-permute-start(f32[4,8,56,256]{3,2,1,0:T(8,128)S(1)} %get-tuple-element.42), channel_id=1, source_target_pairs={{0,8},{8,0},{1,9},{9,1},{2,10},{10,2},{3,11},{11,3},{4,12},{12,4},... | collective-permute-start | bytes 5505032 | tf_op jit(solution)/shard_map/ppermute | solution.py:313
  101.4 2.8 %shard_map.63 = f32[4,8,56,256]{3,2,1,0:T(8,128)} custom-call(f32[128,256]{1,0:T(8,128)S(1)} %bitcast.6, f32[1792,128]{1,0:T(8,128)S(1)} %get-tuple-element.40.buffer_t, f32[4,8,56,256]{3,2,1,0:T(8,128)S(1)} %collective-permute-done.1.arrived), custom_call_target="tpu_custom_call" | custom-call | flops 704643072 | bytes 5000000 | tf_op jit(solution)/shard_map/pallas_call | solution.py:370
  104.3 3.6 %all-to-all-start.4 = ((f32[4,8,56,256]{3,2,1,0:T(8,128)}), f32[4,8,56,256]{3,2,1,0:T(8,128)S(1)}, u32[]{:S(2)}, u32[]{:S(2)}) async-start(f32[4,8,56,256]{3,2,1,0:T(8,128)} %shard_map.63), calls=%async_computation.4 | async-start | bytes 3670016 | tf_op jit(solution)/shard_map/all_to_all | solution.py:309
  109.9 4.6 %collective-permute-done.3 = f32[128,256]{1,0:T(8,128)S(1)} collective-permute-done((f32[128,256]{1,0:T(8,128)S(1)}, f32[128,256]{1,0:T(8,128)S(1)}, u32[]{:S(2)}, u32[]{:S(2)}) %collective-permute-start.3) | collective-permute-done | bytes 131104 | tf_op jit(solution)/shard_map/ppermute | solution.py:331
  116.5 4.9 %collective-permute-done.4 = f32[64,256]{1,0:T(8,128)S(1)} collective-permute-done((f32[64,256]{1,0:T(8,128)S(1)}, f32[64,256]{1,0:T(8,128)S(1)}, u32[]{:S(2)}, u32[]{:S(2)}) %collective-permute-start.4) | collective-permute-done | bytes 65568 | tf_op jit(solution)/shard_map/ppermute | solution.py:331
  123.4 6.6 %collective-permute-done.5 = f32[32,256]{1,0:T(8,128)S(1)} collective-permute-done((f32[32,256]{1,0:T(8,128)S(1)}, f32[32,256]{1,0:T(8,128)S(1)}, u32[]{:S(2)}, u32[]{:S(2)}) %collective-permute-start.5) | collective-permute-done | bytes 32800 | tf_op jit(solution)/shard_map/ppermute | solution.py:331
  132.0 3.5 %all-to-all-start.5 = ((f32[8,56,256]{2,1,0:T(8,128)}), f32[8,56,256]{2,1,0:T(8,128)S(1)}, u32[]{:S(2)}, u32[]{:S(2)}) async-start(f32[8,56,256]{2,1,0:T(8,128)} %shard_map.64), calls=%async_computation.5 | async-start | bytes 917504 | tf_op jit(solution)/shard_map/all_to_all | solution.py:309
  140.1 3.5 %collective-permute-start.7 = (f32[32,256]{1,0:T(8,128)S(1)}, f32[32,256]{1,0:T(8,128)S(1)}, u32[]{:S(2)}, u32[]{:S(2)}) collective-permute-start(f32[32,256]{1,0:T(8,128)S(1)} %add.62), channel_id=1, source_target_pairs={{0,256},{128,384},{256,0},{384,128},{1,257},{129,385},{257,1},{385... | collective-permute-start | bytes 98312 | tf_op jit(solution)/shard_map/ppermute | solution.py:319
  143.7 2.9 %collective-permute-done.7 = f32[32,256]{1,0:T(8,128)S(1)} collective-permute-done((f32[32,256]{1,0:T(8,128)S(1)}, f32[32,256]{1,0:T(8,128)S(1)}, u32[]{:S(2)}, u32[]{:S(2)}) %collective-permute-start.7) | collective-permute-done | bytes 32800 | tf_op jit(solution)/shard_map/ppermute | solution.py:319
  146.6 3.1 %all-to-all-done.5.pieces = f32[8,56,256]{2,1,0:T(8,128)S(1)} async-done(((f32[8,56,256]{2,1,0:T(8,128)}), f32[8,56,256]{2,1,0:T(8,128)S(1)}, u32[]{:S(2)}, u32[]{:S(2)}) %all-to-all-start.5) | async-done | bytes 458784 | tf_op jit(solution)/shard_map/all_to_all | solution.py:309
  149.7 20.0 %all_to_all.48.pieces = f32[8,88,256]{2,1,0:T(8,128)S(1)} all-to-all(f32[8,88,256]{2,1,0:T(8,128)S(1)} %get-tuple-element.50), channel_id=1, replica_groups=mesh['x'=4,'z'=8,'c'=2,'y'=8] {'z'}, dimensions={0} | all-to-all | bytes 1441792 | tf_op jit(solution)/shard_map/all_to_all | solution.py:309
  170.9 3.8 %all-to-all-start.7 = ((f32[4,8,56,256]{3,2,1,0:T(8,128)}), f32[4,8,56,256]{3,2,1,0:T(8,128)S(1)}, u32[]{:S(2)}, u32[]{:S(2)}) async-start(f32[4,8,56,256]{3,2,1,0:T(8,128)} %get-tuple-element.51), calls=%async_computation.7 | async-start | bytes 3670016 | tf_op jit(solution)/shard_map/all_to_all | solution.py:309
  174.7 7.5 %shard_map.67.half = f32[3,128,128]{2,1,0:T(8,128)S(1)} custom-call(f32[256,256]{1,0:T(8,128)S(1)} %get-tuple-element.52.gram), custom_call_target="tpu_custom_call" | custom-call | flops 10000000000 | bytes 100000 | tf_op jit(solution)/shard_map/pallas_call | solution.py:390
  182.2 7.2 %shard_map.68.inverse = f32[256,256]{1,0:T(8,128)S(1)} custom-call(f32[3,128,128]{2,1,0:T(8,128)S(1)} %shard_map.67.half), custom_call_target="tpu_custom_call" | custom-call | flops 10000000000 | bytes 100000 | tf_op jit(solution)/shard_map/pallas_call | solution.py:392
  191.8 9.1 %collective-permute-start.8 = (f32[4,8,56,256]{3,2,1,0:T(8,128)S(1)}, f32[4,8,56,256]{3,2,1,0:T(8,128)}, u32[]{:S(2)}, u32[]{:S(2)}) collective-permute-start(f32[4,8,56,256]{3,2,1,0:T(8,128)S(1)} %all-to-all-done.7.own), channel_id=1, source_target_pairs={{0,8},{8,0},{1,9},{9,1},{2,10},{10,2},{3,11},{11,3},{4,12},{12,4},... | collective-permute-start | bytes 5505032 | tf_op jit(solution)/shard_map/ppermute | solution.py:313
  203.4 3.4 %all-to-all-start.8 = ((f32[16,1,256]{2,1,0:T(1,128)}), f32[16,1,256]{2,1,0:T(1,128)S(1)}, u32[]{:S(2)}, u32[]{:S(2)}) async-start(f32[16,1,256]{2,1,0:T(1,128)} %get-tuple-element.59), calls=%async_computation.8 | async-start | bytes 32768 | tf_op jit(solution)/shard_map/all_to_all | solution.py:309
  206.9 4.5 %shard_map.70 = (f32[128,3584]{1,0:T(8,128)}, f32[8,128]{1,0:T(8,128)S(1)}) custom-call(s32[3]{0:T(128)S(1)} %pad_add_fusion.where, f32[4,8,56,256]{3,2,1,0:T(8,128)S(1)} %all-to-all-done.7.own, f32[4,8,56,256]{3,2,1,0:T(8,128)} %collective-permute-done.8.other, f32[128,256]{1,0:T(8,128)S(1)} %get-tuple-element.55.weights, f32[128,3584]{1,0:T(8,128)} %mom.3, ...), custom_call_target="tpu_custom_call" | custom-call | flops 704643072 | bytes 9000000 | tf_op jit(solution)/shard_map/pallas_call | solution.py:402
  (39 shorter events, 36.3 us)
Async XLA Ops:
  2.3 27.3 %all-to-all-start = ((f32[8,56,256]{2,1,0:T(8,128)}), f32[8,56,256]{2,1,0:T(8,128)S(1)}, u32[]{:S(2)}, u32[]{:S(2)}) async-start(f32[8,56,256]{2,1,0:T(8,128)} %broadcast_in_dim.4), calls=%async_computation | async-start | bytes 917504 | tf_op jit(solution)/shard_map/all_to_all | solution.py:309
  16.0 0.9 copy-start
  56.2 7.1 %collective-permute-start = (f32[4,8,56,256]{3,2,1,0:T(8,128)S(1)}, f32[4,8,56,256]{3,2,1,0:T(8,128)S(1)}, u32[]{:S(2)}, u32[]{:S(2)}) collective-permute-start(f32[4,8,56,256]{3,2,1,0:T(8,128)S(1)} %all_to_all.45.factor), channel_id=1, source_target_pairs={{0,8},{8,0},{1,9},{9,1},{2,10},{10,2},{3,11},{11,3},{4,12},{12,4},... | collective-permute-start | bytes 5505032 | tf_op jit(solution)/shard_map/ppermute | solution.py:313
  61.2 29.5 %copy-start.1 = (f32[1792,128]{1,0:T(8,128)S(1)}, f32[1792,128]{1,0:T(8,128)}, u32[]{:S(2)}) copy-start(f32[1792,128]{1,0:T(8,128)} %copy-done) | copy-start | bytes 2752516
  92.5 8.9 %collective-permute-start.1 = (f32[4,8,56,256]{3,2,1,0:T(8,128)S(1)}, f32[4,8,56,256]{3,2,1,0:T(8,128)S(1)}, u32[]{:S(2)}, u32[]{:S(2)}) collective-permute-start(f32[4,8,56,256]{3,2,1,0:T(8,128)S(1)} %get-tuple-element.42), channel_id=1, source_target_pairs={{0,8},{8,0},{1,9},{9,1},{2,10},{10,2},{3,11},{11,3},{4,12},{12,4},... | collective-permute-start | bytes 5505032 | tf_op jit(solution)/shard_map/ppermute | solution.py:313
  97.6 3.8 %collective-permute-start.2 = (f32[256,256]{1,0:T(8,128)S(1)}, f32[256,256]{1,0:T(8,128)S(1)}, u32[]{:S(2)}, u32[]{:S(2)}) collective-permute-start(f32[256,256]{1,0:T(8,128)S(1)} %get-tuple-element.43), channel_id=1, source_target_pairs={{0,8},{8,0},{1,9},{9,1},{2,10},{10,2},{3,11},{11,3},{4,12},{12,4},... | collective-permute-start | bytes 786440 | tf_op jit(solution)/shard_map/ppermute | solution.py:313
  104.3 26.8 %all-to-all-start.4 = ((f32[4,8,56,256]{3,2,1,0:T(8,128)}), f32[4,8,56,256]{3,2,1,0:T(8,128)S(1)}, u32[]{:S(2)}, u32[]{:S(2)}) async-start(f32[4,8,56,256]{3,2,1,0:T(8,128)} %shard_map.63), calls=%async_computation.4 | async-start | bytes 3670016 | tf_op jit(solution)/shard_map/all_to_all | solution.py:309
  107.9 6.6 %collective-permute-start.3 = (f32[128,256]{1,0:T(8,128)S(1)}, f32[128,256]{1,0:T(8,128)S(1)}, u32[]{:S(2)}, u32[]{:S(2)}) collective-permute-start(f32[128,256]{1,0:T(8,128)S(1)} %constant_dynamic-slice_fusion.2), channel_id=1, source_target_pairs={{0,16},{16,0},{32,48},{48,32},{64,80},{80,64},{96,112},{112,96},{1... | collective-permute-start | bytes 393224 | tf_op jit(solution)/shard_map/ppermute | solution.py:331
  114.6 6.9 %collective-permute-start.4 = (f32[64,256]{1,0:T(8,128)S(1)}, f32[64,256]{1,0:T(8,128)S(1)}, u32[]{:S(2)}, u32[]{:S(2)}) collective-permute-start(f32[64,256]{1,0:T(8,128)S(1)} %constant_dynamic-slice_fusion.1), channel_id=1, source_target_pairs={{0,32},{16,48},{32,0},{48,16},{64,96},{80,112},{96,64},{112,80},{1... | collective-permute-start | bytes 196616 | tf_op jit(solution)/shard_map/ppermute | solution.py:331
  121.5 8.6 %collective-permute-start.5 = (f32[32,256]{1,0:T(8,128)S(1)}, f32[32,256]{1,0:T(8,128)S(1)}, u32[]{:S(2)}, u32[]{:S(2)}) collective-permute-start(f32[32,256]{1,0:T(8,128)S(1)} %constant_dynamic-slice_fusion), channel_id=1, source_target_pairs={{0,64},{16,80},{32,96},{48,112},{64,0},{80,16},{96,32},{112,48},{1... | collective-permute-start | bytes 98312 | tf_op jit(solution)/shard_map/ppermute | solution.py:331
  132.0 17.7 %all-to-all-start.5 = ((f32[8,56,256]{2,1,0:T(8,128)}), f32[8,56,256]{2,1,0:T(8,128)S(1)}, u32[]{:S(2)}, u32[]{:S(2)}) async-start(f32[8,56,256]{2,1,0:T(8,128)} %shard_map.64), calls=%async_computation.5 | async-start | bytes 917504 | tf_op jit(solution)/shard_map/all_to_all | solution.py:309
  135.4 4.7 %collective-permute-start.6 = (f32[32,256]{1,0:T(8,128)S(1)}, f32[32,256]{1,0:T(8,128)S(1)}, u32[]{:S(2)}, u32[]{:S(2)}) collective-permute-start(f32[32,256]{1,0:T(8,128)S(1)} %dynamic-slice_add_fusion.2), channel_id=1, source_target_pairs={{0,128},{128,0},{256,384},{384,256},{1,129},{129,1},{257,385},{385... | collective-permute-start | bytes 98312 | tf_op jit(solution)/shard_map/ppermute | solution.py:319
  140.1 6.4 %collective-permute-start.7 = (f32[32,256]{1,0:T(8,128)S(1)}, f32[32,256]{1,0:T(8,128)S(1)}, u32[]{:S(2)}, u32[]{:S(2)}) collective-permute-start(f32[32,256]{1,0:T(8,128)S(1)} %add.62), channel_id=1, source_target_pairs={{0,256},{128,384},{256,0},{384,128},{1,257},{129,385},{257,1},{385... | collective-permute-start | bytes 98312 | tf_op jit(solution)/shard_map/ppermute | solution.py:319
  170.9 20.9 %all-to-all-start.7 = ((f32[4,8,56,256]{3,2,1,0:T(8,128)}), f32[4,8,56,256]{3,2,1,0:T(8,128)S(1)}, u32[]{:S(2)}, u32[]{:S(2)}) async-start(f32[4,8,56,256]{3,2,1,0:T(8,128)} %get-tuple-element.51), calls=%async_computation.7 | async-start | bytes 3670016 | tf_op jit(solution)/shard_map/all_to_all | solution.py:309
  191.8 15.0 %collective-permute-start.8 = (f32[4,8,56,256]{3,2,1,0:T(8,128)S(1)}, f32[4,8,56,256]{3,2,1,0:T(8,128)}, u32[]{:S(2)}, u32[]{:S(2)}) collective-permute-start(f32[4,8,56,256]{3,2,1,0:T(8,128)S(1)} %all-to-all-done.7.own), channel_id=1, source_target_pairs={{0,8},{8,0},{1,9},{9,1},{2,10},{10,2},{3,11},{11,3},{4,12},{12,4},... | collective-permute-start | bytes 5505032 | tf_op jit(solution)/shard_map/ppermute | solution.py:313
  203.4 10.7 %all-to-all-start.8 = ((f32[16,1,256]{2,1,0:T(1,128)}), f32[16,1,256]{2,1,0:T(1,128)S(1)}, u32[]{:S(2)}, u32[]{:S(2)}) async-start(f32[16,1,256]{2,1,0:T(1,128)} %get-tuple-element.59), calls=%async_computation.8 | async-start | bytes 32768 | tf_op jit(solution)/shard_map/all_to_all | solution.py:309
